TPU v7x, 32 devices: a whole 2x2x4 slice. The times are simulated.
32 devices in a mesh: exp: 8 (over z, x), row: 2 (over y), col: 2 (over core).
Axes of the slice: x: 2, y: 2, z: 4, core: 2. Of those that a mesh axis runs over, the one named last changes fastest.
Arguments:
- layer_input: bfloat16 [2048, 2048], P(('exp', 'row'), 'col'), may hold values from -6 to 6
- attention_gain: bfloat16 [2048], P('col'), may hold values from 0.5 to 1.5
- query_weight: bfloat16 [2048, 3072], P('col', 'row'), may hold values from -0.125 to 0.125
- latent_weight: bfloat16 [2048, 576], P('col'), may hold values from -0.125 to 0.125
- latent_gain: bfloat16 [512], replicated, may hold values from 0.5 to 1.5
- keyvalue_weight: bfloat16 [512, 4096], P(None, ('row', 'col')), may hold values from -0.25 to 0.25
- output_weight: bfloat16 [2048, 2048], P(('row', 'col')), may hold values from -0.375 to 0.375
- feedforward_gain: bfloat16 [2048], P('col'), may hold values from 0.5 to 1.5
- shared_gate: bfloat16 [2048, 2816], P('col', 'row'), may hold values from -0.125 to 0.125
- shared_up: bfloat16 [2048, 2816], P('col', 'row'), may hold values from -0.125 to 0.125
- shared_down: bfloat16 [2816, 2048], P(('row', 'col')), may hold values from -0.109375 to 0.109375
- expert_gate: bfloat16 [16, 2048, 1408], P('exp', 'col', 'row'), may hold values from -0.125 to 0.125
- expert_up: bfloat16 [16, 2048, 1408], P('exp', 'col', 'row'), may hold values from -0.125 to 0.125
- expert_down: bfloat16 [16, 1408, 2048], P('exp', ('row', 'col')), may hold values from -0.15625 to 0.15625
- sequence_lengths: int32 [8, 3], P('exp'), may hold values from 1 to 192, 256 in all within a row
- expert_ids: int32 [2048, 6], P('exp'), may hold values from 0 to 15, all different within a row; in each aligned block of 128 rows (0 to 127, 128 to 255, ...) at most 96 rows name the same one
- expert_weights: float32 [2048, 6], P('exp'), may hold values from 0.06 to 0.28
- output_grad: bfloat16 [2048, 2048], P(('exp', 'row'), 'col'), may hold values from -6 to 6
Outputs:
- layer_output: bfloat16 [2048, 2048], P(('exp', 'row'), 'col')
- input_grad: float32 [2048, 2048], P(('exp', 'row'), 'col')
- attention_gain_grad: float32 [2048], P('col')
- query_weight_grad: float32 [2048, 3072], P('col', 'row')
- latent_weight_grad: float32 [2048, 576], P('col')
- latent_gain_grad: float32 [512], replicated
- keyvalue_weight_grad: float32 [512, 4096], P(None, ('row', 'col'))
- output_weight_grad: float32 [2048, 2048], P(('row', 'col'))
- feedforward_gain_grad: float32 [2048], P('col')
- shared_gate_grad: float32 [2048, 2816], P('col', 'row')
- shared_up_grad: float32 [2048, 2816], P('col', 'row')
- shared_down_grad: float32 [2816, 2048], P(('row', 'col'))
- expert_gate_grad: float32 [16, 2048, 1408], P('exp', 'col', 'row')
- expert_up_grad: float32 [16, 2048, 1408], P('exp', 'col', 'row')
- expert_down_gradient: float32 [16, 1408, 2048], P('exp', ('row', 'col'))
Inputs may be any that keep to these rules, and one draw needn't show every extreme that they name: `sequence_lengths`: each row holds the lengths of the 3 sequences of one data group, in order; they sum to 256 and the largest is 192. `expert_ids`: each row names 6 different experts. Within each aligned block of 128 rows no expert is named by more than 96 rows, and in every draw some expert is named by exactly 96 rows of some block.
All inputs are finite; a program needn't handle non-finite values.
Results may differ from a plain program's by a relative error of at most 0.02.
Values may be sent and summed in bfloat16 or wider, within the bound.
A program may use at most 384 MiB of HBM per device.

v0:
```python
import jax
import jax.numpy as jnp
from jax import lax
from jax.sharding import PartitionSpec as P

DN = 128
DR = 64
DV = 128
R = 512
TOP = 6


EPSILON = 1e-06
ROPE_BASE = 50000.0
NEGATIVE = -1e30


def matmul(former, latter):
    return jnp.dot(former, latter, preferred_element_type=jnp.float32)


def matmul_left(former, latter):
    return lax.dot_general(
        former, latter, (((0,), (0,)), ((), ())), preferred_element_type=jnp.float32
    )


def matmul_right(former, latter):
    return lax.dot_general(
        former, latter, (((1,), (1,)), ((), ())), preferred_element_type=jnp.float32
    )


def rotate(values, cosine_table, sine_table):
    half_width = values.shape[-1] // 2
    former, latter = (values[..., :half_width], values[..., half_width:])
    return jnp.concatenate(
        [former * cosine_table - latter * sine_table, latter * cosine_table + former * sine_table],
        axis=-1,
    )


def unrotate(gradient, cosine_table, sine_table):
    half_width = gradient.shape[-1] // 2
    former, latter = (gradient[..., :half_width], gradient[..., half_width:])
    return jnp.concatenate(
        [former * cosine_table + latter * sine_table, latter * cosine_table - former * sine_table],
        axis=-1,
    )


def sequence_layout(lengths, group_size):
    seq_ends = jnp.cumsum(lengths)
    token_order = jnp.arange(group_size, dtype=jnp.int32)
    segment = jnp.sum((token_order[:, None] >= seq_ends[None, :]).astype(jnp.int32), axis=1)
    seq_starts = seq_ends - lengths
    own_start = jnp.sum(
        jnp.where(
            segment[:, None] == jnp.arange(lengths.shape[0], dtype=jnp.int32)[None, :],
            seq_starts[None, :],
            0,
        ),
        axis=1,
    )
    return (segment, token_order - own_start)


def rope_tables(places):
    inverse_frequency = ROPE_BASE ** (-(jnp.arange(DR // 2, dtype=jnp.float32) * 2.0 / DR))
    angles = places.astype(jnp.float32)[:, None] * inverse_frequency[None, :]
    return (jnp.cos(angles), jnp.sin(angles))


def half_sums(values):
    return lax.psum(values, "col")


def norm_forward(values):
    full_width = values.shape[1] * lax.axis_size("col")
    inverse_rms = lax.rsqrt(half_sums(jnp.sum(values * values, axis=1)) / full_width + EPSILON)[
        :, None
    ]
    return (values * inverse_rms, inverse_rms)


def norm_backward(gradient, normed, inverse_rms, gain_vector):
    full_width = normed.shape[1] * lax.axis_size("col")
    scaled = gradient * gain_vector
    inner_sum = half_sums(jnp.sum(scaled * normed, axis=1)) / full_width
    return (
        inverse_rms * (scaled - normed * inner_sum[:, None]),
        jnp.sum(gradient * normed, axis=0),
    )


def gather_rows(values):
    return lax.all_gather(values, "row", axis=0, tiled=True)


def scatter_rows(values):
    return lax.psum_scatter(values, "row", scatter_dimension=0, tiled=True)


def spread_cols(former, latter):
    return (
        lax.psum_scatter(former, "col", scatter_dimension=1, tiled=True),
        lax.psum_scatter(latter, "col", scatter_dimension=1, tiled=True),
    )


def collect_cols(former, latter):
    return (
        lax.all_gather(former, "col", axis=1, tiled=True),
        lax.all_gather(latter, "col", axis=1, tiled=True),
    )


def send_to_experts(buffer):
    return lax.all_to_all(buffer, "exp", split_axis=0, concat_axis=0, tiled=True)


def send_to_sources(buffer):
    return lax.all_to_all(buffer, "exp", split_axis=0, concat_axis=0, tiled=True)


def spread_down(hidden, weight):
    row_count = lax.axis_size("row")
    col_count = lax.axis_size("col")
    block_rows = hidden.shape[0] // row_count
    half_width = weight.shape[1] // col_count
    first_row = jnp.int32(0)
    pieces = []
    for offset in range(block_rows * lax.axis_size(("row", "col")) // block_rows):
        target = first_row // block_rows + offset
        rows_in = lax.dynamic_slice_in_dim(hidden, target // col_count * block_rows, block_rows, 0)
        columns = lax.dynamic_slice_in_dim(weight, target % col_count * half_width, half_width, 1)
        pieces.append(matmul(rows_in, columns))
    return lax.psum_scatter(
        jnp.concatenate(pieces, axis=0), ("row", "col"), scatter_dimension=0, tiled=True
    )


def collect_down(block):
    gathered = lax.all_gather(block, ("row", "col"), axis=0, tiled=True)
    row_count, col_count = (lax.axis_size("row"), lax.axis_size("col"))
    block_rows, half_width = block.shape
    gathered = gathered.reshape(row_count, col_count, block_rows, half_width).transpose(0, 2, 1, 3)
    return gathered.reshape(row_count * block_rows, col_count * half_width)


def ffn_forward(inputs, w_gate, w_up, w_down):
    col_count = lax.axis_size("col")
    gate_part = matmul(inputs, w_gate)
    up_part = matmul(inputs, w_up)
    slot_count, full_width = gate_part.shape
    gating, upward = spread_cols(
        gate_part.reshape(slot_count, col_count, full_width // col_count),
        up_part.reshape(slot_count, col_count, full_width // col_count),
    )
    gating = gating.reshape(slot_count, -1)
    upward = upward.reshape(slot_count, -1)
    hidden = (jax.nn.silu(gating) * upward).astype(jnp.bfloat16)
    return (spread_down(hidden, w_down), (gating, upward, hidden))


def ffn_backward(grad_block, inputs, w_gate, w_up, w_down, stored):
    gating, upward, hidden = stored
    grad_full = collect_down(grad_block)
    grad_down = matmul_left(hidden, grad_full)
    grad_hidden = matmul_right(grad_full, w_down)
    sigmoid = jax.nn.sigmoid(gating)
    grad_upward = (grad_hidden * jax.nn.silu(gating)).astype(jnp.bfloat16)
    grad_gating = (grad_hidden * upward * sigmoid * (1.0 + gating * (1.0 - sigmoid))).astype(
        jnp.bfloat16
    )
    slot_count = gating.shape[0]
    grad_gating, grad_upward = collect_cols(grad_gating[:, None, :], grad_upward[:, None, :])
    grad_gating = grad_gating.reshape(slot_count, -1)
    grad_upward = grad_upward.reshape(slot_count, -1)
    grad_wgate = matmul_left(inputs, grad_gating)
    grad_wup = matmul_left(inputs, grad_upward)
    grad_inputs = scatter_rows(matmul_right(grad_gating, w_gate) + matmul_right(grad_upward, w_up))
    return (grad_inputs, grad_wgate, grad_wup, grad_down)


def slot_tables(chosen_ids, chosen_weights, expert_count, capacity):
    flat_ids = chosen_ids.reshape(-1)
    matches = (flat_ids[:, None] == jnp.arange(expert_count, dtype=jnp.int32)[None, :]).astype(
        jnp.int32
    )
    ranking = jnp.sum((jnp.cumsum(matches, axis=0) - 1) * matches, axis=1)
    slot_ids = flat_ids * capacity + ranking
    holders = jnp.arange(flat_ids.shape[0], dtype=jnp.int32) // chosen_ids.shape[1]
    owners = jnp.zeros((expert_count * capacity,), jnp.int32).at[slot_ids].set(holders + 1) - 1
    slot_weight = (
        jnp.zeros((expert_count * capacity,), jnp.float32)
        .at[slot_ids]
        .set(chosen_weights.reshape(-1))
    )
    return (slot_ids.reshape(chosen_ids.shape), owners, slot_weight)


def block_mask(segment, first_row, block_size):
    token_order = jnp.arange(segment.shape[0], dtype=jnp.int32)
    return (segment[first_row : first_row + block_size, None] == segment[None, :]) & (
        token_order[None, :] <= token_order[:, None]
    )


def attend_forward(queries, keys_all, values, segment, block_size):
    factor = (DN + DR) ** (-0.5)
    outputs, log_totals = ([], [])
    allowed = block_mask(segment, 0, block_size)
    raw_scores = (
        jnp.einsum("qhd,khd->hqk", queries, keys_all, preferred_element_type=jnp.float32) * factor
    )
    scores = jnp.where(allowed[None], raw_scores, NEGATIVE)
    row_peak = jnp.max(scores, axis=-1, keepdims=True)
    exponent = jnp.exp(scores - row_peak)
    row_total = jnp.sum(exponent, axis=-1, keepdims=True)
    weights = (exponent / row_total).astype(jnp.bfloat16)
    outputs.append(jnp.einsum("hqk,khd->qhd", weights, values, preferred_element_type=jnp.float32))
    log_totals.append(row_peak + jnp.log(row_total))
    return (outputs[0], log_totals)


def attend_backward(queries, keys_all, values, segment, block_size, log_totals, grad_heads):
    factor = (DN + DR) ** (-0.5)
    grad_keys = jnp.zeros(keys_all.shape, jnp.float32)
    grad_values = jnp.zeros(values.shape, jnp.float32)
    grad_queries = []
    for block_number, first_row in enumerate(range(0, keys_all.shape[0], block_size)):
        allowed = block_mask(segment, first_row, block_size)
        raw_scores = (
            jnp.einsum("qhd,khd->hqk", queries, keys_all, preferred_element_type=jnp.float32)
            * factor
        )
        scores = jnp.where(allowed[None], raw_scores, NEGATIVE)
        probabilities = jnp.exp(scores - log_totals[block_number])
        weights = probabilities.astype(jnp.bfloat16)
        grad_probs = jnp.einsum(
            "qhd,khd->hqk", grad_heads, values, preferred_element_type=jnp.float32
        )
        inner_sum = jnp.sum(probabilities * grad_probs, axis=-1, keepdims=True)
        grad_scores = (probabilities * (grad_probs - inner_sum)).astype(jnp.bfloat16)
        grad_queries.append(
            jnp.einsum("hqk,khd->qhd", grad_scores, keys_all, preferred_element_type=jnp.float32)
            * factor
        )
        grad_keys = (
            jnp.einsum("hqk,qhd->khd", grad_scores, queries, preferred_element_type=jnp.float32)
            * factor
        )
        grad_values = jnp.einsum(
            "hqk,qhd->khd", weights, grad_heads, preferred_element_type=jnp.float32
        )
    return (grad_queries[0], grad_keys, grad_values)


def local(
    layer_input,
    attention_gain,
    query_weight,
    latent_weight,
    latent_gain,
    keyvalue_weight,
    output_weight,
    feedforward_gain,
    shared_gate,
    shared_up,
    shared_down,
    expert_gate,
    expert_up,
    expert_down,
    sequence_lengths,
    expert_ids,
    expert_weights,
    output_grad,
):
    row_index = lax.axis_index("row")
    exp_count = lax.axis_size("exp")
    local_tokens = layer_input.shape[0]
    per_device = expert_gate.shape[0]
    experts_all = per_device * exp_count
    capacity = min(local_tokens, 2 * local_tokens * TOP // experts_all)
    residual = layer_input.astype(jnp.float32)
    normed_one, scale_one = norm_forward(residual)
    gain_one = attention_gain.astype(jnp.float32)
    attention_input = (normed_one * gain_one).astype(jnp.bfloat16)
    attention_rows = gather_rows(attention_input)
    group_size = attention_rows.shape[0]
    heads_row = query_weight.shape[1] // (DN + DR)
    query_part = matmul(attention_rows, query_weight).reshape(group_size, heads_row, DN + DR)
    query_nope, query_rope = spread_cols(query_part[..., :DN], query_part[..., DN:])
    latent = half_sums(matmul(attention_rows, latent_weight))
    compressed_raw = latent[:, :R]
    latent_scale = lax.rsqrt(
        jnp.mean(compressed_raw * compressed_raw, axis=1, keepdims=True) + EPSILON
    )
    latent_normed = compressed_raw * latent_scale
    latent_gain_full = latent_gain.astype(jnp.float32)
    compressed = (latent_normed * latent_gain_full).astype(jnp.bfloat16)
    keyvalue = (
        matmul(compressed, keyvalue_weight).astype(jnp.bfloat16).reshape(group_size, -1, DN + DV)
    )
    heads_here = keyvalue.shape[1]
    segment, places = sequence_layout(sequence_lengths[0], group_size)
    cosine_table, sine_table = rope_tables(places)
    rope_key = rotate(latent[:, R:], cosine_table, sine_table).astype(jnp.bfloat16)
    queries = jnp.concatenate(
        [query_nope, rotate(query_rope, cosine_table[:, None, :], sine_table[:, None, :])], axis=-1
    ).astype(jnp.bfloat16)
    keys_all = jnp.concatenate(
        [keyvalue[..., :DN], jnp.broadcast_to(rope_key[:, None, :], (group_size, heads_here, DR))],
        axis=-1,
    )
    values = keyvalue[..., DN:]
    block_size = min(512, group_size)
    attended, log_totals = attend_forward(queries, keys_all, values, segment, block_size)
    attention_out = attended.reshape(group_size, -1).astype(jnp.bfloat16)
    hidden_state = residual + spread_down(attention_out, output_weight)
    normed_two, scale_two = norm_forward(hidden_state)
    gain_two = feedforward_gain.astype(jnp.float32)
    mixer_input = (normed_two * gain_two).astype(jnp.bfloat16)
    mixer_rows = gather_rows(mixer_input)
    shared_out, shared_stored = ffn_forward(mixer_rows, shared_gate, shared_up, shared_down)
    own_ids = lax.dynamic_slice_in_dim(expert_ids, row_index * local_tokens, local_tokens, 0)
    own_weights = lax.dynamic_slice_in_dim(
        expert_weights, row_index * local_tokens, local_tokens, 0
    )
    slot_ids, owners, slot_weight = slot_tables(own_ids, own_weights, experts_all, capacity)
    filled = (owners >= 0)[:, None]
    holder = jnp.maximum(owners, 0)
    outgoing = jnp.where(filled, jnp.take(mixer_input, holder, axis=0), jnp.zeros((), jnp.bfloat16))
    arrived = send_to_experts(outgoing.reshape(exp_count, per_device, capacity, -1))
    expert_inputs, expert_stored, returned = ([], [], [])
    for local_index in range(per_device):
        rows_in = gather_rows(arrived[:, local_index].reshape(exp_count * capacity, -1))
        produced, stored = ffn_forward(
            rows_in, expert_gate[local_index], expert_up[local_index], expert_down[local_index]
        )
        expert_inputs.append(rows_in)
        expert_stored.append(stored)
        returned.append(produced.astype(jnp.bfloat16).reshape(exp_count, capacity, -1))
    returned_rows = send_to_sources(jnp.stack(returned, axis=1)).reshape(experts_all * capacity, -1)
    picked = jnp.take(returned_rows, slot_ids, axis=0).astype(jnp.float32)
    routed = jnp.sum(picked * own_weights[:, :, None], axis=1)
    layer_result = hidden_state + shared_out + routed
    upstream = output_grad.astype(jnp.float32)
    grad_shared, grad_sgate, grad_sup, shared_down_partial = ffn_backward(
        output_grad, mixer_rows, shared_gate, shared_up, shared_down, shared_stored
    )
    slot_grads = (jnp.take(upstream, holder, axis=0) * slot_weight[:, None]).astype(jnp.bfloat16)
    grads_arrived = send_to_experts(slot_grads.reshape(exp_count, per_device, capacity, -1))
    returning_gradients, expert_gate_partial, expert_up_partial, expert_down_partial = (
        [],
        [],
        [],
        [],
    )
    for local_index in range(per_device):
        grad_in, single_gate_gradient, single_up_gradient, grad_down_one = ffn_backward(
            grads_arrived[:, local_index].reshape(exp_count * capacity, -1),
            expert_inputs[local_index],
            expert_gate[local_index],
            expert_up[local_index],
            expert_down[local_index],
            expert_stored[local_index],
        )
        returning_gradients.append(grad_in.astype(jnp.bfloat16).reshape(exp_count, capacity, -1))
        expert_gate_partial.append(single_gate_gradient)
        expert_up_partial.append(single_up_gradient)
        expert_down_partial.append(grad_down_one)
    grad_slots = send_to_sources(jnp.stack(returning_gradients, axis=1)).reshape(
        experts_all * capacity, -1
    )
    grad_routed = jnp.sum(jnp.take(grad_slots, slot_ids, axis=0).astype(jnp.float32), axis=1)
    grad_norm_two, gain_two_grad = norm_backward(
        grad_shared + grad_routed, normed_two, scale_two, gain_two
    )
    grad_hidden = upstream + grad_norm_two
    grad_stream = collect_down(grad_hidden.astype(jnp.bfloat16))
    grad_wo = matmul_left(attention_out, grad_stream)
    grad_heads = (
        matmul_right(grad_stream, output_weight)
        .astype(jnp.bfloat16)
        .reshape(group_size, heads_here, DV)
    )
    grad_queries, grad_keys, grad_values = attend_backward(
        queries, keys_all, values, segment, block_size, log_totals, grad_heads
    )
    grad_qnope = grad_queries[..., :DN].astype(jnp.bfloat16)
    grad_qrope = unrotate(
        grad_queries[..., DN:], cosine_table[:, None, :], sine_table[:, None, :]
    ).astype(jnp.bfloat16)
    grad_qnope, grad_qrope = collect_cols(grad_qnope, grad_qrope)
    grad_query = jnp.concatenate([grad_qnope, grad_qrope], axis=-1).reshape(group_size, -1)
    grad_wq = matmul_left(attention_rows, grad_query)
    grad_rows_query = matmul_right(grad_query, query_weight)
    grad_keyvalue = (
        jnp.concatenate([grad_keys[..., :DN], grad_values], axis=-1)
        .astype(jnp.bfloat16)
        .reshape(group_size, -1)
    )
    grad_wkvb = matmul_left(compressed, grad_keyvalue)
    grad_compressed = matmul_right(grad_keyvalue, keyvalue_weight)
    scaled_latent = grad_compressed * latent_gain_full
    latent_inner = jnp.mean(scaled_latent * latent_normed, axis=1, keepdims=True)
    grad_craw = latent_scale * (scaled_latent - latent_normed * latent_inner)
    latent_gain_part = jnp.sum(grad_compressed * latent_normed, axis=0)
    grad_rope_key = unrotate(jnp.sum(grad_keys[..., DN:], axis=1), cosine_table, sine_table)
    grad_latent, grad_latent_gain = lax.psum(
        (jnp.concatenate([grad_craw, grad_rope_key], axis=1), latent_gain_part), ("row", "col")
    )
    grad_latent = grad_latent.astype(jnp.bfloat16)
    grad_wkva = matmul_left(attention_rows, grad_latent)
    own_latent = lax.dynamic_slice_in_dim(grad_latent, row_index * local_tokens, local_tokens, 0)
    grad_attention_input = scatter_rows(grad_rows_query) + matmul_right(own_latent, latent_weight)
    grad_norm_one, gain_one_grad = norm_backward(
        grad_attention_input, normed_one, scale_one, gain_one
    )
    input_grad = grad_hidden + grad_norm_one
    weight_sums = (
        lax.psum(grad_wq.astype(jnp.bfloat16), "exp").astype(jnp.float32),
        lax.psum(grad_wkva.astype(jnp.bfloat16), "exp").astype(jnp.float32),
        lax.psum(grad_latent_gain.astype(jnp.bfloat16), "exp").astype(jnp.float32),
        lax.psum(grad_wkvb.astype(jnp.bfloat16), "exp").astype(jnp.float32),
        lax.psum(grad_wo.astype(jnp.bfloat16), "exp").astype(jnp.float32),
        lax.psum(grad_sgate.astype(jnp.bfloat16), "exp").astype(jnp.float32),
        lax.psum(grad_sup.astype(jnp.bfloat16), "exp").astype(jnp.float32),
        lax.psum(shared_down_partial.astype(jnp.bfloat16), "exp").astype(jnp.float32),
    )
    gain_sums = lax.psum((gain_one_grad, gain_two_grad), ("exp", "row"))
    return (
        layer_result.astype(jnp.bfloat16),
        input_grad,
        gain_sums[0],
        weight_sums[0],
        weight_sums[1],
        weight_sums[2],
        weight_sums[3],
        weight_sums[4],
        gain_sums[1],
        weight_sums[5],
        weight_sums[6],
        weight_sums[7],
        jnp.stack(expert_gate_partial),
        jnp.stack(expert_up_partial),
        jnp.stack(expert_down_partial),
    )


def solution(mesh):
    in_specs = (
        P(("exp", "row"), "col"),
        P("col"),
        P("col", "row"),
        P("col", None),
        P(),
        P(None, ("row", "col")),
        P(("row", "col"), None),
        P("col"),
        P("col", "row"),
        P("col", "row"),
        P(("row", "col"), None),
        P("exp", "col", "row"),
        P("exp", "col", "row"),
        P("exp", ("row", "col"), None),
        P("exp", None),
        P("exp", None),
        P("exp", None),
        P(("exp", "row"), "col"),
    )
    out_specs = (
        P(("exp", "row"), "col"),
        P(("exp", "row"), "col"),
        P("col"),
        P("col", "row"),
        P("col", None),
        P(),
        P(None, ("row", "col")),
        P(("row", "col"), None),
        P("col"),
        P("col", "row"),
        P("col", "row"),
        P(("row", "col"), None),
        P("exp", "col", "row"),
        P("exp", "col", "row"),
        P("exp", ("row", "col"), None),
    )
    return jax.shard_map(local, mesh=mesh, in_specs=in_specs, out_specs=out_specs, check_vma=False)
```

profile of v0, /device:TPU:0, one launch (start us, length us, event | category | flops | bytes accessed | tf_op | source)
XLA Modules:
  0.0 1644.8 jit_solution(12318262745058746546)
XLA Ops:
  13.4 10.2 all_gather.48
  35.1 12.5 all-reduce.7.cloned.1.call-done
  61.2 10.9 reduce-scatter.17.cloned.1.call-done
  86.3 26.2 %reduce-scatter.21.cloned.1.call-done = f32[128,1024]{1,0:T(8,128)} async-done(((f32[512,1024]{1,0:T(8,128)}), f32[128,1024]{1,0:T(8,128)}) %reduce-scatter.21.cloned.1.call-update) | async-done | bytes 524304 | tf_op jit(solution)/shard_map/reduce_scatter | solution.py:138
  138.7 8.8 gather_fusion.1
  147.5 56.5 %all-to-all-done = bf16[8,2,96,1024]{3,2,1,0:T(8,128)(2,1)} async-done(((bf16[8,2,96,1024]{3,2,1,0:T(8,128)(2,1)}), bf16[8,2,96,1024]{3,2,1,0:T(8,128)(2,1)}, u32[]{:S(2)}, u32[]{:S(2)}) %all-to-all-start) | async-done | bytes 3145760 | tf_op jit(solution)/shard_map/all_to_all | solution.py:119
  217.5 69.6 %all-to-all-done.2 = bf16[8,2,96,1024]{3,2,1,0:T(8,128)(2,1)} async-done(((bf16[8,2,96,1024]{3,2,1,0:T(8,128)(2,1)}), bf16[8,2,96,1024]{3,2,1,0:T(8,128)(2,1)}, u32[]{:S(2)}, u32[]{:S(2)}) %all-to-all-start.2) | async-done | bytes 3145760 | tf_op jit(solution)/shard_map/all_to_all | solution.py:119
  324.6 22.1 %all-gather.25.cloned.1.call-done = bf16[3072,1024]{1,0:T(8,128)(2,1)} async-done(((bf16[768,1024]{1,0:T(8,128)(2,1)}), bf16[3072,1024]{1,0:T(8,128)(2,1)}) %all-gather.25.cloned.1.call-update) | async-done | bytes 6291472 | tf_op jit(solution)/shard_map/all_gather | solution.py:144
  346.7 11.9 copy.215
  364.0 14.3 reduce-scatter.37.cloned.1.call-done
  378.3 9.3 fusion.8
  388.4 39.6 %all-gather.23.cloned.1.call-done = bf16[3072,1024]{1,0:T(8,128)(2,1)} async-done(((bf16[768,1024]{1,0:T(8,128)(2,1)}), bf16[3072,1024]{1,0:T(8,128)(2,1)}) %all-gather.23.cloned.1.call-update) | async-done | bytes 6291472 | tf_op jit(solution)/shard_map/all_gather | solution.py:144
  427.9 11.9 copy.214
  445.2 14.2 reduce-scatter.31.cloned.1.call-done
  459.4 9.3 fusion.16
  473.5 7.4 fusion.29
  487.3 9.3 convolution_add_fusion
  501.2 7.3 fusion.32
  515.0 9.1 convolution_add_fusion.1
  525.0 15.2 all_gather.49
  572.4 28.6 %reduce-scatter.45.cloned.1.call-done = f32[768,1024]{1,0:T(8,128)} async-done(((f32[1536,1024]{1,0:T(8,128)}), f32[768,1024]{1,0:T(8,128)}) %reduce-scatter.45.cloned.1.call-update) | async-done | bytes 3145744 | tf_op jit(solution)/shard_map/reduce_scatter | solution.py:101
  604.3 76.1 %reduce-scatter.43.cloned.1.call-done = f32[768,1024]{1,0:T(8,128)} async-done(((f32[1536,1024]{1,0:T(8,128)}), f32[768,1024]{1,0:T(8,128)}) %reduce-scatter.43.cloned.1.call-update) | async-done | bytes 3145744 | tf_op jit(solution)/shard_map/reduce_scatter | solution.py:101
  690.2 8.5 all-gather.21.cloned.1.call-done
  702.2 8.1 reduce-scatter.25.cloned.1.call-done
  710.3 13.1 reduce-scatter.23.cloned.1.call-done
  734.8 91.4 %reduce-scatter.39.cloned.1.call-done = f32[768,1024]{1,0:T(8,128)} async-done(((f32[3072,1024]{1,0:T(8,128)}), f32[768,1024]{1,0:T(8,128)}) %reduce-scatter.39.cloned.1.call-update) | async-done | bytes 3145744 | tf_op jit(solution)/shard_map/reduce_scatter | solution.py:138
  829.6 98.4 %reduce-scatter.33.cloned.1.call-done = f32[768,1024]{1,0:T(8,128)} async-done(((f32[3072,1024]{1,0:T(8,128)}), f32[768,1024]{1,0:T(8,128)}) %reduce-scatter.33.cloned.1.call-update) | async-done | bytes 3145744 | tf_op jit(solution)/shard_map/reduce_scatter | solution.py:138
  959.7 48.9 %all-to-all-done.1 = bf16[8,2,96,1024]{3,2,1,0:T(8,128)(2,1)} async-done(((bf16[8,2,96,1024]{3,2,1,0:T(8,128)(2,1)}), bf16[8,2,96,1024]{3,2,1,0:T(8,128)(2,1)}, u32[]{:S(2)}, u32[]{:S(2)}) %all-to-all-start.1) | async-done | bytes 3145760 | tf_op jit(solution)/shard_map/all_to_all | solution.py:123
  1078.4 27.5 %all-reduce.10 = (bf16[256,576]{0,1:T(8,128)(2,1)}, bf16[512]{0:T(512)(128)(2,1)S(1)}) all-reduce(f32[256,576]{0,1:T(8,128)} %pad_maximum_fusion.10, f32[512]{0:T(512)S(1)} %get-tuple-element.18), channel_id=1, replica_groups=mesh['exp'=8,'row'=2,'col'=2] {'row','col'}, use_global_device_ids=true, to_apply=%region_39.41 | all-reduce | flops 147968 | bytes 887808 | tf_op jit(solution)/shard_map/psum | solution.py:412
  1149.5 23.0 %psum.129 = bf16[512]{0:T(512)(128)(2,1)S(1)} all-reduce(bf16[512]{0:T(512)(128)(2,1)S(1)} %get-tuple-element.27), channel_id=1, replica_groups=mesh['exp'=8,'row'=2,'col'=2] {'exp'}, use_global_device_ids=true, to_apply=%region_48.50 | all-reduce | flops 512 | bytes 2048 | tf_op jit(solution)/shard_map/psum | solution.py:426
  1178.2 41.1 %all-reduce = (f32[1024]{0:T(1024)}, f32[1024]{0:T(1024)}) all-reduce(f32[1024]{0:T(1024)S(1)} %get-tuple-element.20, f32[1024]{0:T(1024)S(1)} %get-tuple-element.16), channel_id=1, replica_groups=mesh['exp'=8,'row'=2,'col'=2] {'exp','row'}, use_global_device_ids=true, to_apply=%region_43.45 | all-reduce | flops 2048 | bytes 16384 | tf_op jit(solution)/shard_map/psum | solution.py:433
  1221.5 395.8 %all-reduce.9.cloned.1.call-done = (bf16[1024,1536]{1,0:T(8,128)(2,1)}, bf16[1024,576]{0,1:T(8,128)(2,1)}, bf16[512,1024]{1,0:T(8,128)(2,1)}, bf16[512,2048]{1,0...) async-done(((bf16[1024,1536]{1,0:T(8,128)(2,1)}, bf16[1024,576]{0,1:T(8,128)(2,1)}, bf16[512,1024]{1,0:T(8,128)(2,1)}, ...) | async-done | bytes 16121872 | tf_op jit(solution)/shard_map/psum | solution.py:424
  (442 shorter events, 392.6 us)
Async XLA Ops:
  7.2 40.3 %all-reduce.7.cloned.1.call-start = ((), (), s32[]{:S(2)}) async-start(), calls=%async_computation.20 | async-start | bytes 1179648 | tf_op jit(solution)/shard_map/psum | solution.py:75
  27.0 32.6 %reduce-scatter.19.cloned.1.call-start = ((), (), s32[]{:S(2)}) async-start(), calls=%async_computation.22 | async-start | bytes 786432 | tf_op jit(solution)/shard_map/reduce_scatter | solution.py:107
  31.5 40.6 %reduce-scatter.17.cloned.1.call-start = ((), (), s32[]{:S(2)}) async-start(), calls=%async_computation.21 | async-start | bytes 1572864 | tf_op jit(solution)/shard_map/reduce_scatter | solution.py:106
  33.9 78.7 %reduce-scatter.21.cloned.1.call-start = ((), (), s32[]{:S(2)}) async-start(), calls=%async_computation.23 | async-start | bytes 2621440 | tf_op jit(solution)/shard_map/reduce_scatter | solution.py:138
  127.2 76.8 %all-to-all-start = ((bf16[8,2,96,1024]{3,2,1,0:T(8,128)(2,1)}), bf16[8,2,96,1024]{3,2,1,0:T(8,128)(2,1)}, u32[]{:S(2)}, u32[]{:S(2)}) async-start(bf16[8,2,96,1024]{3,2,1,0:T(8,128)(2,1)} %select_select_fusion), calls=%async_computation.6 | async-start | bytes 6291456 | tf_op jit(solution)/shard_map/all_to_all | solution.py:119
  132.9 161.9 %all-gather.19.cloned.1.call-start = ((), (), s32[]{:S(2)}) async-start(), calls=%async_computation.31 | async-start | bytes 4718592 | tf_op jit(solution)/shard_map/all_gather | solution.py:97
  212.3 74.7 %all-to-all-start.2 = ((bf16[8,2,96,1024]{3,2,1,0:T(8,128)(2,1)}), bf16[8,2,96,1024]{3,2,1,0:T(8,128)(2,1)}, u32[]{:S(2)}, u32[]{:S(2)}) async-start(bf16[8,2,96,1024]{3,2,1,0:T(8,128)(2,1)} %multiply_convert_fusion), calls=%async_computation.15 | async-start | bytes 6291456 | tf_op jit(solution)/shard_map/all_to_all | solution.py:119
  216.8 93.3 %all-gather.17.cloned.1.call-start = ((), (), s32[]{:S(2)}) async-start(), calls=%async_computation.27 | async-start | bytes 4718592 | tf_op jit(solution)/shard_map/all_gather | solution.py:97
  217.4 129.3 %all-gather.25.cloned.1.call-start = ((), (), s32[]{:S(2)}) async-start(), calls=%async_computation.39 | async-start | bytes 7864320 | tf_op jit(solution)/shard_map/all_gather | solution.py:144
  291.1 72.9 %reduce-scatter.35.cloned.1.call-start = ((), (), s32[]{:S(2)}) async-start(), calls=%async_computation.32 | async-start | bytes 6488064 | tf_op jit(solution)/shard_map/reduce_scatter | solution.py:106
  301.6 76.7 %reduce-scatter.37.cloned.1.call-start = ((), (), s32[]{:S(2)}) async-start(), calls=%async_computation.33 | async-start | bytes 6488064 | tf_op jit(solution)/shard_map/reduce_scatter | solution.py:107
  309.5 118.5 %all-gather.23.cloned.1.call-start = ((), (), s32[]{:S(2)}) async-start(), calls=%async_computation.37 | async-start | bytes 7864320 | tf_op jit(solution)/shard_map/all_gather | solution.py:144
  310.1 135.1 %reduce-scatter.29.cloned.1.call-start = ((), (), s32[]{:S(2)}) async-start(), calls=%async_computation.28 | async-start | bytes 6488064 | tf_op jit(solution)/shard_map/reduce_scatter | solution.py:106
  317.3 142.1 %reduce-scatter.31.cloned.1.call-start = ((), (), s32[]{:S(2)}) async-start(), calls=%async_computation.29 | async-start | bytes 6488064 | tf_op jit(solution)/shard_map/reduce_scatter | solution.py:107
  324.2 149.3 %all-gather.33.cloned.1.call-start = ((), (), s32[]{:S(2)}) async-start(), calls=%async_computation.45 | async-start | bytes 3244032 | tf_op jit(solution)/shard_map/all_gather | solution.py:113
  387.6 99.7 %all-gather.35.cloned.1.call-start = ((), (), s32[]{:S(2)}) async-start(), calls=%async_computation.46 | async-start | bytes 3244032 | tf_op jit(solution)/shard_map/all_gather | solution.py:114
  388.2 113.0 %all-gather.29.cloned.1.call-start = ((), (), s32[]{:S(2)}) async-start(), calls=%async_computation.43 | async-start | bytes 3244032 | tf_op jit(solution)/shard_map/all_gather | solution.py:113
  468.7 46.3 %all-gather.31.cloned.1.call-start = ((), (), s32[]{:S(2)}) async-start(), calls=%async_computation.44 | async-start | bytes 3244032 | tf_op jit(solution)/shard_map/all_gather | solution.py:114
  469.2 131.8 %reduce-scatter.45.cloned.1.call-start = ((), (), s32[]{:S(2)}) async-start(), calls=%async_computation.40 | async-start | bytes 9437184 | tf_op jit(solution)/shard_map/reduce_scatter | solution.py:101
  496.6 183.8 %reduce-scatter.43.cloned.1.call-start = ((), (), s32[]{:S(2)}) async-start(), calls=%async_computation.38 | async-start | bytes 9437184 | tf_op jit(solution)/shard_map/reduce_scatter | solution.py:101
  524.2 174.5 %all-gather.21.cloned.1.call-start = ((), (), s32[]{:S(2)}) async-start(), calls=%async_computation.35 | async-start | bytes 1310720 | tf_op jit(solution)/shard_map/all_gather | solution.py:144
  524.9 185.4 %reduce-scatter.25.cloned.1.call-start = ((), (), s32[]{:S(2)}) async-start(), calls=%async_computation.25 | async-start | bytes 2162688 | tf_op jit(solution)/shard_map/reduce_scatter | solution.py:107
  545.5 178.0 %reduce-scatter.23.cloned.1.call-start = ((), (), s32[]{:S(2)}) async-start(), calls=%async_computation.24 | async-start | bytes 2162688 | tf_op jit(solution)/shard_map/reduce_scatter | solution.py:106
  549.9 276.4 %reduce-scatter.39.cloned.1.call-start = ((), (), s32[]{:S(2)}) async-start(), calls=%async_computation.34 | async-start | bytes 15728640 | tf_op jit(solution)/shard_map/reduce_scatter | solution.py:138
  561.0 366.9 %reduce-scatter.33.cloned.1.call-start = ((), (), s32[]{:S(2)}) async-start(), calls=%async_computation.30 | async-start | bytes 15728640 | tf_op jit(solution)/shard_map/reduce_scatter | solution.py:138
  684.7 247.6 %all-to-all-start.3 = ((bf16[8,2,96,1024]{3,2,1,0:T(8,128)(2,1)}), bf16[8,2,96,1024]{3,2,1,0:T(8,128)(2,1)}, u32[]{:S(2)}, u32[]{:S(2)}) async-start(bf16[8,2,96,1024]{3,2,1,0:T(8,128)(2,1)} %pad_maximum_fusion.6), calls=%async_computation.18 | async-start | bytes 6291456 | tf_op jit(solution)/shard_map/all_to_all | solution.py:123
  932.3 76.3 %all-to-all-start.1 = ((bf16[8,2,96,1024]{3,2,1,0:T(8,128)(2,1)}), bf16[8,2,96,1024]{3,2,1,0:T(8,128)(2,1)}, u32[]{:S(2)}, u32[]{:S(2)}) async-start(bf16[8,2,96,1024]{3,2,1,0:T(8,128)(2,1)} %pad_maximum_fusion.5), calls=%async_computation.13 | async-start | bytes 6291456 | tf_op jit(solution)/shard_map/all_to_all | solution.py:123
  937.8 87.0 %reduce-scatter.41.cloned.1.call-start = ((), (), s32[]{:S(2)}) async-start(), calls=%async_computation.36 | async-start | bytes 1572864 | tf_op jit(solution)/shard_map/reduce_scatter | solution.py:101
  942.2 86.8 %reduce-scatter.27.cloned.1.call-start = ((), (), s32[]{:S(2)}) async-start(), calls=%async_computation.26 | async-start | bytes 2621440 | tf_op jit(solution)/shard_map/reduce_scatter | solution.py:138
  948.3 98.5 %all-gather.27.cloned.1.call-start = ((), (), s32[]{:S(2)}) async-start(), calls=%async_computation.41 | async-start | bytes 1310720 | tf_op jit(solution)/shard_map/all_gather | solution.py:144
  1031.8 141.2 %reduce-scatter.47.cloned.1.call-start = ((), (), s32[]{:S(2)}) async-start(), calls=%async_computation.42 | async-start | bytes 1572864 | tf_op jit(solution)/shard_map/reduce_scatter | solution.py:101
  1075.9 541.4 %all-reduce.9.cloned.1.call-start = ((), (), s32[]{:S(2)}) async-start(), calls=%async_computation.47 | async-start | bytes 32243712 | tf_op jit(solution)/shard_map/psum | solution.py:424
  (94 other events, 660.2 us)
Sparse Core Ops, SparseCore 0:
  27.1 20.3 all-reduce.6
  50.4 9.1 reduce-scatter.18
  62.4 9.6 reduce-scatter.16
  79.9 32.5 reduce-scatter.20
  208.1 43.0 all-gather.18
  253.2 44.9 all-gather.16
  300.3 46.3 all-gather.24
  349.6 12.1 reduce-scatter.34
  364.8 13.4 reduce-scatter.36
  380.3 47.6 all-gather.22
  430.8 12.1 reduce-scatter.28
  445.9 13.4 reduce-scatter.30
  461.5 11.9 all-gather.32
  475.4 11.8 all-gather.34
  489.3 11.8 all-gather.28
  503.1 11.8 all-gather.30
  517.1 83.8 reduce-scatter.44
  603.3 77.0 reduce-scatter.42
  681.9 16.6 all-gather.20
  701.3 8.9 reduce-scatter.24
  713.2 10.1 reduce-scatter.22
  726.0 100.2 reduce-scatter.38
  828.9 99.0 reduce-scatter.32
  942.3 20.7 reduce-scatter.40
  966.3 31.3 reduce-scatter.26
  1031.9 14.8 all-gather.26
  1076.0 28.6 reduce-scatter.46
  1116.2 501.0 all-reduce.8
where the time goes:
time: 1650 us; the launch traced here: 1640 us
  waiting for transfers between devices  1070 us (65%)
  matrix products  177 us (11%)
  blocking collectives  136 us (8%)
  local copies, waits for them, and re-layouts  123 us (7%)
  other arithmetic  100 us (6%)
  starting transfers between devices  23.8 us (1%)
    psum x1, waiting for transfers between devices, local(): lax.psum(grad_wq.astype(jnp.bfloat16), 'exp').astype(jnp.float32)  396 us
    reduce_scatter x4, waiting for transfers between devices, spread_down(): lax.psum_scatter(jnp.concatenate(pieces, axis=0), ('row', 'col'), scatter...  216 us
    all_to_all x2, waiting for transfers between devices, send_to_experts(): lax.all_to_all(buffer, 'exp', split_axis=0, concat_axis=0, tiled=True)  126 us
    reduce_scatter x4, waiting for transfers between devices, scatter_rows(): return lax.psum_scatter(values, 'row', scatter_dimension=0, tiled=True)  105 us
    all_gather x4, waiting for transfers between devices, collect_down(): gathered = lax.all_gather(block, ('row', 'col'), axis=0, tiled=True)  75.7 us
    dot_general x13, matrix products, matmul_right(): lax.dot_general(former, latter, (((1,), (1,)), ((), ())), preferred_eleme...  70.8 us
    dot_general x25, matrix products, matmul(): return jnp.dot(former, latter, preferred_element_type=jnp.float32)  58.6 us
    all_to_all x2, waiting for transfers between devices, send_to_sources(): lax.all_to_all(buffer, 'exp', split_axis=0, concat_axis=0, tiled=True)  48.9 us
  transfers between devices with their start and end apart: 32, of which 24 were waited for; matrix products, arithmetic and copies ran while one was open for 19% of the time, Pallas kernels for 0%

commit v1 on v0

v1 whole, which is shorter than its diff:
```python
import functools

import jax
import jax.numpy as jnp
from jax import lax
from jax.experimental import pallas as pl
from jax.experimental.pallas import tpu as pltpu
from jax.sharding import PartitionSpec as P

DN = 128
DR = 64
DV = 128
R = 512
TOP = 6


EPSILON = 1e-06
ROPE_BASE = 50000.0
NEGATIVE = -1e30


def matmul(former, latter):
    return jnp.dot(former, latter, preferred_element_type=jnp.float32)


def matmul_left(former, latter):
    return lax.dot_general(
        former, latter, (((0,), (0,)), ((), ())), preferred_element_type=jnp.float32
    )


def matmul_right(former, latter):
    return lax.dot_general(
        former, latter, (((1,), (1,)), ((), ())), preferred_element_type=jnp.float32
    )


def sequence_layout(lengths, group_size):
    seq_ends = jnp.cumsum(lengths)
    token_order = jnp.arange(group_size, dtype=jnp.int32)
    segment = jnp.sum((token_order[:, None] >= seq_ends[None, :]).astype(jnp.int32), axis=1)
    seq_starts = seq_ends - lengths
    own_start = jnp.sum(
        jnp.where(
            segment[:, None] == jnp.arange(lengths.shape[0], dtype=jnp.int32)[None, :],
            seq_starts[None, :],
            0,
        ),
        axis=1,
    )
    return (segment, token_order - own_start)


def rope_tables(places):
    inverse_frequency = ROPE_BASE ** (-(jnp.arange(DR // 2, dtype=jnp.float32) * 2.0 / DR))
    angles = places.astype(jnp.float32)[:, None] * inverse_frequency[None, :]
    return (jnp.cos(angles), jnp.sin(angles))


MESH = pl.DeviceIdType.MESH
VMEM_LIMIT = 60 * 1024 * 1024
HALF = 2


def full_spec(array):
    zeros = (0,) * array.ndim
    return pl.BlockSpec(array.shape, lambda *_: zeros)


ANY_SPEC = pl.BlockSpec(memory_space=pl.ANY)


def swap_core(values):
    return lax.ppermute(values, "col", [(0, 1), (1, 0)])


def half_sums(values):
    return lax.psum(values, "col")


def norm_backward(gradient, normed, inverse_rms, gain_vector):
    full_width = normed.shape[1] * lax.axis_size("col")
    scaled = gradient * gain_vector
    inner_sum = half_sums(jnp.sum(scaled * normed, axis=1)) / full_width
    return (
        inverse_rms * (scaled - normed * inner_sum[:, None]),
        jnp.sum(gradient * normed, axis=0),
    )


def rotary(values, cosine_both, sine_signed):
    half = values.shape[-1] // 2
    swapped = jnp.concatenate([values[:, half:], values[:, :half]], axis=-1)
    return values * cosine_both + swapped * sine_signed


def project_kernel(
    _, own, other, gain_own, gain_other, query_own, query_other, latent_own, latent_other,
    latent_gain, keyvalue_weight, cosine_both, sine_signed, query, keyvalue, rope_key, *rest,
    everyone
):
    rows_own = own[...].astype(jnp.float32)
    rows_other = other[...].astype(jnp.float32)
    total = jnp.sum(rows_own * rows_own, axis=1, keepdims=True)
    total = total + jnp.sum(rows_other * rows_other, axis=1, keepdims=True)
    scale = lax.rsqrt(total / (2 * own.shape[1]) + EPSILON)
    rows_own = (rows_own * scale * gain_own[:1]).astype(jnp.bfloat16)
    rows_other = (rows_other * scale * gain_other[:1]).astype(jnp.bfloat16)
    queries = matmul(rows_own, query_own[...]) + matmul(rows_other, query_other[...])
    cosine, sine = cosine_both[...], sine_signed[...]
    for first in range(0, query.shape[1], DN + DR):
        rope = rotary(queries[:, first + DN : first + DN + DR], cosine, sine)
        query[:, first : first + DN + DR] = jnp.concatenate(
            [queries[:, first : first + DN], rope], axis=1
        ).astype(jnp.bfloat16)
    latent = matmul_right(rows_own, latent_own[...]) + matmul_right(rows_other, latent_other[...])
    raw = latent[:, :R]
    latent_scale = lax.rsqrt(jnp.mean(raw * raw, axis=1, keepdims=True) + EPSILON)
    latent_normed = raw * latent_scale
    compressed = (latent_normed * latent_gain[...]).astype(jnp.bfloat16)
    keyvalue[...] = matmul(compressed, keyvalue_weight[...]).astype(jnp.bfloat16)
    rope_key[...] = rotary(latent[:, R:], cosine, sine).astype(jnp.bfloat16)
    if everyone:
        rest[0][...] = rows_own.T
        rest[1][...] = compressed.T
    else:
        rest[0][...] = latent_normed
        rest[1][...] = latent_scale


def project(col, own, other, cosine_both, sine_signed, weights, everyone):
    count, width = own.shape
    tile = min(256, count)
    query_width = weights[3].shape[1]
    keyvalue_width = weights[7].shape[1]

    def rows(columns):
        return pl.BlockSpec((tile, columns), lambda step, col: (step, 0))

    def turned(features):
        return pl.BlockSpec((features, tile), lambda step, col: (0, step))

    shapes = [
        ((count, query_width), jnp.bfloat16, rows(query_width)),
        ((count, keyvalue_width), jnp.bfloat16, rows(keyvalue_width)),
        ((count, DR), jnp.bfloat16, rows(DR)),
    ]
    if everyone:
        shapes += [
            ((width, count), jnp.bfloat16, turned(width)),
            ((R, count), jnp.bfloat16, turned(R)),
        ]
    else:
        shapes += [((count, R), jnp.float32, rows(R)), ((count, 1), jnp.float32, rows(1))]
    weight_specs = [full_spec(array) for array in weights]
    weight_specs[2] = pl.BlockSpec((width, query_width), lambda step, col: (0, col[0]))
    flops = 2 * count * (2 * width * (query_width + R + DR) + R * keyvalue_width)
    return pl.pallas_call(
        functools.partial(project_kernel, everyone=everyone),
        out_shape=[jax.ShapeDtypeStruct(shape, kind) for shape, kind, _ in shapes],
        grid_spec=pltpu.PrefetchScalarGridSpec(
            num_scalar_prefetch=1,
            grid=(count // tile,),
            in_specs=[rows(width), rows(width)] + weight_specs + [rows(DR), rows(DR)],
            out_specs=[spec for _, _, spec in shapes],
        ),
        compiler_params=pltpu.CompilerParams(vmem_limit_bytes=VMEM_LIMIT),
        cost_estimate=pl.CostEstimate(
            flops=flops, bytes_accessed=count * 12000 + 7 * 1024 * 1024, transcendentals=0
        ),
    )(col, own, other, *weights, cosine_both, sine_signed)


def attention_kernel(
    lengths, query, keyvalue, rope_key, *rest, backward
):
    if backward:
        cosine_both, sine_signed, grad_out, attended, grad_query, grad_keyvalue, grad_rope = rest
        cosine, sine = cosine_both[...], sine_signed[...]
    else:
        (attended,) = rest
    group = pl.program_id(0)
    size = query.shape[0]
    heads = query.shape[1] // (DN + DR)
    factor = (DN + DR) ** (-0.5)
    row = lax.broadcasted_iota(jnp.int32, (size, size), 0)
    column = lax.broadcasted_iota(jnp.int32, (size, size), 1)
    allowed = column <= row
    end = jnp.int32(0)
    for number in range(lengths.shape[1] - 1):
        end = end + lengths[group, number]
        allowed = allowed & ((row < end) == (column < end))
    rope_keys = rope_key[...]
    rope_total = jnp.zeros((size, DR), jnp.float32)
    for head in range(heads):
        first = head * (DN + DR)
        queries = query[:, first : first + DN + DR]
        first_key = head * (DN + DV)
        keys = jnp.concatenate([keyvalue[:, first_key : first_key + DN], rope_keys], axis=1)
        values = keyvalue[:, first_key + DN : first_key + DN + DV]
        scores = jnp.where(allowed, matmul_right(queries, keys) * factor, NEGATIVE)
        exponent = jnp.exp(scores - jnp.max(scores, axis=1, keepdims=True))
        probabilities = exponent / jnp.sum(exponent, axis=1, keepdims=True)
        weights = probabilities.astype(jnp.bfloat16)
        result = matmul(weights, values).astype(jnp.bfloat16)
        if backward:
            attended[head * DV : (head + 1) * DV, :] = result.T
        else:
            attended[:, head * DV : (head + 1) * DV] = result
        if backward:
            grad_head = grad_out[:, head * DV : (head + 1) * DV]
            grad_probs = matmul_right(grad_head, values)
            inner = jnp.sum(probabilities * grad_probs, axis=1, keepdims=True)
            grad_scores = (probabilities * (grad_probs - inner)).astype(jnp.bfloat16)
            grad_queries = matmul(grad_scores, keys) * factor
            grad_keys = matmul_left(grad_scores, queries) * factor
            unrotated = rotary(grad_queries[:, DN:], cosine, -sine)
            grad_query[:, first : first + DN + DR] = jnp.concatenate(
                [grad_queries[:, :DN], unrotated], axis=1
            ).astype(jnp.bfloat16)
            grad_keyvalue[:, first_key : first_key + DN] = grad_keys[:, :DN].astype(jnp.bfloat16)
            grad_keyvalue[:, first_key + DN : first_key + DN + DV] = matmul_left(
                weights, grad_head
            ).astype(jnp.bfloat16)
            rope_total = rope_total + grad_keys[:, DN:]
    if backward:
        grad_rope[...] = rotary(rope_total, cosine, -sine)


def attend(
    lengths, query, keyvalue, rope_key, cosine_both=None, sine_signed=None, grad_out=None
):
    groups = lengths.shape[0]
    size = query.shape[0] // groups
    heads = query.shape[1] // (DN + DR)

    def block(width):
        return pl.BlockSpec((size, width), lambda group, lengths: (group, 0))

    def result(width, kind):
        return jax.ShapeDtypeStruct((groups * size, width), kind)

    operands = [query, keyvalue, rope_key]
    results = [result(heads * DV, jnp.bfloat16)]
    out_specs = [block(heads * DV)]
    if grad_out is not None:
        results = [jax.ShapeDtypeStruct((heads * DV, groups * size), jnp.bfloat16)]
        out_specs = [pl.BlockSpec((heads * DV, size), lambda group, lengths: (0, group))]
        operands += [cosine_both, sine_signed, grad_out]
        results += [
            result(heads * (DN + DR), jnp.bfloat16),
            result(heads * (DN + DV), jnp.bfloat16),
            result(DR, jnp.float32),
        ]
        out_specs += [block(array.shape[1]) for array in results[1:]]
    products = 7 if grad_out is not None else 2
    return pl.pallas_call(
        functools.partial(attention_kernel, backward=grad_out is not None),
        out_shape=results,
        grid_spec=pltpu.PrefetchScalarGridSpec(
            num_scalar_prefetch=1,
            grid=(groups,),
            in_specs=[block(array.shape[1]) for array in operands],
            out_specs=out_specs,
        ),
        compiler_params=pltpu.CompilerParams(vmem_limit_bytes=VMEM_LIMIT),
        cost_estimate=pl.CostEstimate(
            flops=groups * heads * products * 2 * size * size * 160,
            bytes_accessed=groups * size * heads * (1024 + 512 + 2000),
            transcendentals=groups * heads * size * size,
        ),
    )(lengths, *operands)


def positions():
    exp_count = lax.axis_size("exp")
    slow = min(4, exp_count)
    fast = exp_count // slow
    row_count = lax.axis_size("row")
    exp_index = lax.axis_index("exp")
    place = (exp_index // fast, exp_index % fast, lax.axis_index("row"), lax.axis_index("col"))
    return place, (slow, fast, row_count)


def peers(with_core):
    (slow_at, fast_at, row_at, col_at), (slow, fast, row_count) = positions()
    slow_ids = [
        {"exp": (slow_at + step) % slow * fast + fast_at} for step in range(1, slow)
    ]
    fast_ids = [
        {"exp": slow_at * fast + (fast_at + step) % fast} for step in range(1, fast)
    ]
    row_ids = [{"row": (row_at + step) % row_count} for step in range(1, row_count)]
    core_ids = [{"col": 1 - col_at}] if with_core else []
    return slow_ids, fast_ids, row_ids, core_ids


def enter(groups):
    barrier = pltpu.get_barrier_semaphore()
    count = 0
    for group in groups:
        for device in group:
            pl.semaphore_signal(barrier, inc=1, device_id=device, device_id_type=MESH)
            count += 1
    pl.semaphore_wait(barrier, count)


def remote(src, dst, sems, index, device):
    copy = pltpu.make_async_remote_copy(
        src_ref=src,
        dst_ref=dst,
        send_sem=sems.at[(0, *index)],
        recv_sem=sems.at[(1, *index)],
        device_id=device,
        device_id_type=MESH,
    )
    copy.start()
    return copy


def wait_arrived(dst, sems, index):
    pltpu.make_async_copy(dst, dst, sems.at[(1, *index)]).wait()


def start_kernel(
    rows, tables, query, latent, gain,
    rows_own, rows_other, tables_all, query_other, latent_other, gain_other,
    local_sems, row_sems, core_rows, slow_sems, fast_sems, core_sems
):
    (slow_at, fast_at, row_at, col_at), (slow, fast, row_count) = positions()
    slow_ids, fast_ids, row_ids, core_ids = peers(True)
    core = core_ids[0]
    width = query_other.shape[1]
    mine = slow_at * fast + fast_at
    given = pl.ds(pl.multiple_of((1 - col_at) * width, width), width)
    enter((slow_ids, fast_ids, row_ids, core_ids))
    kept = [
        pltpu.make_async_copy(rows, rows_own.at[row_at], local_sems.at[0]),
        pltpu.make_async_copy(tables, tables_all.at[mine], local_sems.at[1]),
    ]
    for copy in kept:
        copy.start()
    started = [
        remote(rows, rows_own.at[row_at], row_sems, (number,), device)
        for number, device in enumerate(row_ids)
    ]
    started.append(remote(rows, rows_other.at[row_at], core_rows, (0,), core))
    started.append(remote(gain, gain_other, core_sems, (0,), core))
    started.append(remote(query.at[:, given], query_other, core_sems, (1,), core))
    started.append(remote(latent, latent_other, core_sems, (2,), core))
    for number, device in enumerate(slow_ids):
        started.append(remote(tables, tables_all.at[mine], slow_sems, (number,), device))
    for number, device in enumerate(fast_ids):
        started.append(remote(tables, tables_all.at[mine], fast_sems, (number, 0), device))
    for offset in range(1, row_count):
        index = (row_at + row_count - offset) % row_count
        wait_arrived(rows_own.at[index], row_sems, (offset - 1,))
        started.append(
            remote(rows_own.at[index], rows_other.at[index], core_rows, (offset,), core)
        )
    for offset in range(1, slow):
        index = (slow_at + slow - offset) % slow * fast + fast_at
        wait_arrived(tables_all.at[index], slow_sems, (offset - 1,))
        for number, device in enumerate(fast_ids):
            started.append(
                remote(
                    tables_all.at[index], tables_all.at[index], fast_sems, (number, offset), device
                )
            )
    for offset in range(slow):
        for number in range(1, fast):
            index = (slow_at + slow - offset) % slow * fast + (fast_at + fast - number) % fast
            wait_arrived(tables_all.at[index], fast_sems, (number - 1, offset))
    for offset in range(row_count):
        index = (row_at + row_count - offset) % row_count
        wait_arrived(rows_other.at[index], core_rows, (offset,))
    for number, target in enumerate((gain_other, query_other, latent_other)):
        wait_arrived(target, core_sems, (number,))
    for copy in started:
        copy.wait_send()
    for copy in kept:
        copy.wait()


def begin(rows, tables, query, latent, gain, collective_id):
    exp_count, row_count = lax.axis_size("exp"), lax.axis_size("row")
    slow = min(4, exp_count)
    fast = exp_count // slow

    def like(*shape, array):
        return jax.ShapeDtypeStruct(shape, array.dtype)

    return pl.pallas_call(
        start_kernel,
        out_shape=[
            like(row_count, *rows.shape, array=rows),
            like(row_count, *rows.shape, array=rows),
            like(exp_count, *tables.shape, array=tables),
            like(query.shape[0], query.shape[1] // 2, array=query),
            like(*latent.shape, array=latent),
            like(*gain.shape, array=gain),
        ],
        in_specs=[ANY_SPEC] * 5,
        out_specs=[ANY_SPEC] * 6,
        scratch_shapes=[
            pltpu.SemaphoreType.DMA((2,)),
            pltpu.SemaphoreType.DMA((2, row_count - 1)),
            pltpu.SemaphoreType.DMA((2, row_count)),
            pltpu.SemaphoreType.DMA((2, slow - 1)),
            pltpu.SemaphoreType.DMA((2, fast - 1, slow)),
            pltpu.SemaphoreType.DMA((2, 3)),
        ],
        compiler_params=pltpu.CompilerParams(
            collective_id=collective_id, has_side_effects=True
        ),
    )(rows, tables, query, latent, gain)


def mix_kernel(
    attended, weight, rows, gain, hidden, normed, inverse, mixer,
    given, from_core, rows_out, from_rows, squares, squares_in, core_sems, row_sems
):
    (_, _, row_at, col_at), (_, _, row_count) = positions()
    _, _, row_ids, core_ids = peers(True)
    core = core_ids[0]
    count, width = rows.shape
    enter((row_ids, core_ids))
    own_half = pl.ds(pl.multiple_of(col_at * width, width), width)
    other_half = pl.ds(pl.multiple_of((1 - col_at) * width, width), width)
    given[...] = matmul(attended[...], weight[:, other_half]).astype(jnp.bfloat16)
    started = [remote(given, from_core, core_sems, (0,), core)]
    total = matmul(attended[...], weight[:, own_half])
    wait_arrived(from_core, core_sems, (0,))
    total = total + from_core[...].astype(jnp.float32)
    rows_out[...] = total.astype(jnp.bfloat16).reshape(rows_out.shape)
    for number, device in enumerate(row_ids):
        goal = (row_at + number + 1) % row_count
        started.append(remote(rows_out.at[goal], from_rows.at[number], row_sems, (number,), device))
    state = rows[...].astype(jnp.float32) + rows_out[row_at].astype(jnp.float32)
    for number in range(row_count - 1):
        wait_arrived(from_rows.at[number], row_sems, (number,))
        state = state + from_rows[number].astype(jnp.float32)
    hidden[...] = state
    own_squares = jnp.sum(state * state, axis=1, keepdims=True)
    squares[...] = jnp.broadcast_to(own_squares, squares.shape)
    started.append(remote(squares, squares_in, core_sems, (1,), core))
    wait_arrived(squares_in, core_sems, (1,))
    scale = lax.rsqrt((squares[...] + squares_in[...]) / (2 * width) + EPSILON)
    inverse[...] = scale
    unit = state * scale[:, :1]
    normed[...] = unit
    mixer[...] = (unit * gain[...]).astype(jnp.bfloat16)
    for copy in started:
        copy.wait_send()


def mix(attended, weight, rows, gain, collective_id):
    row_count = lax.axis_size("row")
    count, width = rows.shape
    vmem = pl.BlockSpec(memory_space=pltpu.VMEM)
    wide = jax.ShapeDtypeStruct((count, width), jnp.float32)
    return pl.pallas_call(
        mix_kernel,
        out_shape=[
            wide,
            wide,
            jax.ShapeDtypeStruct((count, 128), jnp.float32),
            jax.ShapeDtypeStruct((count, width), jnp.bfloat16),
        ],
        in_specs=[vmem] * 4,
        out_specs=[vmem] * 4,
        scratch_shapes=[
            pltpu.VMEM((row_count * count, width), jnp.bfloat16),
            pltpu.VMEM((row_count * count, width), jnp.bfloat16),
            pltpu.VMEM((row_count, count, width), jnp.bfloat16),
            pltpu.VMEM((row_count - 1, count, width), jnp.bfloat16),
            pltpu.VMEM((count, 128), jnp.float32),
            pltpu.VMEM((count, 128), jnp.float32),
            pltpu.SemaphoreType.DMA((2, 2)),
            pltpu.SemaphoreType.DMA((2, row_count - 1)),
        ],
        compiler_params=pltpu.CompilerParams(
            collective_id=collective_id, has_side_effects=True, vmem_limit_bytes=VMEM_LIMIT
        ),
    )(attended, weight, rows, gain)


def gather_kernel(
    source, own, other, local_sem, slow_sems, fast_sems, row_sems, low_sems, high_sems,
    core_sems, core_half_sems
):
    (slow_at, fast_at, row_at, _), (slow, fast, row_count) = positions()
    slow_ids, fast_ids, row_ids, core_ids = peers(True)
    core = core_ids[0]
    half = source.shape[0] // 2
    low, high = pl.ds(0, half), pl.ds(half, half)
    started = []

    def block(slow_off, fast_off, row_off):
        slow_index = (slow_at + slow - slow_off) % slow
        fast_index = (fast_at + fast - fast_off) % fast
        return (slow_index * fast + fast_index) * row_count + (row_at + row_count - row_off) % row_count

    def send(src, dst, sems, index, device):
        copy = pltpu.make_async_remote_copy(
            src_ref=src,
            dst_ref=dst,
            send_sem=sems.at[(0, *index)],
            recv_sem=sems.at[(1, *index)],
            device_id=device,
            device_id_type=MESH,
        )
        copy.start()
        started.append(copy)

    def arrived(dst, sems, index):
        pltpu.make_async_copy(dst, dst, sems.at[(1, *index)]).wait()

    enter((slow_ids, fast_ids, row_ids, core_ids))
    mine = block(0, 0, 0)
    keep = pltpu.make_async_copy(source, own.at[mine], local_sem)
    keep.start()
    for number, device in enumerate(slow_ids):
        send(source, own.at[mine], slow_sems, (number,), device)

    def forward_line(src, index, line):
        for number, device in enumerate(fast_ids):
            send(src, own.at[index], fast_sems, (number, line), device)
        for number, device in enumerate(row_ids):
            send(src, own.at[index], row_sems, (number, line), device)
        send(src, other.at[index], core_sems, (0, 0, line), core)

    forward_line(source, mine, 0)
    for line in range(1, slow):
        index = block(line, 0, 0)
        arrived(own.at[index], slow_sems, (line - 1,))
        forward_line(own.at[index], index, line)
    for line in range(slow):
        for fast_off in range(1, fast):
            index = block(line, fast_off, 0)
            arrived(own.at[index], fast_sems, (fast_off - 1, line))
            for number, device in enumerate(row_ids):
                send(
                    own.at[index, low], own.at[index, low], low_sems,
                    (fast_off - 1, number, line), device,
                )
            send(own.at[index], other.at[index], core_sems, (fast_off, 0, line), core)
        for row_off in range(1, row_count):
            index = block(line, 0, row_off)
            arrived(own.at[index], row_sems, (row_off - 1, line))
            for number, device in enumerate(fast_ids):
                send(
                    own.at[index, high], own.at[index, high], high_sems,
                    (number, row_off - 1, line), device,
                )
            send(own.at[index], other.at[index], core_sems, (0, row_off, line), core)
    for line in range(slow):
        for fast_off in range(1, fast):
            for row_off in range(1, row_count):
                index = block(line, fast_off, row_off)
                spot = (fast_off - 1, row_off - 1, line)
                for number, (rows, sems) in enumerate(((low, low_sems), (high, high_sems))):
                    arrived(own.at[index, rows], sems, spot)
                    send(
                        own.at[index, rows], other.at[index, rows], core_half_sems,
                        (number, *spot), core,
                    )
    for line in range(slow):
        for fast_off in range(fast):
            for row_off in range(row_count):
                index = block(line, fast_off, row_off)
                if fast_off and row_off:
                    spot = (fast_off - 1, row_off - 1, line)
                    for number, rows in enumerate((low, high)):
                        arrived(other.at[index, rows], core_half_sems, (number, *spot))
                else:
                    arrived(other.at[index], core_sems, (fast_off, row_off, line))
    for copy in started:
        copy.wait_send()
    keep.wait()


def gather_everywhere(values, collective_id):
    exp_count, row_count = lax.axis_size("exp"), lax.axis_size("row")
    slow = min(4, exp_count)
    fast = exp_count // slow
    rows, width = values.shape
    blocks = exp_count * row_count
    result = jax.ShapeDtypeStruct((blocks, rows, width), values.dtype)
    own, other = pl.pallas_call(
        gather_kernel,
        out_shape=[result, result],
        in_specs=[ANY_SPEC],
        out_specs=[ANY_SPEC, ANY_SPEC],
        scratch_shapes=[
            pltpu.SemaphoreType.DMA,
            pltpu.SemaphoreType.DMA((2, slow - 1)),
            pltpu.SemaphoreType.DMA((2, fast - 1, slow)),
            pltpu.SemaphoreType.DMA((2, row_count - 1, slow)),
            pltpu.SemaphoreType.DMA((2, fast - 1, row_count - 1, slow)),
            pltpu.SemaphoreType.DMA((2, fast - 1, row_count - 1, slow)),
            pltpu.SemaphoreType.DMA((2, fast, row_count, slow)),
            pltpu.SemaphoreType.DMA((2, 2, fast - 1, row_count - 1, slow)),
        ],
        compiler_params=pltpu.CompilerParams(
            collective_id=collective_id, has_side_effects=True
        ),
        cost_estimate=pl.CostEstimate(
            flops=0, bytes_accessed=4 * blocks * rows * width * 4, transcendentals=0
        ),
    )(values)
    return own.reshape(blocks * rows, width), other.reshape(blocks * rows, width)


def scatter_kernel(*refs, backward):
    if backward:
        gating, upward, gate, up, own_gating, own_upward, shared_gate, shared_up = refs[:8]
        lefts = [gating.at[0], gating.at[1], upward.at[0], upward.at[1]]
        refs = refs[8:]
    else:
        hidden, down, down_other, own_hidden, other_hidden, shared, shared_other = refs[:7]
        lefts = [hidden.at[0], hidden.at[1]]
        refs = refs[7:]
    count = len(lefts)
    (
        result, left_tiles, rights, extra_left, extra_right, part, from_row, from_fast,
        from_fast_late, from_row_late, from_slow,
        left_sems, right_sems, extra_sems, row_sems, fast_sems, fast_late_sems, row_late_sems,
        slow_sems,
    ) = refs
    (slow_at, fast_at, row_at, col_at), (slow, fast, row_count) = positions()
    slow_ids, fast_ids, row_ids, core_ids = peers(False)
    exp_count = slow * fast
    exp_index = lax.axis_index("exp")
    rows, width = result.shape
    half = rows // 2
    low, high = pl.ds(0, half), pl.ds(half, half)
    group = rows * row_count
    group_rows = pl.ds(pl.multiple_of(exp_index * group, group), group)
    own_half = pl.ds(pl.multiple_of(col_at * width, width), width)

    def slow_of(turn):
        return (slow_at + 1 + turn) % slow

    def order(step):
        return slow_of(step // fast) * fast + (fast_at + 1 + step % fast) % fast

    def loads(step, slot):
        first = pl.multiple_of(order(step) * group, group)
        return [
            pltpu.make_async_copy(
                left.at[:, pl.ds(first, group)], left_tiles.at[slot, number],
                left_sems.at[slot, number],
            )
            for number, left in enumerate(lefts)
        ]

    if backward:
        right_pairs = [(array.at[side], rights.at[2 * number + side])
                       for number, array in enumerate((gate, up)) for side in range(2)]
        extra_pairs = [
            (own_gating.at[group_rows], extra_left.at[0]),
            (own_upward.at[group_rows], extra_left.at[1]),
            (shared_gate, extra_right.at[0]),
            (shared_up, extra_right.at[1]),
        ]
        extra_product = matmul_right
    else:
        split = down.shape[1]
        right_pairs = []
        for side in range(2):
            for source, place in ((down, col_at), (down_other, 1 - col_at)):
                spot = pl.ds(pl.multiple_of(place * split, 16), split)
                right_pairs.append((source.at[side, :, own_half], rights.at[side, spot]))
        extra_pairs = [
            (own_hidden.at[:, group_rows], extra_left.at[0]),
            (other_hidden, extra_left.at[1]),
            (shared.at[:, own_half], extra_right.at[0]),
            (shared_other.at[:, own_half], extra_right.at[1]),
        ]
        extra_product = matmul_left
    prepared = [
        pltpu.make_async_copy(source, target, right_sems.at[number])
        for number, (source, target) in enumerate(right_pairs)
    ]
    extras = [
        pltpu.make_async_copy(source, target, extra_sems.at[number])
        for number, (source, target) in enumerate(extra_pairs)
    ]
    for copy in prepared + loads(0, 0) + extras:
        copy.start()
    enter((slow_ids, fast_ids, row_ids))
    for copy in prepared:
        copy.wait()

    def make(step):
        slot = step % 2

        @pl.when(step + 1 < exp_count)
        def _():
            for copy in loads(step + 1, 1 - slot):
                copy.start()

        for copy in loads(step, slot):
            copy.wait()
        index = order(step)
        total = matmul_left(left_tiles[slot, 0], rights[0])
        for number in range(1, count):
            total = total + matmul_left(left_tiles[slot, number], rights[number])
        part[index] = total.astype(jnp.bfloat16).reshape(row_count, rows, width)

        @pl.when(step == exp_count - 1)
        def _():
            for copy in extras:
                copy.wait()
            extra = extra_product(extra_left[0], extra_right[0])
            extra = extra + extra_product(extra_left[1], extra_right[1])
            before = part[index].astype(jnp.float32)
            part[index] = (before + extra.reshape(before.shape)).astype(jnp.bfloat16)

        for number, device in enumerate(row_ids):
            goal = (row_at + number + 1) % row_count
            remote(
                part.at[index, goal, low], from_row.at[number, index], row_sems,
                (number, index), device,
            )
        slow_index = index // fast
        for number, device in enumerate(fast_ids):

            @pl.when(index % fast == (fast_at + number + 1) % fast)
            def _():
                for goal in range(row_count):
                    remote(
                        part.at[index, goal, high], from_fast.at[number, slow_index, goal],
                        fast_sems, (number, slow_index, goal), device,
                    )

    def add_up(index, goal, span, arrivals):
        total = part[index, goal, span].astype(jnp.float32)
        for buffer, sems, spot in arrivals:
            wait_arrived(buffer.at[spot], sems, spot)
            total = total + buffer[spot].astype(jnp.float32)
        return total

    def of_rows(index):
        return [(from_row, row_sems, (number, index)) for number in range(row_count - 1)]

    def of_fasts(slow_index, goal):
        return [
            (from_fast, fast_sems, (number, slow_index, goal)) for number in range(fast - 1)
        ]

    def second(slow_index):
        for number, device in enumerate(fast_ids):
            index = slow_index * fast + (fast_at + number + 1) % fast
            part[index, row_at, low] = add_up(index, row_at, low, of_rows(index)).astype(
                jnp.bfloat16
            )
            remote(
                part.at[index, row_at, low], from_fast_late.at[number, slow_index],
                fast_late_sems, (number, slow_index), device,
            )
        mine = slow_index * fast + fast_at
        for number, device in enumerate(row_ids):
            goal = (row_at + number + 1) % row_count
            part[mine, goal, high] = add_up(
                mine, goal, high, of_fasts(slow_index, goal)
            ).astype(jnp.bfloat16)
            remote(
                part.at[mine, goal, high], from_row_late.at[number, slow_index],
                row_late_sems, (number, slow_index), device,
            )

    def finish(slow_index, span, late):
        mine = slow_index * fast + fast_at
        if late == 0:
            arrivals = of_rows(mine) + [
                (from_fast_late, fast_late_sems, (number, slow_index))
                for number in range(fast - 1)
            ]
        else:
            arrivals = of_fasts(slow_index, row_at) + [
                (from_row_late, row_late_sems, (number, slow_index))
                for number in range(row_count - 1)
            ]
        return add_up(mine, row_at, span, arrivals)

    def third(number):
        slow_index = slow_of(number)
        mine = slow_index * fast + fast_at
        for late, span in enumerate((low, high)):
            part[mine, row_at, span] = finish(slow_index, span, late).astype(jnp.bfloat16)
            remote(
                part.at[mine, row_at, span], from_slow.at[late, number], slow_sems,
                (late, number), slow_ids[number],
            )

    for turn in range(slow + 1):
        if turn < slow:
            pl.loop(turn * fast, turn * fast + fast)(make)
        if turn >= 1:
            second(slow_of(turn - 1))
        if turn >= 2:
            third(turn - 2)
    for late, span in enumerate((low, high)):
        total = finish(slow_at, span, late)
        for number in range(slow - 1):
            wait_arrived(from_slow.at[late, number], slow_sems, (late, number))
            total = total + from_slow[late, number].astype(jnp.float32)
        result[span, :] = total

    def sent(src, sems, index):
        pltpu.make_async_copy(src, src, sems.at[(0, *index)]).wait()

    @pl.loop(0, exp_count)
    def _(index):
        for number in range(row_count - 1):
            sent(from_row.at[number, index], row_sems, (number, index))

    @pl.loop(0, slow)
    def _(slow_index):
        for number in range(fast - 1):
            for goal in range(row_count):
                spot = (number, slow_index, goal)
                sent(from_fast.at[spot], fast_sems, spot)
            sent(from_fast_late.at[number, slow_index], fast_late_sems, (number, slow_index))
        for number in range(row_count - 1):
            sent(from_row_late.at[number, slow_index], row_late_sems, (number, slow_index))

    for number in range(slow - 1):
        for late in range(2):
            sent(from_slow.at[late, number], slow_sems, (late, number))


def scatter_products(operands, backward, collective_id):
    exp_count, row_count = lax.axis_size("exp"), lax.axis_size("row")
    slow = min(4, exp_count)
    fast = exp_count // slow
    _, units, tokens = operands[0].shape
    rows = tokens // exp_count // row_count
    group = rows * row_count
    half = rows // 2
    kind = jnp.bfloat16
    if backward:
        count, (width, shared_units) = 4, operands[6].shape
        extra_shapes = [(2, group, shared_units), (2, width, shared_units)]
    else:
        count, shared_units, width = 2, operands[5].shape[0], operands[1].shape[2] // 2
        extra_shapes = [(2, shared_units, group), (2, shared_units, width)]
    return pl.pallas_call(
        functools.partial(scatter_kernel, backward=backward),
        out_shape=jax.ShapeDtypeStruct((rows, width), jnp.float32),
        in_specs=[ANY_SPEC] * len(operands),
        out_specs=pl.BlockSpec(memory_space=pltpu.VMEM),
        scratch_shapes=[
            pltpu.VMEM((2, count, units, group), kind),
            pltpu.VMEM((count, units, width), kind),
            pltpu.VMEM(extra_shapes[0], kind),
            pltpu.VMEM(extra_shapes[1], kind),
            pltpu.VMEM((exp_count, row_count, rows, width), kind),
            pltpu.VMEM((row_count - 1, exp_count, half, width), kind),
            pltpu.VMEM((fast - 1, slow, row_count, half, width), kind),
            pltpu.VMEM((fast - 1, slow, half, width), kind),
            pltpu.VMEM((row_count - 1, slow, half, width), kind),
            pltpu.VMEM((2, slow - 1, half, width), kind),
            pltpu.SemaphoreType.DMA((2, count)),
            pltpu.SemaphoreType.DMA((4,)),
            pltpu.SemaphoreType.DMA((4,)),
            pltpu.SemaphoreType.DMA((2, row_count - 1, exp_count)),
            pltpu.SemaphoreType.DMA((2, fast - 1, slow, row_count)),
            pltpu.SemaphoreType.DMA((2, fast - 1, slow)),
            pltpu.SemaphoreType.DMA((2, row_count - 1, slow)),
            pltpu.SemaphoreType.DMA((2, 2, slow - 1)),
        ],
        compiler_params=pltpu.CompilerParams(
            collective_id=collective_id, has_side_effects=True, vmem_limit_bytes=VMEM_LIMIT
        ),
        cost_estimate=pl.CostEstimate(
            flops=2 * tokens * units * width * count,
            bytes_accessed=tokens * units * count * 2 + 60 * 1024 * 1024,
            transcendentals=0,
        ),
    )(*operands)


def unit_grads(gating, upward, grad_hidden):
    sigmoid = jax.nn.sigmoid(gating)
    silu = gating * sigmoid
    grad_upward = (grad_hidden * silu).astype(jnp.bfloat16)
    grad_gating = (grad_hidden * upward * sigmoid * (1.0 + gating * (1.0 - sigmoid))).astype(
        jnp.bfloat16
    )
    return silu * upward, grad_gating, grad_upward


def units_kernel(
    mixer_own, mixer_other, grad_own, grad_other, token_weight,
    expert_gate, gate_other, expert_up, up_other, expert_down, down_other,
    shared_gate, shared_gate_other, shared_up, shared_up_other, shared_down, shared_down_other,
    all_mixer_own, all_mixer_other, all_grad_own, all_grad_other,
    expert_hidden, expert_gating, expert_upward, shared_hidden, shared_gating, shared_upward,
    mixer_turned,
    gates, ups, downs, shared_gates, shared_ups, shared_downs, tiles, shared_tiles,
    shared_turned, shared_rows,
    weight_sems, local_sems, send_sems, recv_sems, shared_local, shared_send, shared_recv,
    row_sems,
):
    step = pl.program_id(0)
    steps = pl.num_programs(0)
    col = lax.axis_index("col")
    core = {"col": 1 - col}
    tile, width = mixer_own.shape
    split = expert_down.shape[1]
    shared_split = shared_down.shape[0]
    shared_steps = steps // 2
    halves = [pl.ds(pl.multiple_of(side * width, width), width) for side in (col, 1 - col)]
    targets = [expert_hidden, expert_gating, expert_upward]
    shared_targets = [shared_gating, shared_upward]

    def weight_copies():
        pairs = [
            (expert_gate.at[col], gates.at[0]),
            (gate_other, gates.at[1]),
            (expert_up.at[col], ups.at[0]),
            (up_other, ups.at[1]),
        ]
        own_rows = pl.ds(pl.multiple_of(col * split, 16), split)
        other_rows = pl.ds(pl.multiple_of((1 - col) * split, 16), split)
        shared_own = pl.ds(pl.multiple_of(col * shared_split, 16), shared_split)
        shared_other = pl.ds(pl.multiple_of((1 - col) * shared_split, 16), shared_split)
        for side in range(2):
            pairs += [
                (expert_down.at[col, :, halves[side]], downs.at[side, own_rows]),
                (down_other.at[col, :, halves[side]], downs.at[side, other_rows]),
            ]
        pairs += [
            (shared_gate, shared_gates.at[0]),
            (shared_gate_other, shared_gates.at[1]),
            (shared_up, shared_ups.at[0]),
            (shared_up_other, shared_ups.at[1]),
        ]
        for side in range(2):
            pairs += [
                (shared_down.at[:, halves[side]], shared_downs.at[side, shared_own]),
                (shared_down_other.at[:, halves[side]], shared_downs.at[side, shared_other]),
            ]
        return [
            pltpu.make_async_copy(src, dst, weight_sems.at[number])
            for number, (src, dst) in enumerate(pairs)
        ]

    def row_copies(turn, slot):
        first = pl.multiple_of((col * shared_steps + turn) * tile, tile)
        arrays = (all_mixer_own, all_mixer_other, all_grad_own, all_grad_other)
        return [
            pltpu.make_async_copy(
                array.at[pl.ds(first, tile)], shared_rows.at[slot, number],
                row_sems.at[slot, number],
            )
            for number, array in enumerate(arrays)
        ]

    def results(at, slot):
        columns = pl.ds(pl.multiple_of(at * tile, tile), tile)
        local, far = [], []
        for number, target in enumerate(targets):
            spot = target.at[col, :, columns]
            local.append(
                pltpu.make_async_copy(tiles.at[slot, number], spot, local_sems.at[slot, number])
            )
            far.append(
                pltpu.make_async_remote_copy(
                    src_ref=tiles.at[slot, number],
                    dst_ref=spot,
                    send_sem=send_sems.at[slot, number],
                    recv_sem=recv_sems.at[number, at],
                    device_id=core,
                    device_id_type=MESH,
                )
            )
        return local, far

    def shared_results(turn, slot):
        first = pl.multiple_of((col * shared_steps + turn) * tile, tile)
        span = pl.ds(first, tile)
        own_rows = pl.ds(pl.multiple_of(col * shared_split, 16), shared_split)
        other_rows = pl.ds(pl.multiple_of((1 - col) * shared_split, 16), shared_split)
        pairs = [
            (shared_tiles.at[slot, number], target.at[span], shared_tiles.at[slot, number])
            for number, target in enumerate(shared_targets)
        ]
        pairs.append(
            (
                shared_turned.at[slot, own_rows], shared_hidden.at[:, span],
                shared_turned.at[slot, other_rows],
            )
        )
        local = [
            pltpu.make_async_copy(src, dst, shared_local.at[slot, number])
            for number, (src, dst, _) in enumerate(pairs)
        ]
        far = [
            pltpu.make_async_remote_copy(
                src_ref=src,
                dst_ref=dst,
                send_sem=shared_send.at[slot, number],
                recv_sem=shared_recv.at[number, turn],
                device_id=core,
                device_id_type=MESH,
            )
            for number, (_, dst, src) in enumerate(pairs)
        ]
        return local, far

    def wait_out(pair):
        local, far = pair
        for copy in local:
            copy.wait()
        for copy in far:
            copy.wait_send()

    weights_early = 8

    @pl.when(step == 0)
    def _():
        for copy in weight_copies() + row_copies(0, 0):
            copy.start()
        enter(([core],))
        for copy in weight_copies()[:weights_early]:
            copy.wait()

    slot = step % 2

    @pl.when(step >= 2)
    def _():
        wait_out(results(step - 2, slot))

    mixers = (mixer_own[...], mixer_other[...])
    grads = (grad_own[...], grad_other[...])
    mixer_turned[...] = mixers[0].T

    def both(pair, weights, product):
        return product(pair[0], weights[0]) + product(pair[1], weights[1])

    def turned(weights, pair):
        return matmul_right(weights[0], pair[0]) + matmul_right(weights[1], pair[1])

    scale = token_weight[:1, :]
    hidden, gating, upward = unit_grads(
        turned(gates, mixers), turned(ups, mixers), turned(downs, grads) * scale
    )
    tiles[slot, 0] = (hidden * scale).astype(jnp.bfloat16)
    tiles[slot, 1] = gating
    tiles[slot, 2] = upward
    local, far = results(step, slot)
    for copy in local + far:
        copy.start()

    @pl.when(step == 0)
    def _():
        for copy in weight_copies()[weights_early:]:
            copy.wait()

    @pl.when(step % 2 == 0)
    def _():
        turn = step // 2
        turn_slot = turn % 2

        @pl.when(turn >= 2)
        def _():
            wait_out(shared_results(turn - 2, turn_slot))

        for copy in row_copies(turn, turn_slot):
            copy.wait()

        @pl.when(turn + 1 < shared_steps)
        def _():
            for copy in row_copies(turn + 1, 1 - turn_slot):
                copy.start()

        rows = [shared_rows[turn_slot, number] for number in range(4)]
        hidden, gating, upward = unit_grads(
            both(rows[:2], shared_gates, matmul),
            both(rows[:2], shared_ups, matmul),
            both(rows[2:], shared_downs, matmul_right),
        )
        shared_tiles[turn_slot, 0] = gating
        shared_tiles[turn_slot, 1] = upward
        shared_turned[turn_slot] = hidden.astype(jnp.bfloat16).T
        local, far = shared_results(turn, turn_slot)
        for copy in local + far:
            copy.start()

    @pl.when(step == steps - 1)
    def _():
        for back in range(2):
            at = steps - 1 - back
            wait_out(results(at, at % 2))
            turn = shared_steps - 1 - back
            wait_out(shared_results(turn, turn % 2))

        @pl.loop(0, steps)
        def _(at):
            columns = pl.ds(pl.multiple_of(at * tile, tile), tile)
            for number, target in enumerate(targets):
                spot = target.at[1 - col, :, columns]
                pltpu.make_async_copy(spot, spot, recv_sems.at[number, at]).wait()

        @pl.loop(0, shared_steps)
        def _(turn):
            first = pl.multiple_of(((1 - col) * shared_steps + turn) * tile, tile)
            span = pl.ds(first, tile)
            for number, target in enumerate(shared_targets):
                pltpu.make_async_copy(
                    target.at[span], target.at[span], shared_recv.at[number, turn]
                ).wait()
            spot = shared_hidden.at[:, span]
            pltpu.make_async_copy(spot, spot, shared_recv.at[2, turn]).wait()


def run_units(mixer, grad, token_weight, weights, collective_id):
    tokens, width = mixer[0].shape
    tile = 256
    units = weights[0].shape[1]
    shared_units = weights[6].shape[1]
    rows = pl.BlockSpec((tile, width), lambda step: (step, 0))
    kind = jnp.bfloat16
    pair = jax.ShapeDtypeStruct((2, units, tokens), kind)
    shared = jax.ShapeDtypeStruct((tokens, shared_units), kind)
    half = jax.ShapeDtypeStruct((shared_units // 2, tokens), kind)
    steps = tokens // tile
    return pl.pallas_call(
        units_kernel,
        out_shape=[
            pair, pair, pair, half, shared, shared, jax.ShapeDtypeStruct((width, tokens), kind)
        ],
        grid=(steps,),
        in_specs=[rows] * 4
        + [pl.BlockSpec((8, tile), lambda step: (0, step))]
        + [ANY_SPEC] * (len(weights) + 4),
        out_specs=[ANY_SPEC] * 6 + [pl.BlockSpec((width, tile), lambda step: (0, step))],
        scratch_shapes=[
            pltpu.VMEM((2, units, width), kind),
            pltpu.VMEM((2, units, width), kind),
            pltpu.VMEM((2, units, width), kind),
            pltpu.VMEM((2, width, shared_units), kind),
            pltpu.VMEM((2, width, shared_units), kind),
            pltpu.VMEM((2, shared_units, width), kind),
            pltpu.VMEM((2, 3, units, tile), kind),
            pltpu.VMEM((2, 2, tile, shared_units), kind),
            pltpu.VMEM((2, shared_units, tile), kind),
            pltpu.VMEM((2, 4, tile, width), kind),
            pltpu.SemaphoreType.DMA((16,)),
            pltpu.SemaphoreType.DMA((2, 3)),
            pltpu.SemaphoreType.DMA((2, 3)),
            pltpu.SemaphoreType.DMA((3, steps)),
            pltpu.SemaphoreType.DMA((2, 3)),
            pltpu.SemaphoreType.DMA((2, 3)),
            pltpu.SemaphoreType.DMA((3, steps // 2)),
            pltpu.SemaphoreType.DMA((2, 4)),
        ],
        compiler_params=pltpu.CompilerParams(
            collective_id=collective_id, has_side_effects=True, vmem_limit_bytes=VMEM_LIMIT
        ),
        cost_estimate=pl.CostEstimate(
            flops=2 * tokens * units * width * 2 * 6,
            bytes_accessed=50 * 1024 * 1024,
            transcendentals=2 * tokens * units,
        ),
    )(*mixer, *grad, token_weight, *weights, *mixer, *grad)


def product_kernel(left, right, result):
    product = matmul(left[...].reshape(left.shape[-2:]), right[...])
    result[...] = product.reshape(result.shape)


def product_cost(tokens, left_rows, width, parts):
    return pl.CostEstimate(
        flops=2 * tokens * left_rows * width * parts,
        bytes_accessed=tokens * (left_rows * parts + width) * 2 + left_rows * width * parts * 4,
        transcendentals=0,
    )


def stacked_grads(left, right):
    parts, units, tokens = left.shape
    width = right.shape[1]
    return pl.pallas_call(
        product_kernel,
        out_shape=jax.ShapeDtypeStruct((parts, units, width), jnp.float32),
        grid=(parts,),
        in_specs=[
            pl.BlockSpec((1, units, tokens), lambda part: (part, 0, 0)),
            full_spec(right),
        ],
        out_specs=pl.BlockSpec((1, units, width), lambda part: (part, 0, 0)),
        compiler_params=pltpu.CompilerParams(vmem_limit_bytes=VMEM_LIMIT),
        cost_estimate=product_cost(tokens, units, width, parts),
    )(left, right)


def row_grads(left, right):
    features, tokens = left.shape
    units = right.shape[1]
    block = min(256, features)
    return pl.pallas_call(
        product_kernel,
        out_shape=jax.ShapeDtypeStruct((features, units), jnp.float32),
        grid=(features // block,),
        in_specs=[pl.BlockSpec((block, tokens), lambda step: (step, 0)), full_spec(right)],
        out_specs=pl.BlockSpec((block, units), lambda step: (step, 0)),
        compiler_params=pltpu.CompilerParams(vmem_limit_bytes=VMEM_LIMIT),
        cost_estimate=product_cost(tokens, features, units, 1),
    )(left, right)


def down_kernel(_, left, own, other, result):
    @pl.when(pl.program_id(1) == 0)
    def _():
        result[0] = matmul(left[0], own[...])

    @pl.when(pl.program_id(1) == 1)
    def _():
        result[0] = matmul(left[0], other[...])


def sided_grads(col, left, own, other, halved):
    parts, units, tokens = left.shape
    units = units // 2 if halved else units
    width = own.shape[1]
    whole = pl.BlockSpec((tokens, width), lambda part, side, col: (0, 0))
    return pl.pallas_call(
        down_kernel,
        out_shape=jax.ShapeDtypeStruct((parts, units, 2 * width), jnp.float32),
        grid_spec=pltpu.PrefetchScalarGridSpec(
            num_scalar_prefetch=1,
            grid=(parts, 2),
            in_specs=[
                pl.BlockSpec(
                    (1, units, tokens),
                    lambda part, side, col: (part, col[0] if halved else 0, 0),
                ),
                whole,
                whole,
            ],
            out_specs=pl.BlockSpec(
                (1, units, width), lambda part, side, col: (part, 0, (col[0] + side) % 2)
            ),
        ),
        compiler_params=pltpu.CompilerParams(vmem_limit_bytes=VMEM_LIMIT),
        cost_estimate=product_cost(tokens, units, 2 * width, parts),
    )(col, left, own, other)


def sums_kernel(
    source, result, running, slow_in, fast_in, row_in, core_in,
    slow_sems, fast_sems, row_sems, core_sems,
):
    slow_ids, fast_ids, row_ids, core_ids = peers(True)
    enter((slow_ids, fast_ids, row_ids, core_ids))
    total = source[...]
    stages = (
        (slow_ids, slow_in, slow_sems),
        (fast_ids, fast_in, fast_sems),
        (row_ids, row_in, row_sems),
        (core_ids, core_in, core_sems),
    )
    last = lax.broadcasted_iota(jnp.int32, source.shape, 0) == 2
    for stage, (devices, buffer, sems) in enumerate(stages):
        running[stage] = total
        copies = [
            pltpu.make_async_remote_copy(
                src_ref=running.at[stage],
                dst_ref=buffer.at[number],
                send_sem=sems.at[0, number],
                recv_sem=sems.at[1, number],
                device_id=device,
                device_id_type=MESH,
            )
            for number, device in enumerate(devices)
        ]
        for copy in copies:
            copy.start()
        for number, copy in enumerate(copies):
            copy.wait_recv()
            arrived = buffer[number]
            total = total + (jnp.where(last, arrived, 0.0) if stage == 3 else arrived)
        for copy in copies:
            copy.wait_send()
    result[...] = total


def sum_everywhere(values, collective_id):
    exp_count, row_count = lax.axis_size("exp"), lax.axis_size("row")
    slow = min(4, exp_count)
    fast = exp_count // slow
    counts = (slow - 1, fast - 1, row_count - 1, 1)
    vmem = pl.BlockSpec(memory_space=pltpu.VMEM)
    return pl.pallas_call(
        sums_kernel,
        out_shape=jax.ShapeDtypeStruct(values.shape, values.dtype),
        in_specs=[vmem],
        out_specs=vmem,
        scratch_shapes=[pltpu.VMEM((4, *values.shape), values.dtype)]
        + [pltpu.VMEM((count, *values.shape), values.dtype) for count in counts]
        + [pltpu.SemaphoreType.DMA((2, count)) for count in counts],
        compiler_params=pltpu.CompilerParams(
            collective_id=collective_id, has_side_effects=True
        ),
    )(values)


def local(
    layer_input,
    attention_gain,
    query_weight,
    latent_weight,
    latent_gain,
    keyvalue_weight,
    output_weight,
    feedforward_gain,
    shared_gate,
    shared_up,
    shared_down,
    expert_gate,
    expert_up,
    expert_down,
    sequence_lengths,
    expert_ids,
    expert_weights,
    output_grad,
):
    exp_index, row_index, col_index = (
        lax.axis_index("exp"),
        lax.axis_index("row"),
        lax.axis_index("col"),
    )
    exp_count = lax.axis_size("exp")
    local_tokens, half_width = layer_input.shape
    full_width = 2 * half_width
    per_device = expert_gate.shape[0]
    group_size = local_tokens * lax.axis_size("row")
    tokens = group_size * exp_count
    group_start = exp_index * group_size

    def part_of(array, side, axis):
        width = array.shape[axis] // 2
        return lax.dynamic_slice_in_dim(array, side * width, width, axis)

    def split_exchange(array, axis):
        return part_of(array, col_index, axis), swap_core(part_of(array, 1 - col_index, axis))

    def own_rows(array):
        return lax.dynamic_slice_in_dim(array, group_start, group_size, 0)

    col = col_index.reshape(1)
    top = expert_ids.shape[1]
    tables = jnp.concatenate(
        [
            expert_ids.astype(jnp.float32),
            expert_weights,
            jnp.broadcast_to(
                sequence_lengths.astype(jnp.float32), (group_size, sequence_lengths.shape[1])
            ),
        ],
        axis=1,
    )
    tables = jnp.pad(tables, ((0, 0), (0, 128 - tables.shape[1])))
    latent_turned = latent_weight.T
    gate_turned, up_turned = expert_gate.swapaxes(1, 2), expert_up.swapaxes(1, 2)
    gain_own = jnp.broadcast_to(attention_gain.astype(jnp.float32), (8, half_width))
    rows_own, rows_other, tables_all, query_other, latent_other, gain_other = begin(
        layer_input, tables, query_weight, latent_turned, gain_own, 6
    )
    rows_own = rows_own.reshape(group_size, half_width)
    rows_other = rows_other.reshape(group_size, half_width)
    tables_all = tables_all.reshape(tokens, -1)
    gate_other = swap_core(lax.dynamic_index_in_dim(gate_turned, 1 - col_index, 0, keepdims=False))
    up_other = swap_core(lax.dynamic_index_in_dim(up_turned, 1 - col_index, 0, keepdims=False))
    down_other = swap_core(expert_down)
    shared_gate_other = swap_core(shared_gate)
    shared_up_other = swap_core(shared_up)
    shared_down_other = swap_core(shared_down)
    weights = (
        gain_own, gain_other, query_weight, query_other, latent_turned, latent_other,
        latent_gain.astype(jnp.float32)[None], keyvalue_weight,
    )
    grad_own = lax.all_gather(output_grad, ("exp", "row"), axis=0, tiled=True)

    ids_all = tables_all[:, :top].astype(jnp.int32)
    router_all = tables_all[:, top : 2 * top]
    sequences = sequence_lengths.shape[1]
    lengths_all = tables_all[::group_size, 2 * top : 2 * top + sequences].astype(jnp.int32)

    def tables_of(lengths):
        _, places = jax.vmap(lambda one: sequence_layout(one, group_size))(lengths)
        cosine, sine = rope_tables(places.reshape(-1))
        return jnp.concatenate([cosine, cosine], axis=1), jnp.concatenate([-sine, sine], axis=1)

    own_cosine, own_sine = tables_of(sequence_lengths)
    cosine_all, sine_all = tables_of(lengths_all)

    query, keyvalue, rope_key, own_normed, own_scale = project(
        col, rows_own, rows_other, own_cosine, own_sine, weights, False
    )
    (attended,) = attend(sequence_lengths, query, keyvalue, rope_key)
    gain_two = feedforward_gain.astype(jnp.float32)
    residual = layer_input.astype(jnp.float32)
    hidden_state, normed_two, scale_two, mixer_input = mix(
        attended, output_weight, layer_input, gain_two[None], 7
    )
    scale_two = scale_two[:, :1]
    grad_own, mixer_input = lax.optimization_barrier((grad_own, mixer_input))
    grad_other = swap_core(grad_own)
    mixer = gather_everywhere(mixer_input, 0)
    late_input, mixer = lax.optimization_barrier((layer_input, mixer))
    input_own = lax.all_gather(late_input, ("exp", "row"), axis=0, tiled=True)

    own_expert = exp_index * per_device + col_index
    token_weight = jnp.sum(jnp.where(ids_all == own_expert, router_all, 0.0), axis=1)
    token_weight = jnp.broadcast_to(token_weight[None], (8, tokens))
    (
        both_hidden, both_gating, both_upward, shared_hidden, shared_gating, shared_upward,
        mixer_turned,
    ) = run_units(
        mixer,
        (grad_own, grad_other),
        token_weight,
        (
            gate_turned, gate_other, up_turned, up_other, expert_down, down_other,
            shared_gate, shared_gate_other, shared_up, shared_up_other,
            shared_down, shared_down_other,
        ),
        1,
    )
    mixer_grad = scatter_products(
        (
            both_gating, both_upward, gate_turned, up_turned, shared_gating, shared_upward,
            shared_gate, shared_up,
        ),
        True,
        2,
    )

    upstream = output_grad.astype(jnp.float32)
    grad_norm_two, gain_two_grad = norm_backward(mixer_grad, normed_two, scale_two, gain_two)
    grad_hidden = upstream + grad_norm_two
    stream_own, stream_other = gather_everywhere(grad_hidden.astype(jnp.bfloat16), 3)

    input_own, stream_own = lax.optimization_barrier((input_own, stream_own))
    input_other = swap_core(input_own)
    query_all, keyvalue_all, rope_key_all, attention_turned, compressed_turned = project(
        col, input_own, input_other, cosine_all, sine_all, weights, True
    )
    output_own, output_other = (
        part_of(output_weight, col_index, 1),
        part_of(output_weight, 1 - col_index, 1),
    )
    grad_heads = (
        matmul_right(stream_own, output_own) + matmul_right(stream_other, output_other)
    ).astype(jnp.bfloat16)
    attended_turned, grad_query, grad_keyvalue, grad_rope = attend(
        lengths_all, query_all, keyvalue_all, rope_key_all, cosine_all, sine_all, grad_heads
    )
    grad_query_other = swap_core(grad_query)

    grad_compressed = matmul_right(own_rows(grad_keyvalue), keyvalue_weight)
    scaled_latent = grad_compressed * latent_gain.astype(jnp.float32)
    latent_inner = jnp.mean(scaled_latent * own_normed, axis=1, keepdims=True)
    grad_craw = own_scale * (scaled_latent - own_normed * latent_inner)
    latent_gain_part = jnp.sum(grad_compressed * own_normed, axis=0)
    grad_latent = lax.psum(
        jnp.concatenate([grad_craw, own_rows(grad_rope)], axis=1), ("row", "col")
    ).astype(jnp.bfloat16)
    own_latent = lax.dynamic_slice_in_dim(grad_latent, row_index * local_tokens, local_tokens, 0)
    latent_all = lax.all_gather(own_latent, ("exp", "row"), axis=0, tiled=True)
    own_query = part_of(query_weight, col_index, 1)
    rows_query = matmul_right(own_rows(grad_query), own_query) + swap_core(
        matmul_right(own_rows(grad_query), query_other)
    )
    grad_rows_query = lax.psum_scatter(rows_query, "row", scatter_dimension=0, tiled=True)
    grad_attention_input = grad_rows_query + matmul_right(own_latent, latent_weight)
    inverse_one = lax.rsqrt(
        half_sums(jnp.sum(residual * residual, axis=1)) / full_width + EPSILON
    )[:, None]
    normed_one = residual * inverse_one
    gain_one = attention_gain.astype(jnp.float32)
    grad_norm_one, gain_one_grad = norm_backward(
        grad_attention_input, normed_one, inverse_one, gain_one
    )
    input_grad = grad_hidden + grad_norm_one

    other_hidden = swap_core(
        lax.dynamic_slice_in_dim(shared_hidden, group_start, group_size, 1)
    )
    produced = scatter_products(
        (
            both_hidden, expert_down, down_other, shared_hidden, other_hidden,
            shared_down, shared_down_other,
        ),
        False,
        4,
    )
    layer_result = (hidden_state + produced).astype(jnp.bfloat16)

    expert_gate_grad = stacked_grads(both_gating, mixer[0]).swapaxes(1, 2)
    expert_up_grad = stacked_grads(both_upward, mixer[0]).swapaxes(1, 2)
    expert_down_grad = sided_grads(col, both_hidden, grad_own, grad_other, True)
    shared_gate_grad = row_grads(mixer_turned, shared_gating)
    shared_up_grad = row_grads(mixer_turned, shared_upward)
    shared_down_grad = sided_grads(col, shared_hidden[None], grad_own, grad_other, False)[0]
    output_weight_grad = sided_grads(
        col, attended_turned[None], stream_own, stream_other, False
    )[0]
    keyvalue_weight_grad = matmul(compressed_turned, grad_keyvalue)
    query_weight_grad = sided_grads(
        col, attention_turned[None], grad_query, grad_query_other, False
    )[0]
    latent_weight_grad = matmul(attention_turned, latent_all)
    padded = jnp.pad(latent_gain_part, (0, half_width - latent_gain_part.shape[0]))
    sums = sum_everywhere(
        jnp.pad(jnp.stack([gain_one_grad, gain_two_grad, padded]), ((0, 5), (0, 0))), 5
    )
    return (
        layer_result,
        input_grad,
        sums[0],
        query_weight_grad,
        latent_weight_grad,
        sums[2, : latent_gain_part.shape[0]],
        keyvalue_weight_grad,
        output_weight_grad,
        sums[1],
        shared_gate_grad,
        shared_up_grad,
        shared_down_grad,
        expert_gate_grad,
        expert_up_grad,
        expert_down_grad,
    )


def solution(mesh):
    in_specs = (
        P(("exp", "row"), "col"),
        P("col"),
        P("col", "row"),
        P("col", None),
        P(),
        P(None, ("row", "col")),
        P(("row", "col"), None),
        P("col"),
        P("col", "row"),
        P("col", "row"),
        P(("row", "col"), None),
        P("exp", "col", "row"),
        P("exp", "col", "row"),
        P("exp", ("row", "col"), None),
        P("exp", None),
        P("exp", None),
        P("exp", None),
        P(("exp", "row"), "col"),
    )
    out_specs = (
        P(("exp", "row"), "col"),
        P(("exp", "row"), "col"),
        P("col"),
        P("col", "row"),
        P("col", None),
        P(),
        P(None, ("row", "col")),
        P(("row", "col"), None),
        P("col"),
        P("col", "row"),
        P("col", "row"),
        P(("row", "col"), None),
        P("exp", "col", "row"),
        P("exp", "col", "row"),
        P("exp", ("row", "col"), None),
    )
    return jax.shard_map(local, mesh=mesh, in_specs=in_specs, out_specs=out_specs, check_vma=False)
```

time: 1650 us -> 624 us (0.38)
  waiting for transfers between devices: 1070 us -> 26.4 us
  Pallas kernels: 0 us -> 484 us
  matrix products: 177 us -> 31.8 us
  local copies, waits for them, and re-layouts: 123 us -> 12.4 us
  blocking collectives: 136 us -> 26.5 us
  other arithmetic: 100 us -> 17.9 us
  starting transfers between devices: 23.8 us -> 2.85 us
    pallas_call x0 -> x20, Pallas kernels: none -> 484 us  [the longest x2 118 us: scatter_products(): pl.pallas_call(functools.partial(scatter_kernel, backward=backward), out_...]
    psum x2 -> x0, waiting for transfers between devices: 408 us -> none  [the longest x1 396 us: local(): lax.psum(grad_wq.astype(jnp.bfloat16), 'exp').astype(jnp.float32)]
    reduce_scatter x16 -> x1, waiting for transfers between devices: 385 us -> 0.01 us  [local(): lax.psum_scatter(rows_query, 'row', scatter_dimension=0, tiled=True)]
    all_to_all x4 -> x0, waiting for transfers between devices: 175 us -> none  [the longest x2 126 us: send_to_experts(): lax.all_to_all(buffer, 'exp', split_axis=0, concat_axis=0, tiled=True)]
    all_gather x10 -> x3, waiting for transfers between devices: 97.2 us -> 25.6 us  [the longest x1 25.6 us: local(): grad_own = lax.all_gather(output_grad, ('exp', 'row'), axis=0, tiled=True)]
    psum x3 -> x1, blocking collectives: 91.5 us -> 21.5 us  [local(): lax.psum(jnp.concatenate([grad_craw, own_rows(grad_rope)], axis=1), ('row...]
    dot_general x13 -> x6, matrix products: 70.8 us -> 18.2 us  [matmul_right(): lax.dot_general(former, latter, (((1,), (1,)), ((), ())), preferred_eleme...]
    dot_general x19 -> x0, matrix products: 48.1 us -> none  [the longest x13 41.6 us: matmul_left(): lax.dot_general(former, latter, (((0,), (0,)), ((), ())), preferred_eleme...]
  transfers between devices with their start and end apart: 32 -> 15, of which waited for: 24 -> 1; matrix products, arithmetic and copies ran while one was open for 19% -> 9% of each run, Pallas kernels for 0% -> 79%
where the time goes in v1:
time: 624 us; the launch traced here: 617 us
  Pallas kernels  484 us (78%)
  matrix products  31.8 us (5%)
  blocking collectives  26.5 us (4%)
  waiting for transfers between devices  26.4 us (4%)
  other arithmetic  17.9 us (3%)
  between operations  14.5 us (2%)
  local copies, waits for them, and re-layouts  12.4 us (2%)
    pallas_call x2, Pallas kernels, scatter_products(): pl.pallas_call(functools.partial(scatter_kernel, backward=backward), out_...  118 us
    pallas_call x2, Pallas kernels, gather_everywhere(): pl.pallas_call(gather_kernel, out_shape=[result, result], in_specs=[ANY_S...  96.9 us
    pallas_call x1, Pallas kernels, run_units(): pl.pallas_call(units_kernel, out_shape=[pair, pair, pair, half, shared, s...  56.4 us
    pallas_call x4, Pallas kernels, sided_grads(): pl.pallas_call(down_kernel, out_shape=jax.ShapeDtypeStruct((parts, units,...  47 us
    pallas_call x2, Pallas kernels, attend(): pl.pallas_call(functools.partial(attention_kernel, backward=grad_out is n...  33.1 us
    pallas_call x2, Pallas kernels, project(): pl.pallas_call(functools.partial(project_kernel, everyone=everyone), out_...  32.3 us
    pallas_call x1, Pallas kernels, begin(): pl.pallas_call(start_kernel, out_shape=[like(row_count, *rows.shape, arra...  26 us
    all_gather x1, waiting for transfers between devices, local(): grad_own = lax.all_gather(output_grad, ('exp', 'row'), axis=0, tiled=True)  25.6 us
  transfers between devices with their start and end apart: 15, of which 1 were waited for; matrix products, arithmetic and copies ran while one was open for 9% of the time, Pallas kernels for 79%

profile of v1, /device:TPU:0, one launch (start us, length us, event | category | flops | bytes accessed | tf_op | source)
XLA Modules:
  0.0 616.8 jit_solution(13916634525076304197)
XLA Ops:
  8.0 2.7 dynamic-slice_bitcast_fusion
  14.4 26.0 %shard_map.289 = (bf16[2,128,1024]{2,1,0:T(8,128)(2,1)}, bf16[2,128,1024]{2,1,0:T(8,128)(2,1)}, f32[8,256,128]{2,1,0:T(8,128)}, bf16[1024,768]{1,0:T(8,128)(2,1)...) custom-call(bf16[128,1024]{1,0:T(8,128)(2,1)} %rows.3, f32[256,128]{1,0:T(8,128)} %pad.12.tables, ...), custom_call_target="tpu_custom_call" | custom-call | tf_op jit(solution)/shard_map/pallas_call | solution.py:393
  42.0 6.9 %shard_map.290 = (bf16[256,768]{1,0:T(8,128)(2,1)}, bf16[256,1024]{1,0:T(8,128)(2,1)}, bf16[256,64]{1,0:T(8,128)(2,1)}, f32[256,512]{1,0:T(8,128)}, f32[256,1]{1,0:T(8,128)}) custom-call(s32[1]{0:T(128)} %bitcast._, bf16[256,1024]{1,0:T(8,128)(2,1)} %bitcast.62, bf16[256,1024]{1,0:T(8,128)(2,1)} %bitcast.63, f32[8,1024]{1,0:T(8,128)} %broadcast_in_dim.50.gain.gain_own, ...), custom_call_target="tpu_custom_call" | custom-call | flops 1677721600 | bytes 10412032 | tf_op jit(solution)/shard_map/pallas_call | solution.py:158
  48.9 3.8 shard_map.291.attended
  52.7 15.2 %shard_map.292 = (f32[128,1024]{1,0:T(8,128)}, f32[128,1024]{1,0:T(8,128)}, f32[128,128]{1,0:T(8,128)}, bf16[128,1024]{1,0:T(8,128)(2,1)}) custom-call(bf16[256,512]{1,0:T(8,128)(2,1)} %shard_map.291.attended, bf16[512,2048]{1,0:T(8,128)(2,1)} %weight.1, bf16[128,1024]{1,0:T(8,128)(2,1)} %rows.3, f32[1,1024]{1,0:T(1,128)} %bitcast.64), custom_call_target="tpu_custom_call" | custom-call | tf_op jit(solution)/shard_map/pallas_call | solution.py:462
  67.9 25.6 %all-gather.4.cloned.1.call-done.grad_own.all_grad_own.own = bf16[2048,1024]{1,0:T(8,128)(2,1)} async-done(((bf16[128,1024]{1,0:T(8,128)(2,1)}), bf16[2048,1024]{1,0:T(8,128)(2,1)}) %all-gather.4.cloned.1.call-update) | async-done | bytes 4194320 | tf_op jit(solution)/shard_map/all_gather | solution.py:1389
  94.6 48.9 %shard_map.293 = (bf16[16,128,1024]{2,1,0:T(8,128)(2,1)}, bf16[16,128,1024]{2,1,0:T(8,128)(2,1)}) custom-call(bf16[128,1024]{1,0:T(8,128)(2,1)} %get-tuple-element.67.source), custom_call_target="tpu_custom_call" | custom-call | bytes 33554432 | tf_op jit(solution)/shard_map/pallas_call | solution.py:590
  146.0 56.4 %shard_map.294 = (bf16[2,704,2048]{2,1,0:T(8,128)(2,1)}, bf16[2,704,2048]{2,1,0:T(8,128)(2,1)}, bf16[2,704,2048]{2,1,0:T(8,128)(2,1)}, bf16[704,2048]{1,0:T(8,12...) custom-call(bf16[2048,1024]{1,0:T(8,128)(2,1)} %bitcast.76, ...), custom_call_target="tpu_custom_call" | custom-call | flops 35433480192 | bytes 52428800 | tf_op jit(solution)/shard_map/pallas_call | solution.py:1132
  202.5 52.8 %shard_map.296 = f32[128,1024]{1,0:T(8,128)} custom-call(bf16[2,704,2048]{2,1,0:T(8,128)(2,1)} %get-tuple-element.77.refs_0_.left, bf16[2,704,2048]{2,1,0:T(8,128)(2,1)} %get-tuple-element.78.refs_1_.left, bf16[2,704,1024]{2,1,0:T(8,128)(2,1)} %bitcast.59, bf16[2,704,1024]{2,1,0:T(8,128)(2,1)} %bitcast.61, ...), custom_call_target="tpu_custom_call" | custom-call | flops 11811160064 | bytes 74448896 | tf_op jit(solution)/shard_map/pallas_call | solution.py:850
  256.5 2.5 all-reduce.3
  260.9 48.0 %shard_map.297 = (bf16[16,128,1024]{2,1,0:T(8,128)(2,1)}, bf16[16,128,1024]{2,1,0:T(8,128)(2,1)}) custom-call(bf16[128,1024]{1,0:T(8,128)(2,1)} %fusion.33.source), custom_call_target="tpu_custom_call" | custom-call | bytes 33554432 | tf_op jit(solution)/shard_map/pallas_call | solution.py:590
  310.2 3.7 fusion.24
  317.7 11.6 %shard_map.304 = f32[1024,1408]{1,0:T(8,128)} custom-call(bf16[1024,2048]{1,0:T(8,128)(2,1)} %get-tuple-element.98.left, bf16[2048,1408]{1,0:T(8,128)(2,1)} %get-tuple-element.80.refs_5_.right), custom_call_target="tpu_custom_call" | custom-call | flops 5905580032 | bytes 15728640 | tf_op jit(solution)/shard_map/pallas_call | solution.py:1207
  329.3 4.8 fusion.8
  334.1 3.9 add_convert_fusion.rest_2_
  338.1 25.4 %shard_map.298 = (bf16[2048,768]{1,0:T(8,128)(2,1)}, bf16[2048,1024]{1,0:T(8,128)(2,1)}, bf16[2048,64]{1,0:T(8,128)(2,1)}, bf16[1024,2048]{1,0:T(8,128)(2,1)}, bf16[512,2048]{1,0:T(8,128)(2,1)}) custom-call(s32[1]{0:T(128)} %bitcast._, bf16[2048,1024]{1,0:T(8,128)(2,1)} %all-gather.6.cloned.1.call-done.own, bf16[2048,1024]{1,0:T(8,128)(2,1)} %collective-permute-done.8.other, ...), custom_call_target="tpu_custom_call" | custom-call | flops 13421772800 | bytes 31916032 | tf_op jit(solution)/shard_map/pallas_call | solution.py:158
  363.4 29.3 %shard_map.299 = (bf16[512,2048]{1,0:T(8,128)(2,1)}, bf16[2048,768]{1,0:T(8,128)(2,1)}, bf16[2048,1024]{1,0:T(8,128)(2,1)}, f32[2048,64]{1,0:T(8,128)}) custom-call(s32[8,3]{1,0:T(8,128)} %copy-done.19, bf16[2048,768]{1,0:T(8,128)(2,1)} %get-tuple-element.85.query, bf16[2048,1024]{1,0:T(8,128)(2,1)} %get-tuple-element.86.keyvalue, ...), custom_call_target="tpu_custom_call" | custom-call | flops 4697620480 | bytes 28966912 | tf_op jit(solution)/shard_map/pallas_call | solution.py:257
  392.7 2.6 fusion.21
  395.7 11.7 %shard_map.303 = f32[1024,1408]{1,0:T(8,128)} custom-call(bf16[1024,2048]{1,0:T(8,128)(2,1)} %get-tuple-element.98.left, bf16[2048,1408]{1,0:T(8,128)(2,1)} %get-tuple-element.79.refs_4_.right), custom_call_target="tpu_custom_call" | custom-call | flops 5905580032 | bytes 15728640 | tf_op jit(solution)/shard_map/pallas_call | solution.py:1207
  407.4 11.1 %shard_map.307 = f32[2,704,1024]{2,1,0:T(8,128)} custom-call(bf16[2,704,2048]{2,1,0:T(8,128)(2,1)} %get-tuple-element.78.refs_1_.left, bf16[2048,1024]{1,0:T(8,128)(2,1)} %bitcast.78), custom_call_target="tpu_custom_call" | custom-call | flops 5905580032 | bytes 15728640 | tf_op jit(solution)/shard_map/pallas_call | solution.py:1189
  418.5 2.9 fusion.2
  421.5 11.0 %shard_map.306 = f32[2,704,1024]{2,1,0:T(8,128)} custom-call(bf16[2,704,2048]{2,1,0:T(8,128)(2,1)} %get-tuple-element.77.refs_0_.left, bf16[2048,1024]{1,0:T(8,128)(2,1)} %bitcast.79), custom_call_target="tpu_custom_call" | custom-call | flops 5905580032 | bytes 15728640 | tf_op jit(solution)/shard_map/pallas_call | solution.py:1189
  435.4 21.5 %all-reduce.5 = bf16[256,576]{1,0:T(8,128)(2,1)S(1)} all-reduce(f32[256,576]{1,0:T(8,128)S(1)} %pad_maximum_fusion.2), channel_id=1, replica_groups=mesh['exp'=8,'row'=2,'col'=2] {'row','col'}, use_global_device_ids=true, to_apply=%region_13.14 | all-reduce | flops 147456 | bytes 884736 | tf_op jit(solution)/shard_map/psum | solution.py:1473
  457.6 11.9 %shard_map.308 = f32[2,352,2048]{2,1,0:T(8,128)} custom-call(s32[1]{0:T(128)} %bitcast._, bf16[2,704,2048]{2,1,0:T(8,128)(2,1)} %get-tuple-element.74.refs_0_.left, bf16[2048,1024]{1,0:T(8,128)(2,1)} %all-gather.4.cloned.1.call-done.grad_own.all_grad_own.own, bf16[2048,1024]{1,0:T(8,128)(2,1)} %collective-permute-done.grad_other.all_grad_other.other), custom_call_target="tpu_custom_call" | custom-call | flops 5905580032 | bytes 17039360 | tf_op jit(solution)/shard_map/pallas_call | solution.py:1233
  469.6 12.2 %shard_map.305 = f32[1,704,2048]{2,1,0:T(8,128)} custom-call(s32[1]{0:T(128)} %bitcast._, bf16[1,704,2048]{2,1,0:T(8,128)(2,1)} %bitcast.65, bf16[2048,1024]{1,0:T(8,128)(2,1)} %all-gather.4.cloned.1.call-done.grad_own.all_grad_own.own, bf16[2048,1024]{1,0:T(8,128)(2,1)} %collective-permute-done.grad_other.all_grad_other.other), custom_call_target="tpu_custom_call" | custom-call | flops 5905580032 | bytes 17039360 | tf_op jit(solution)/shard_map/pallas_call | solution.py:1233
  481.8 65.2 %shard_map.295 = f32[128,1024]{1,0:T(8,128)} custom-call(bf16[2,704,2048]{2,1,0:T(8,128)(2,1)} %get-tuple-element.74.refs_0_.left, bf16[2,352,2048]{2,1,0:T(8,128)(2,1)} %refs_1_.1, bf16[2,352,2048]{2,1,0:T(8,128)(2,1)} %collective-permute-done.3.down_other.refs_2_, bf16[704,2048]{1,0:T(8,128)(2,1)} %get-tuple-element.75.refs_3_, ...), custom_call_target="tpu_custom_call" | custom-call | flops 5905580032 | bytes 68681728 | tf_op jit(solution)/shard_map/pallas_call | solution.py:850
  548.8 10.1 %shard_map.302 = f32[1,512,2048]{2,1,0:T(8,128)} custom-call(s32[1]{0:T(128)} %bitcast._, bf16[1,512,2048]{2,1,0:T(8,128)(2,1)} %bitcast.92, bf16[2048,1024]{1,0:T(8,128)(2,1)} %bitcast.81, bf16[2048,1024]{1,0:T(8,128)(2,1)} %bitcast.82), custom_call_target="tpu_custom_call" | custom-call | flops 4294967296 | bytes 14680064 | tf_op jit(solution)/shard_map/pallas_call | solution.py:1233
  558.9 6.6 %fusion.36 = f32[512,1024]{1,0:T(8,128)} fusion(bf16[512,2048]{1,0:T(8,128)(2,1)} %get-tuple-element.96, bf16[2048,1024]{1,0:T(8,128)(2,1)} %get-tuple-element.92), kind=kOutput, calls=%fused_computation.81 | convolution fusion | flops 2147483648 | bytes 8388608 | tf_op jit(solution)/shard_map/dot_general | solution.py:23
  568.4 14.3 %shard_map.300 = f32[8,1024]{1,0:T(8,128)} custom-call(f32[8,1024]{1,0:T(8,128)} %select_maximum_fusion.source), custom_call_target="tpu_custom_call" | custom-call | tf_op jit(solution)/shard_map/pallas_call | solution.py:1300
  584.0 2.5 psum.31
  590.1 12.8 %shard_map.301 = f32[1,1024,1536]{2,1,0:T(8,128)} custom-call(s32[1]{0:T(128)} %bitcast._, bf16[1,1024,2048]{2,1,0:T(8,128)(2,1)} %bitcast.90, bf16[2048,768]{1,0:T(8,128)(2,1)} %get-tuple-element.90.own, bf16[2048,768]{1,0:T(8,128)(2,1)} %collective-permute-done.10.other), custom_call_target="tpu_custom_call" | custom-call | flops 6442450944 | bytes 16777216 | tf_op jit(solution)/shard_map/pallas_call | solution.py:1233
  602.9 7.1 %fusion.35 = f32[1024,576]{0,1:T(8,128)} fusion(bf16[1024,2048]{1,0:T(8,128)(2,1)} %get-tuple-element.95, bf16[2048,576]{1,0:T(8,128)(2,1)} %all-gather.8.cloned.1.call-done), kind=kOutput, calls=%fused_computation.80 | convolution fusion | flops 2415919104 | bytes 8912896 | tf_op jit(solution)/shard_map/dot_general | solution.py:23
  (140 shorter events, 31.4 us)
Async XLA Ops:
  7.2 86.3 %all-gather.4.cloned.1.call-start = ((), (), s32[]{:S(2)}) async-start(), calls=%async_computation.1 | async-start | bytes 4456448 | tf_op jit(solution)/shard_map/all_gather | solution.py:1389
  8.0 301.0 %all-gather.6.cloned.1.call-start = ((), (), s32[]{:S(2)}) async-start(), calls=%async_computation.2 | async-start | bytes 4456448 | tf_op jit(solution)/shard_map/all_gather | solution.py:1418
  10.8 83.3 %collective-permute-start.2 = (bf16[704,1024]{1,0:T(8,128)(2,1)}, bf16[704,1024]{1,0:T(8,128)(2,1)}, u32[]{:S(2)}, u32[]{:S(2)}) collective-permute-start(bf16[704,1024]{1,0:T(8,128)(2,1)} %dynamic-slice_bitcast_fusion), channel_id=1, source_target_pairs={{0,1},{1,0},{2,3},{3,2},{4,5},{5,4},{6,7},{7,6},{8,9},{9,8},{10,11... | collective-permute-start | bytes 4325384 | tf_op jit(solution)/shard_map/ppermute | solution.py:74
  11.3 83.2 %collective-permute-start.1 = (bf16[704,1024]{1,0:T(8,128)(2,1)S(1)}, bf16[704,1024]{1,0:T(8,128)(2,1)}, u32[]{:S(2)}, u32[]{:S(2)}) collective-permute-start(bf16[704,1024]{1,0:T(8,128)(2,1)S(1)} %dynamic-slice_bitcast_fusion.1), channel_id=1, source_target_pairs={{0,1},{1,0},{2,3},{3,2},{4,5},{5,4},{6,7},{7,6},{8,9},{9,8},{10,11... | collective-permute-start | bytes 4325384 | tf_op jit(solution)/shard_map/ppermute | solution.py:74
  48.9 95.7 %copy-start.2 = (bf16[128,1024]{1,0:T(8,128)(2,1)S(1)}, bf16[128,1024]{1,0:T(8,128)(2,1)}, u32[]{:S(2)}) copy-start(bf16[128,1024]{1,0:T(8,128)(2,1)} %rows.3) | copy-start | bytes 786436
  48.9 95.8 %copy-start.6 = (f32[8,256,128]{2,1,0:T(8,128)S(1)}, f32[8,256,128]{2,1,0:T(8,128)}, u32[]{:S(2)}) copy-start(f32[8,256,128]{2,1,0:T(8,128)} %get-tuple-element.73) | copy-start | bytes 3145732
  93.5 51.9 %collective-permute-start = (bf16[2048,1024]{1,0:T(8,128)(2,1)}, bf16[2048,1024]{1,0:T(8,128)(2,1)}, u32[]{:S(2)}, u32[]{:S(2)}) collective-permute-start(bf16[2048,1024]{1,0:T(8,128)(2,1)} %all-gather.4.cloned.1.call-done.grad_own.all_grad_own.own), channel_id=1, source_target_pairs={{0,1},{1,0},{2,3},{3,2},{4,5},{5,4},{6,7},{7,6},{8,9},{9,8},{10,11... | collective-permute-start | bytes 12582920 | tf_op jit(solution)/shard_map/ppermute | solution.py:74
  93.5 51.8 %collective-permute-start.4 = (bf16[1024,1408]{1,0:T(8,128)(2,1)}, bf16[1024,1408]{1,0:T(8,128)(2,1)}, u32[]{:S(2)}, u32[]{:S(2)}) collective-permute-start(bf16[1024,1408]{1,0:T(8,128)(2,1)} %refs_6_.1), channel_id=1, source_target_pairs={{0,1},{1,0},{2,3},{3,2},{4,5},{5,4},{6,7},{7,6},{8,9},{9,8},{10,11... | collective-permute-start | bytes 8650760 | tf_op jit(solution)/shard_map/ppermute | solution.py:74
  94.0 51.3 %collective-permute-start.5 = (bf16[1024,1408]{1,0:T(8,128)(2,1)}, bf16[1024,1408]{1,0:T(8,128)(2,1)}, u32[]{:S(2)}, u32[]{:S(2)}) collective-permute-start(bf16[1024,1408]{1,0:T(8,128)(2,1)} %refs_7_.1), channel_id=1, source_target_pairs={{0,1},{1,0},{2,3},{3,2},{4,5},{5,4},{6,7},{7,6},{8,9},{9,8},{10,11... | collective-permute-start | bytes 8650760 | tf_op jit(solution)/shard_map/ppermute | solution.py:74
  94.0 51.3 %collective-permute-start.6 = (bf16[704,2048]{1,0:T(8,128)(2,1)}, bf16[704,2048]{1,0:T(8,128)(2,1)}, u32[]{:S(2)}, u32[]{:S(2)}) collective-permute-start(bf16[704,2048]{1,0:T(8,128)(2,1)} %refs_5_.1), channel_id=1, source_target_pairs={{0,1},{1,0},{2,3},{3,2},{4,5},{5,4},{6,7},{7,6},{8,9},{9,8},{10,11... | collective-permute-start | bytes 8650760 | tf_op jit(solution)/shard_map/ppermute | solution.py:74
  94.6 50.8 %collective-permute-start.3 = (bf16[2,352,2048]{2,1,0:T(8,128)(2,1)}, bf16[2,352,2048]{2,1,0:T(8,128)(2,1)}, u32[]{:S(2)}, u32[]{:S(2)}) collective-permute-start(bf16[2,352,2048]{2,1,0:T(8,128)(2,1)} %refs_1_.1), channel_id=1, source_target_pairs={{0,1},{1,0},{2,3},{3,2},{4,5},{5,4},{6,7},{7,6},{8,9},{9,8},{10,11... | collective-permute-start | bytes 8650760 | tf_op jit(solution)/shard_map/ppermute | solution.py:74
  143.6 421.9 %reduce-scatter.2.cloned.1.call-start = ((), (), s32[]{:S(2)}) async-start(), calls=%async_computation.3 | async-start | bytes 1572864 | tf_op jit(solution)/shard_map/reduce_scatter | solution.py:1482
  202.4 52.8 %copy-start.4 = (f32[128,1024]{1,0:T(8,128)S(1)}, f32[128,1024]{1,0:T(8,128)}, u32[]{:S(2)}) copy-start(f32[128,1024]{1,0:T(8,128)} %get-tuple-element.81) | copy-start | bytes 1572868
  202.4 52.8 %copy-start.17 = (f32[1024]{0:T(1024)S(1)}, f32[1024]{0:T(1024)}, u32[]{:S(2)}) copy-start(f32[1024]{0:T(1024)} %convert_element_type.84) | copy-start | bytes 12292
  202.5 56.6 %copy-start.8 = (bf16[128,1024]{1,0:T(8,128)(2,1)S(1)}, bf16[128,1024]{1,0:T(8,128)(2,1)}, u32[]{:S(2)}) copy-start(bf16[128,1024]{1,0:T(8,128)(2,1)} %param.35) | copy-start | bytes 786436
  255.3 54.9 %copy-start.16 = (f32[256,1]{1,0:T(8,128)S(1)}, f32[256,1]{1,0:T(8,128)}, u32[]{:S(2)}) copy-start(f32[256,1]{1,0:T(8,128)} %get-tuple-element.91) | copy-start | bytes 3076
  309.0 29.0 %collective-permute-start.8 = (bf16[2048,1024]{1,0:T(8,128)(2,1)}, bf16[2048,1024]{1,0:T(8,128)(2,1)}, u32[]{:S(2)}, u32[]{:S(2)}) collective-permute-start(bf16[2048,1024]{1,0:T(8,128)(2,1)} %all-gather.6.cloned.1.call-done.own), channel_id=1, source_target_pairs={{0,1},{1,0},{2,3},{3,2},{4,5},{5,4},{6,7},{7,6},{8,9},{9,8},{10,11... | collective-permute-start | bytes 12582920 | tf_op jit(solution)/shard_map/ppermute | solution.py:74
  317.6 164.1 %collective-permute-start.7 = (bf16[704,256]{1,0:T(8,128)(2,1)}, bf16[704,256]{1,0:T(8,128)(2,1)}, u32[]{:S(2)}, u32[]{:S(2)}) collective-permute-start(bf16[704,256]{1,0:T(8,128)(2,1)} %constant_dynamic-slice_fusion.1), channel_id=1, source_target_pairs={{0,1},{1,0},{2,3},{3,2},{4,5},{5,4},{6,7},{7,6},{8,9},{9,8},{10,11... | collective-permute-start | bytes 1081352 | tf_op jit(solution)/shard_map/ppermute | solution.py:74
  317.7 11.6 %copy-start.10 = (bf16[512,2048]{1,0:T(8,128)(2,1)S(1)}, bf16[512,2048]{1,0:T(8,128)(2,1)}, u32[]{:S(2)}) copy-start(bf16[512,2048]{1,0:T(8,128)(2,1)} %weight.1) | copy-start | bytes 6291460
  363.4 29.3 %copy-start.3 = (bf16[1024,768]{1,0:T(8,128)(2,1)S(1)}, bf16[1024,768]{1,0:T(8,128)(2,1)}, u32[]{:S(2)}) copy-start(bf16[1024,768]{1,0:T(8,128)(2,1)} %get-tuple-element.60.query_other) | copy-start | bytes 4718596
  395.3 23.2 %collective-permute-start.9 = (f32[256,1024]{1,0:T(8,128)}, f32[256,1024]{1,0:T(8,128)}, u32[]{:S(2)}, u32[]{:S(2)}) collective-permute-start(f32[256,1024]{1,0:T(8,128)} %fusion.21), channel_id=1, source_target_pairs={{0,1},{1,0},{2,3},{3,2},{4,5},{5,4},{6,7},{7,6},{8,9},{9,8},{10,11... | collective-permute-start | bytes 3145736 | tf_op jit(solution)/shard_map/ppermute | solution.py:74
  407.4 11.1 %copy-start = (bf16[1024,1536]{1,0:T(8,128)(2,1)S(1)}, bf16[1024,1536]{1,0:T(8,128)(2,1)}, u32[]{:S(2)}) copy-start(bf16[1024,1536]{1,0:T(8,128)(2,1)} %query_own.3) | copy-start | bytes 9437188
  421.4 12.0 %copy-start.7 = (bf16[512,1024]{1,0:T(8,128)(2,1)S(1)}, bf16[512,1024]{1,0:T(8,128)(2,1)}, u32[]{:S(2)}) copy-start(bf16[512,1024]{1,0:T(8,128)(2,1)} %keyvalue_weight.3) | copy-start | bytes 3145732
  421.5 12.0 %copy-start.11 = (f32[256,512]{1,0:T(8,128)S(1)}, f32[256,512]{1,0:T(8,128)}, u32[]{:S(2)}) copy-start(f32[256,512]{1,0:T(8,128)} %get-tuple-element.93) | copy-start | bytes 1572868
  421.5 12.0 %copy-start.18 = (f32[512]{0:T(512)S(1)}, f32[512]{0:T(512)}, u32[]{:S(2)}) copy-start(f32[512]{0:T(512)} %convert_element_type.81) | copy-start | bytes 6148
  421.5 181.4 %all-gather.8.cloned.1.call-start = ((), (), s32[]{:S(2)}) async-start(), calls=%async_computation.4 | async-start | bytes 2785280 | tf_op jit(solution)/shard_map/all_gather | solution.py:1477
  481.8 108.4 %collective-permute-start.10 = (bf16[2048,768]{1,0:T(8,128)(2,1)}, bf16[2048,768]{1,0:T(8,128)(2,1)}, u32[]{:S(2)}, u32[]{:S(2)}) collective-permute-start(bf16[2048,768]{1,0:T(8,128)(2,1)} %get-tuple-element.90.own), channel_id=1, source_target_pairs={{0,1},{1,0},{2,3},{3,2},{4,5},{5,4},{6,7},{7,6},{8,9},{9,8},{10,11... | collective-permute-start | bytes 9437192 | tf_op jit(solution)/shard_map/ppermute | solution.py:74
  481.8 65.2 %copy-start.15 = (f32[128,1024]{1,0:T(8,128)S(1)}, f32[128,1024]{1,0:T(8,128)}, u32[]{:S(2)}) copy-start(f32[128,1024]{1,0:T(8,128)} %get-tuple-element.65) | copy-start | bytes 1572868
  558.9 6.6 %copy-start.13 = (bf16[128,576]{1,0:T(8,128)(2,1)S(1)}, bf16[128,576]{1,0:T(8,128)(2,1)}, u32[]{:S(2)}) copy-start(bf16[128,576]{1,0:T(8,128)(2,1)} %dynamic-slice_convert_fusion) | copy-start | bytes 442372
  558.9 29.0 %copy-start.9 = (bf16[128,1024]{1,0:T(8,128)(2,1)S(1)}, bf16[128,1024]{1,0:T(8,128)(2,1)}, u32[]{:S(2)}) copy-start(bf16[128,1024]{1,0:T(8,128)(2,1)} %param.35) | copy-start | bytes 786436
  565.5 22.4 %copy-start.5 = (f32[128,1024]{1,0:T(8,128)S(1)}, f32[128,1024]{1,0:T(8,128)}, u32[]{:S(2)}) copy-start(f32[128,1024]{1,0:T(8,128)} %shard_map.296) | copy-start | bytes 1572868
  565.5 22.4 %copy-start.12 = (f32[128,1024]{1,0:T(8,128)S(1)}, f32[128,1024]{1,0:T(8,128)}, u32[]{:S(2)}) copy-start(f32[128,1024]{1,0:T(8,128)} %reduce-scatter.2.cloned.1.call-done) | copy-start | bytes 1572868
  (10 other events, 51.7 us)
Sparse Core Ops, SparseCore 0:
  10.8 82.6 all-gather.3
  143.7 80.3 all-gather.5
  421.6 28.8 reduce-scatter.1
  457.8 82.2 all-gather.7

commit v2 on v1

v2 whole, which is shorter than its diff:
```python
import functools

import jax
import jax.numpy as jnp
from jax import lax
from jax.experimental import pallas as pl
from jax.experimental.pallas import tpu as pltpu
from jax.sharding import PartitionSpec as P

DN = 128
DR = 64
DV = 128
R = 512
TOP = 6


EPSILON = 1e-06
ROPE_BASE = 50000.0
NEGATIVE = -1e30


def matmul(former, latter):
    return jnp.dot(former, latter, preferred_element_type=jnp.float32)


def matmul_left(former, latter):
    return lax.dot_general(
        former, latter, (((0,), (0,)), ((), ())), preferred_element_type=jnp.float32
    )


def matmul_right(former, latter):
    return lax.dot_general(
        former, latter, (((1,), (1,)), ((), ())), preferred_element_type=jnp.float32
    )


def sequence_layout(lengths, group_size):
    seq_ends = jnp.cumsum(lengths)
    token_order = jnp.arange(group_size, dtype=jnp.int32)
    segment = jnp.sum((token_order[:, None] >= seq_ends[None, :]).astype(jnp.int32), axis=1)
    seq_starts = seq_ends - lengths
    own_start = jnp.sum(
        jnp.where(
            segment[:, None] == jnp.arange(lengths.shape[0], dtype=jnp.int32)[None, :],
            seq_starts[None, :],
            0,
        ),
        axis=1,
    )
    return (segment, token_order - own_start)


def rope_tables(places):
    inverse_frequency = ROPE_BASE ** (-(jnp.arange(DR // 2, dtype=jnp.float32) * 2.0 / DR))
    angles = places.astype(jnp.float32)[:, None] * inverse_frequency[None, :]
    return (jnp.cos(angles), jnp.sin(angles))


MESH = pl.DeviceIdType.MESH
VMEM_LIMIT = 60 * 1024 * 1024
LOG2_E = 1.4426950408889634


def full_spec(array):
    zeros = (0,) * array.ndim
    return pl.BlockSpec(array.shape, lambda *_: zeros)


ANY_SPEC = pl.BlockSpec(memory_space=pl.ANY)


def swap_core(values):
    return lax.ppermute(values, "col", [(0, 1), (1, 0)])


def half_sums(values):
    return lax.psum(values, "col")


def norm_backward(gradient, normed, inverse_rms, gain_vector):
    full_width = normed.shape[1] * lax.axis_size("col")
    scaled = gradient * gain_vector
    inner_sum = half_sums(jnp.sum(scaled * normed, axis=1)) / full_width
    return (
        inverse_rms * (scaled - normed * inner_sum[:, None]),
        jnp.sum(gradient * normed, axis=0),
    )


TABLE = dict(ids=0, router=8, first=16, cosine=32, sine=64)


def rotary_tables(table):
    cosine = table[:, TABLE["cosine"] : TABLE["cosine"] + DR // 2]
    sine = table[:, TABLE["sine"] : TABLE["sine"] + DR // 2]
    return jnp.concatenate([cosine, cosine], axis=1), jnp.concatenate([-sine, sine], axis=1)


def first_keys(table):
    return table[:, TABLE["first"] : TABLE["first"] + 1].astype(jnp.int32)


def rotary(values, cosine_both, sine_signed):
    half = values.shape[-1] // 2
    swapped = jnp.concatenate([values[:, half:], values[:, :half]], axis=-1)
    return values * cosine_both + swapped * sine_signed


def project_rows(
    rows_own, rows_other, gain_own, gain_other, query_own, query_other, latent_own, latent_other,
    latent_gain, keyvalue_weight, table, query, keyvalue, rope_key
):
    rows_own = rows_own.astype(jnp.float32)
    rows_other = rows_other.astype(jnp.float32)
    total = jnp.sum(rows_own * rows_own, axis=1, keepdims=True)
    total = total + jnp.sum(rows_other * rows_other, axis=1, keepdims=True)
    scale = lax.rsqrt(total / (2 * rows_own.shape[1]) + EPSILON)
    rows_own = (rows_own * scale * gain_own[:1]).astype(jnp.bfloat16)
    rows_other = (rows_other * scale * gain_other[:1]).astype(jnp.bfloat16)
    queries = matmul(rows_own, query_own[...]) + matmul(rows_other, query_other[...])
    cosine, sine = rotary_tables(table)
    for first in range(0, query.shape[1], DN + DR):
        rope = rotary(queries[:, first + DN : first + DN + DR], cosine, sine)
        query[:, first : first + DN + DR] = jnp.concatenate(
            [queries[:, first : first + DN], rope], axis=1
        ).astype(jnp.bfloat16)
    latent = matmul_right(rows_own, latent_own[...]) + matmul_right(rows_other, latent_other[...])
    raw = latent[:, :R]
    latent_scale = lax.rsqrt(jnp.mean(raw * raw, axis=1, keepdims=True) + EPSILON)
    latent_normed = raw * latent_scale
    compressed = (latent_normed * latent_gain[:1]).astype(jnp.bfloat16)
    keyvalue[...] = matmul(compressed, keyvalue_weight[...]).astype(jnp.bfloat16)
    rope_key[...] = rotary(latent[:, R:], cosine, sine).astype(jnp.bfloat16)
    return rows_own, compressed, latent_normed, latent_scale, scale


def softmax_parts(queries, keys, bias):
    scores = matmul_right(queries, keys) * ((DN + DR) ** (-0.5) * LOG2_E) + bias
    exponent = jnp.exp2(scores - jnp.max(scores, axis=1, keepdims=True))
    return exponent * (1.0 / jnp.sum(exponent, axis=1, keepdims=True))


def mask_bias(first_key):
    size = first_key.shape[0]
    row = lax.broadcasted_iota(jnp.int32, (size, size), 0)
    column = lax.broadcasted_iota(jnp.int32, (size, size), 1)
    return jnp.where((column <= row) & (column >= first_key), 0.0, NEGATIVE)


def head_keys(keyvalue, rope_keys, head):
    first = head * (DN + DV)
    keys = jnp.concatenate([keyvalue[:, first : first + DN], rope_keys], axis=1)
    return keys, keyvalue[:, first + DN : first + DN + DV]


def attend_kernel(table, query, keyvalue, rope_key, attended):
    bias = mask_bias(first_keys(table))
    rope_keys = rope_key[...]
    for head in range(query.shape[1] // (DN + DR)):
        first = head * (DN + DR)
        keys, values = head_keys(keyvalue, rope_keys, head)
        weights = softmax_parts(query[:, first : first + DN + DR], keys, bias)
        attended[:, head * DV : (head + 1) * DV] = matmul(
            weights.astype(jnp.bfloat16), values
        ).astype(jnp.bfloat16)


def attention_body(
    table, query, keyvalue, rope_key, stream_own, stream_other,
    output_own, output_other, attended, grad_query, grad_keyvalue, grad_rope
):
    factor = (DN + DR) ** (-0.5)
    bias = mask_bias(first_keys(table))
    cosine, sine = rotary_tables(table)
    rope_keys = rope_key[...]
    size = query.shape[0]
    grad_heads = matmul_right(stream_own[0], output_own[...]) + matmul_right(
        stream_other[0], output_other[...]
    )
    grad_heads = grad_heads.astype(jnp.bfloat16)
    rope_total = jnp.zeros((size, DR), jnp.float32)
    for head in range(query.shape[1] // (DN + DR)):
        first = head * (DN + DR)
        first_kv = head * (DN + DV)
        queries = query[:, first : first + DN + DR]
        keys, values = head_keys(keyvalue, rope_keys, head)
        probabilities = softmax_parts(queries, keys, bias)
        weights = probabilities.astype(jnp.bfloat16)
        result = matmul(weights, values)
        attended[head * DV : (head + 1) * DV, :] = result.astype(jnp.bfloat16).T
        grad_head = grad_heads[:, head * DV : (head + 1) * DV]
        inner = jnp.sum(result * grad_head.astype(jnp.float32), axis=1, keepdims=True)
        grad_scores = (probabilities * (matmul_right(grad_head, values) - inner)).astype(
            jnp.bfloat16
        )
        grad_queries = matmul(grad_scores, keys) * factor
        grad_keys = matmul_left(grad_scores, queries) * factor
        unrotated = rotary(grad_queries[:, DN:], cosine, -sine)
        grad_query[:, first : first + DN + DR] = jnp.concatenate(
            [grad_queries[:, :DN], unrotated], axis=1
        ).astype(jnp.bfloat16)
        grad_keyvalue[:, first_kv : first_kv + DN] = grad_keys[:, :DN].astype(jnp.bfloat16)
        grad_keyvalue[:, first_kv + DN : first_kv + DN + DV] = matmul_left(
            weights, grad_head
        ).astype(jnp.bfloat16)
        rope_total = rope_total + grad_keys[:, DN:]
    grad_rope[...] = rotary(rope_total, cosine, -sine)


def positions():
    exp_count = lax.axis_size("exp")
    slow = min(4, exp_count)
    fast = exp_count // slow
    row_count = lax.axis_size("row")
    exp_index = lax.axis_index("exp")
    place = (exp_index // fast, exp_index % fast, lax.axis_index("row"), lax.axis_index("col"))
    return place, (slow, fast, row_count)


def peers(with_core):
    (slow_at, fast_at, row_at, col_at), (slow, fast, row_count) = positions()
    slow_ids = [
        {"exp": (slow_at + step) % slow * fast + fast_at} for step in range(1, slow)
    ]
    fast_ids = [
        {"exp": slow_at * fast + (fast_at + step) % fast} for step in range(1, fast)
    ]
    row_ids = [{"row": (row_at + step) % row_count} for step in range(1, row_count)]
    core_ids = [{"col": 1 - col_at}] if with_core else []
    return slow_ids, fast_ids, row_ids, core_ids


def enter(groups):
    barrier = pltpu.get_barrier_semaphore()
    count = 0
    for group in groups:
        for device in group:
            pl.semaphore_signal(barrier, inc=1, device_id=device, device_id_type=MESH)
            count += 1
    pl.semaphore_wait(barrier, count)


def remote(src, dst, sems, index, device):
    copy = pltpu.make_async_remote_copy(
        src_ref=src,
        dst_ref=dst,
        send_sem=sems.at[(0, *index)],
        recv_sem=sems.at[(1, *index)],
        device_id=device,
        device_id_type=MESH,
    )
    copy.start()
    return copy


def wait_arrived(dst, sems, index):
    pltpu.make_async_copy(dst, dst, sems.at[(1, *index)]).wait()


def sent(src, sems, index):
    pltpu.make_async_copy(src, src, sems.at[(0, *index)]).wait()


class Gather:
    def __init__(self, source, own, other, sems, by_core):
        self.source, self.own, self.other = source, own, other
        self.far = own if by_core else other
        self.place, self.sizes = positions()
        self.fast_ids, self.row_ids, core_ids = peers(True)[1:]
        self.core = core_ids[0]
        self.half = source.shape[0] // 2
        (
            self.local, self.up, self.down, self.fast, self.row, self.low, self.high,
            self.core_sems, self.core_half,
        ) = sems

    @staticmethod
    def sems():
        exp_count, row_count = lax.axis_size("exp"), lax.axis_size("row")
        slow = min(4, exp_count)
        fast = exp_count // slow
        corner = (fast - 1, row_count - 1, slow)
        return [pltpu.SemaphoreType.DMA] + [
            pltpu.SemaphoreType.DMA((2, *shape))
            for shape in (
                (slow - 1,), (slow - 1,), (fast - 1, slow), (row_count - 1, slow), corner, corner,
                (fast, row_count, slow), (2, *corner),
            )
        ]

    def index(self, line, fast_off, row_off):
        _, fast_at, row_at, _ = self.place
        _, fast, row_count = self.sizes
        fast_index = (fast_at + fast - fast_off) % fast
        return (line * fast + fast_index) * row_count + (row_at + row_count - row_off) % row_count

    def part(self, ref, number):
        return ref.at[pl.ds(number * self.half, self.half)]

    def keep(self):
        mine = self.index(self.place[0], 0, 0)
        return pltpu.make_async_copy(self.source, self.own(mine), self.local)

    def along(self, up, src, index, number):
        slow_at, fast_at = self.place[:2]
        slow, fast, _ = self.sizes

        @pl.when(slow_at < slow - 1 if up else slow_at > 0)
        def _():
            goal = (slow_at + 1 if up else slow_at - 1) * fast + fast_at
            remote(
                src, self.own(index), self.up if up else self.down, (number,), {"exp": goal}
            )

    def spread(self, src, line):
        index = self.index(line, 0, 0)
        for number, device in enumerate(self.fast_ids):
            remote(src, self.own(index), self.fast, (number, line), device)
        for number, device in enumerate(self.row_ids):
            remote(src, self.own(index), self.row, (number, line), device)
        remote(src, self.far(index), self.core_sems, (0, 0, line), self.core)

    def start(self):
        self.keep().start()
        mine = self.index(self.place[0], 0, 0)
        self.along(True, self.source, mine, 0)
        self.along(False, self.source, mine, 0)
        self.spread(self.source, self.place[0])

    def lines(self, number, act):
        slow_at, slow = self.place[0], self.sizes[0]
        if number == 0:
            act(slow_at, None)
            return

        @pl.when(slow_at >= number)
        def _():
            act(slow_at - number, True)

        @pl.when(slow_at + number < slow)
        def _():
            act(slow_at + number, False)

    def hop(self, number):
        def act(line, up):
            block = self.own(self.index(line, 0, 0))
            wait_arrived(block, self.up if up else self.down, (number - 1,))
            if number < self.sizes[0] - 1:
                self.along(up, block, self.index(line, 0, 0), number)
            self.spread(block, line)

        self.lines(number, act)

    def corner(self, number):
        _, fast, row_count = self.sizes

        def act(line, _):
            for fast_off in range(1, fast):
                index = self.index(line, fast_off, 0)
                block = self.own(index)
                wait_arrived(block, self.fast, (fast_off - 1, line))
                for count, device in enumerate(self.row_ids):
                    low = self.part(block, 0)
                    remote(low, low, self.low, (fast_off - 1, count, line), device)
                remote(block, self.far(index), self.core_sems, (fast_off, 0, line), self.core)
            for row_off in range(1, row_count):
                index = self.index(line, 0, row_off)
                block = self.own(index)
                wait_arrived(block, self.row, (row_off - 1, line))
                for count, device in enumerate(self.fast_ids):
                    high = self.part(block, 1)
                    remote(high, high, self.high, (count, row_off - 1, line), device)
                remote(block, self.far(index), self.core_sems, (0, row_off, line), self.core)

        self.lines(number, act)

    def last(self, number):
        _, fast, row_count = self.sizes

        def act(line, _):
            for fast_off in range(1, fast):
                for row_off in range(1, row_count):
                    index = self.index(line, fast_off, row_off)
                    spot = (fast_off - 1, row_off - 1, line)
                    for count, sems in enumerate((self.low, self.high)):
                        half = self.part(self.own(index), count)
                        wait_arrived(half, sems, spot)
                        remote(
                            half, self.part(self.far(index), count), self.core_half,
                            (count, *spot), self.core,
                        )

        self.lines(number, act)

    def ready(self, line, fast_off):
        row_count = self.sizes[2]

        @pl.when(fast_off == 0)
        def _():
            for row_off in range(row_count):
                block = self.other(self.index(line, 0, row_off))
                wait_arrived(block, self.core_sems, (0, row_off, line))

        @pl.when(fast_off > 0)
        def _():
            block = self.other(self.index(line, fast_off, 0))
            wait_arrived(block, self.core_sems, (fast_off, 0, line))
            for row_off in range(1, row_count):
                block = self.other(self.index(line, fast_off, row_off))
                for count in range(2):
                    spot = (count, fast_off - 1, row_off - 1, line)
                    wait_arrived(self.part(block, count), self.core_half, spot)

    def finish(self, all_ready=False):
        slow_at = self.place[0]
        slow, fast, row_count = self.sizes
        whole = self.own(self.index(slow_at, 0, 0))
        half = self.part(whole, 0)

        @pl.loop(0, slow)
        def _(line):
            for fast_off in range(fast):
                for row_off in range(row_count):
                    block = self.other(self.index(line, fast_off, row_off))
                    if fast_off and row_off:
                        spot = (fast_off - 1, row_off - 1, line)
                        for count in range(2):
                            if not all_ready:
                                wait_arrived(
                                    self.part(block, count), self.core_half, (count, *spot)
                                )
                            sent(half, self.core_half, (count, *spot))
                        sent(half, self.low, spot)
                        sent(half, self.high, spot)
                    else:
                        if not all_ready:
                            wait_arrived(block, self.core_sems, (fast_off, row_off, line))
                        sent(whole, self.core_sems, (fast_off, row_off, line))
            for count in range(fast - 1):
                sent(whole, self.fast, (count, line))
            for count in range(row_count - 1):
                sent(whole, self.row, (count, line))

        for number in range(slow - 1):

            @pl.when((slow_at >= number) & (slow_at < slow - 1))
            def _():
                sent(whole, self.up, (number,))

            @pl.when((slow_at + number < slow) & (slow_at > 0))
            def _():
                sent(whole, self.down, (number,))

        if not all_ready:
            self.keep().wait()

    def steps(self):
        slow = self.sizes[0]
        return (
            [functools.partial(self.hop, number) for number in range(1, slow)]
            + [functools.partial(self.corner, number) for number in range(slow)]
            + [functools.partial(self.last, number) for number in range(slow)]
        )


def prologue_kernel(
    rows, gain, latent_gain, keyvalue_weight, output_weight, table,
    gain_two, tables, query_weight, latent_weight, upstream, rows_source,
    gate, up, down, shared_gate, shared_up, shared_down,
    latent_normed, latent_scale, inverse_one, hidden, normed, inverse, mixer,
    tables_all, grad_all, rows_all, query_far, latent_far, gain_far,
    gate_far, up_far, down_far, shared_gate_far, shared_up_far, shared_down_far,
    rows_own, rows_other, query_own, query_other, latent_own, latent_other, gain_other,
    query, keyvalue, rope_key, attended, scales, given, from_core, rows_out, from_rows,
    squares, squares_in,
    local_sems, row_sems, core_rows, slow_sems, fast_sems, core_sems, mix_core, mix_rows,
    weight_sems, *gather_sems
):
    (slow_at, fast_at, row_at, col_at), (slow, fast, row_count) = positions()
    slow_ids, fast_ids, row_ids, core_ids = peers(True)
    core = core_ids[0]
    count, width = rows.shape
    mine = slow_at * fast + fast_at
    query_width = query_own.shape[1]
    own_heads = pl.ds(pl.multiple_of(col_at * query_width, query_width), query_width)
    given_heads = pl.ds(pl.multiple_of((1 - col_at) * query_width, query_width), query_width)
    gather = Gather(
        upstream, lambda index: grad_all.at[index, col_at],
        lambda index: grad_all.at[index, 1 - col_at], gather_sems[: len(gather_sems) // 2], True,
    )
    loads = [
        pltpu.make_async_copy(query_weight.at[:, own_heads], query_own, local_sems.at[0]),
        pltpu.make_async_copy(latent_weight, latent_own, local_sems.at[1]),
        pltpu.make_async_copy(tables, tables_all.at[mine], local_sems.at[2]),
    ]
    for copy in loads:
        copy.start()
    rows_own[row_at] = rows[...]
    enter((slow_ids, fast_ids, row_ids, core_ids))
    started = [
        remote(rows, rows_own.at[row_at], row_sems, (number,), device)
        for number, device in enumerate(row_ids)
    ]
    started.append(remote(rows, rows_other.at[row_at], core_rows, (0,), core))
    started.append(remote(gain, gain_other, core_sems, (0,), core))
    started.append(remote(query_weight.at[:, given_heads], query_other, core_sems, (1,), core))
    started.append(remote(latent_weight, latent_other, core_sems, (2,), core))
    for number, device in enumerate(slow_ids):
        started.append(remote(tables, tables_all.at[mine], slow_sems, (number,), device))
    for number, device in enumerate(fast_ids):
        started.append(remote(tables, tables_all.at[mine], fast_sems, (number, 0), device))
    gather.start()
    late = Gather(
        rows_source, lambda index: rows_all.at[index, col_at],
        lambda index: rows_all.at[index, 1 - col_at], gather_sems[len(gather_sems) // 2 :], True,
    )
    steps = gather.steps()
    late_steps = [late.start] + late.steps()
    for offset in range(1, row_count):
        index = (row_at + row_count - offset) % row_count
        wait_arrived(rows_own.at[index], row_sems, (offset - 1,))
        started.append(
            remote(rows_own.at[index], rows_other.at[index], core_rows, (offset,), core)
        )
    for offset in range(row_count):
        index = (row_at + row_count - offset) % row_count
        wait_arrived(rows_other.at[index], core_rows, (offset,))
    steps.pop(0)()
    for number, target in enumerate((gain_other, query_other, latent_other)):
        wait_arrived(target, core_sems, (number,))
    exchanged = [
        (gate.at[1 - col_at], gate_far), (up.at[1 - col_at], up_far), (down, down_far),
        (shared_gate, shared_gate_far), (shared_up, shared_up_far), (shared_down, shared_down_far),
    ]
    for number, (source, target) in enumerate(exchanged):
        started.append(remote(source, target, weight_sems, (number,), core))
    for copy in loads:
        copy.wait()
    steps.pop(0)()
    keeps = [
        pltpu.make_async_copy(source, target, local_sems.at[number])
        for number, (source, target) in enumerate(
            ((query_other, query_far), (latent_other, latent_far), (gain_other, gain_far))
        )
    ]
    for copy in keeps:
        copy.start()
    _, _, latent_unit, latent_rms, scale = project_rows(
        rows_own[...].reshape(row_count * count, width),
        rows_other[...].reshape(row_count * count, width),
        gain, gain_other, query_own, query_other, latent_own, latent_other, latent_gain,
        keyvalue_weight, table, query, keyvalue, rope_key,
    )
    latent_normed[...] = latent_unit
    latent_scale[...] = latent_rms
    scales[...] = jnp.broadcast_to(scale, scales.shape)
    inverse_one[...] = scales[pl.ds(pl.multiple_of(row_at * count, count), count), :]
    steps.pop(0)()
    attend_kernel(table, query, keyvalue, rope_key, attended)
    steps.pop(0)()
    for offset in range(1, slow):
        index = (slow_at + slow - offset) % slow * fast + fast_at
        wait_arrived(tables_all.at[index], slow_sems, (offset - 1,))
        for number, device in enumerate(fast_ids):
            started.append(
                remote(
                    tables_all.at[index], tables_all.at[index], fast_sems, (number, offset), device
                )
            )

    own_half = pl.ds(pl.multiple_of(col_at * width, width), width)
    other_half = pl.ds(pl.multiple_of((1 - col_at) * width, width), width)
    given[...] = matmul(attended[...], output_weight[:, other_half]).astype(jnp.bfloat16)
    started.append(remote(given, from_core, mix_core, (0,), core))
    total = matmul(attended[...], output_weight[:, own_half])
    wait_arrived(from_core, mix_core, (0,))
    total = total + from_core[...].astype(jnp.float32)
    rows_out[...] = total.astype(jnp.bfloat16).reshape(rows_out.shape)
    for number, device in enumerate(row_ids):
        goal = (row_at + number + 1) % row_count
        started.append(remote(rows_out.at[goal], from_rows.at[number], mix_rows, (number,), device))
    steps.pop(0)()
    state = rows[...].astype(jnp.float32) + rows_out[row_at].astype(jnp.float32)
    for number in range(row_count - 1):
        wait_arrived(from_rows.at[number], mix_rows, (number,))
        state = state + from_rows[number].astype(jnp.float32)
    hidden[...] = state
    own_squares = jnp.sum(state * state, axis=1, keepdims=True)
    squares[...] = jnp.broadcast_to(own_squares, squares.shape)
    started.append(remote(squares, squares_in, mix_core, (1,), core))
    steps.pop(0)()
    late_steps.pop(0)()
    wait_arrived(squares_in, mix_core, (1,))
    rms = lax.rsqrt((squares[...] + squares_in[...]) / (2 * width) + EPSILON)
    inverse[...] = rms
    unit = state * rms[:, :1]
    normed[...] = unit
    mixer[...] = (unit * gain_two[...]).astype(jnp.bfloat16)
    while steps or late_steps:
        for queue in (steps, late_steps):
            if queue:
                queue.pop(0)()
    for offset in range(slow):
        for number in range(1, fast):
            index = (slow_at + slow - offset) % slow * fast + (fast_at + fast - number) % fast
            wait_arrived(tables_all.at[index], fast_sems, (number - 1, offset))
    gather.finish()
    late.finish()
    for number, (_, target) in enumerate(exchanged):
        wait_arrived(target, weight_sems, (number,))
    for copy in started:
        copy.wait_send()
    for copy in keeps:
        copy.wait()


def prologue(
    rows, gain, latent_gain, keyvalue_weight, output_weight, gain_two, tables,
    query_weight, latent_weight, upstream, others, collective_id
):
    exp_count, row_count = lax.axis_size("exp"), lax.axis_size("row")
    slow = min(4, exp_count)
    fast = exp_count // slow
    count, width = rows.shape
    group = row_count * count
    query_width = query_weight.shape[1] // 2
    keyvalue_width = keyvalue_weight.shape[1]
    latent_width = latent_weight.shape[0]
    low = jnp.bfloat16
    high = jnp.float32
    vmem = pl.BlockSpec(memory_space=pltpu.VMEM)
    wide = jax.ShapeDtypeStruct((count, width), high)
    narrow = jax.ShapeDtypeStruct((count, 128), high)
    dma = pltpu.SemaphoreType.DMA
    return pl.pallas_call(
        prologue_kernel,
        out_shape=[
            jax.ShapeDtypeStruct((group, R), high),
            jax.ShapeDtypeStruct((group, 1), high),
            narrow, wide, wide, narrow,
            jax.ShapeDtypeStruct((count, width), low),
            jax.ShapeDtypeStruct((exp_count, *tables.shape), high),
            jax.ShapeDtypeStruct((exp_count * row_count, 2, count, width), low),
            jax.ShapeDtypeStruct((exp_count * row_count, 2, count, width), low),
            jax.ShapeDtypeStruct((width, query_width), low),
            jax.ShapeDtypeStruct(latent_weight.shape, low),
            jax.ShapeDtypeStruct(gain.shape, high),
            *[
                jax.ShapeDtypeStruct(array.shape[number < 2 :], low)
                for number, array in enumerate(others)
            ],
        ],
        in_specs=[vmem] * 7 + [ANY_SPEC] * 11,
        out_specs=[vmem] * 7 + [ANY_SPEC] * 12,
        scratch_shapes=[
            pltpu.VMEM((row_count, count, width), low),
            pltpu.VMEM((row_count, count, width), low),
            pltpu.VMEM((width, query_width), low),
            pltpu.VMEM((width, query_width), low),
            pltpu.VMEM((latent_width, width), low),
            pltpu.VMEM((latent_width, width), low),
            pltpu.VMEM(gain.shape, high),
            pltpu.VMEM((group, query_width), low),
            pltpu.VMEM((group, keyvalue_width), low),
            pltpu.VMEM((group, DR), low),
            pltpu.VMEM((group, keyvalue_width // 2), low),
            pltpu.VMEM((group, 128), high),
            pltpu.VMEM((group, width), low),
            pltpu.VMEM((group, width), low),
            pltpu.VMEM((row_count, count, width), low),
            pltpu.VMEM((row_count - 1, count, width), low),
            pltpu.VMEM((count, 128), high),
            pltpu.VMEM((count, 128), high),
            dma((3,)),
            dma((2, row_count - 1)),
            dma((2, row_count)),
            dma((2, slow - 1)),
            dma((2, fast - 1, slow)),
            dma((2, 3)),
            dma((2, 2)),
            dma((2, row_count - 1)),
            dma((2, 6)),
            *Gather.sems(),
            *Gather.sems(),
        ],
        compiler_params=pltpu.CompilerParams(
            collective_id=collective_id, has_side_effects=True, vmem_limit_bytes=VMEM_LIMIT
        ),
    )(
        rows, gain, latent_gain, keyvalue_weight, output_weight, tables, gain_two, tables,
        query_weight, latent_weight, upstream, rows, *others,
    )


def pipeline(body, grid, inputs, outputs):
    pltpu.emit_pipeline(
        body,
        grid=grid,
        in_specs=[pl.BlockSpec(block, place) for _, block, place in inputs],
        out_specs=[pl.BlockSpec(block, place) for _, block, place in outputs],
    )(*[ref for ref, _, _ in inputs], *[ref for ref, _, _ in outputs])


def product_body(total, axis, steps):
    def body(left, right, result):
        step = pl.program_id(axis)
        product = matmul(
            left[...].reshape(-1, left.shape[-1]), right[...].reshape(-1, right.shape[-1])
        )
        spot = total.at[pl.ds(0, product.shape[0]), pl.ds(0, product.shape[1])]

        @pl.when(step == 0)
        def _():
            spot[...] = product

        @pl.when((step > 0) & (step < steps - 1))
        def _():
            spot[...] += product

        @pl.when(step == steps - 1)
        def _():
            result[...] = (spot[...] + product).reshape(result.shape).astype(result.dtype)

    return body


DEPTH = 1024


def stacked_job(left, right, result, total):
    parts, units, tokens = left.shape
    width = right.shape[2]
    steps = tokens // DEPTH

    def run():
        pipeline(
            product_body(total, 1, steps),
            (parts, steps),
            [
                (left, (1, units, DEPTH), lambda part, step: (part, 0, step)),
                (right, (1, DEPTH, width), lambda part, step: (0, step, 0)),
            ],
            [(result, (1, units, width), lambda part, step: (part, 0, 0))],
        )

    return run


def row_job(left, right, result, total):
    features, tokens = left.shape
    units = right.shape[1]
    steps = tokens // DEPTH

    def run():
        pipeline(
            product_body(total, 0, steps),
            (steps,),
            [
                (left, (features, DEPTH), lambda step: (0, step)),
                (right, (DEPTH, units), lambda step: (step, 0)),
            ],
            [(result, (features, units), lambda step: (0, 0))],
        )

    return run


def expert_down_job(left, right, result, total):
    parts, units, tokens = left.shape
    _, _, rows, width = right.shape
    steps = tokens // DEPTH
    col = lax.axis_index("col")

    def run():
        pipeline(
            product_body(total, 1, steps),
            (2, steps),
            [
                (left, (parts, units // 2, DEPTH), lambda side, step: (0, col, step)),
                (right, (DEPTH // rows, 1, rows, width), lambda side, step: (step, side, 0, 0)),
            ],
            [(result, (parts, units // 2, width), lambda side, step: (0, 0, side))],
        )

    return run


def shared_down_job(left, right, result, total):
    units, tokens = left.shape
    _, _, rows, width = right.shape
    steps = tokens // DEPTH

    def run():
        pipeline(
            product_body(total, 1, steps),
            (2, steps),
            [
                (left, (units, DEPTH), lambda side, step: (0, step)),
                (right, (DEPTH // rows, 1, rows, width), lambda side, step: (step, side, 0, 0)),
            ],
            [(result, (units, width), lambda side, step: (0, side))],
        )

    return run


def sided_job(left, right, result, total):
    units, tokens = left.shape
    width = right.shape[2]
    steps = tokens // DEPTH
    col = lax.axis_index("col")

    def run():
        pipeline(
            product_body(total, 1, steps),
            (2, steps),
            [
                (left, (units, DEPTH), lambda side, step: (0, step)),
                (right, (1, DEPTH, width), lambda side, step: (side, step, 0)),
            ],
            [(result, (units, width), lambda side, step: (0, (col + side) % 2))],
        )

    return run


def project_body(own, other, *rest):
    rows, width = own.shape[0] * own.shape[2], own.shape[3]
    normed, compressed, _, _, _ = project_rows(
        own[...].reshape(rows, width), other[...].reshape(rows, width), *rest[:-2]
    )
    rest[-2][...] = normed.T
    rest[-1][...] = compressed.T


def project_jobs(values, weights, tables, results, parts):
    blocks, _, rows, width = values.shape
    tile_blocks = 256 // rows
    steps = blocks // tile_blocks // parts
    col = lax.axis_index("col")
    query_width = weights[3].shape[1]

    def job(part):
        def at(step):
            return part * steps + step

        def table(array):
            return (array, (256, array.shape[1]), lambda step: (at(step), 0))

        def whole(array):
            return (array, array.shape, lambda step: (0, 0))

        def run():
            inputs = [
                (values, (tile_blocks, 1, rows, width), lambda step: (at(step), col, 0, 0)),
                (values, (tile_blocks, 1, rows, width), lambda step: (at(step), 1 - col, 0, 0)),
            ]
            weight_inputs = [whole(array) for array in weights]
            weight_inputs[2] = (weights[2], (width, query_width), lambda step: (0, col))
            inputs += weight_inputs + [table(tables)]
            outputs = [table(array) for array in results[:3]]
            outputs += [
                (array, (array.shape[0], 256), lambda step: (0, at(step))) for array in results[3:]
            ]
            pipeline(project_body, (steps,), inputs, outputs)

        return run

    return [job(part) for part in range(parts)]


def attention_jobs(arrays, stream, output_weight, results, groups, parts):
    size = arrays[0].shape[0] // groups
    width = stream.shape[2]
    col = lax.axis_index("col")
    steps = groups // parts

    def job(part):
        def at(step):
            return part * steps + step

        def table(array):
            return (array, (size, array.shape[1]), lambda step: (at(step), 0))

        def run():
            inputs = [table(array) for array in arrays]
            inputs += [
                (stream, (1, size, width), lambda step: (0, at(step), 0)),
                (stream, (1, size, width), lambda step: (1, at(step), 0)),
                (output_weight, (output_weight.shape[0], width), lambda step: (0, col)),
                (output_weight, (output_weight.shape[0], width), lambda step: (0, 1 - col)),
            ]
            outputs = [
                (results[0], (results[0].shape[0], size), lambda step: (0, at(step)))
            ] + [table(array) for array in results[1:]]
            pipeline(attention_body, (steps,), inputs, outputs)

        return run

    return [job(part) for part in range(parts)]


TOTAL = (1024, 1408)


def jobs_kernel(*refs, make_jobs, inputs):
    for job in make_jobs(refs[:inputs], refs[inputs:-1], refs[-1]):
        job()


def run_jobs(make_jobs, operands, shapes):
    return pl.pallas_call(
        functools.partial(jobs_kernel, make_jobs=make_jobs, inputs=len(operands)),
        out_shape=shapes,
        in_specs=[ANY_SPEC] * len(operands),
        out_specs=[ANY_SPEC] * len(shapes),
        scratch_shapes=[pltpu.VMEM(TOTAL, jnp.float32)],
        compiler_params=pltpu.CompilerParams(vmem_limit_bytes=VMEM_LIMIT),
    )(*operands)


def no_jobs(inputs, outputs, total):
    return []


def gather_kernel(*refs, make_jobs, inputs, sems):
    source, job_inputs, target = refs[0], refs[1 : 1 + inputs], refs[1 + inputs]
    total, gather_sems = refs[-sems - 1], refs[-sems:]
    jobs = make_jobs(job_inputs, refs[2 + inputs : -sems - 1], total)
    gather = Gather(
        source, lambda index: target.at[0, index], lambda index: target.at[1, index], gather_sems,
        False,
    )

    def work():
        if jobs:
            jobs.pop(0)()

    enter(peers(True))
    gather.start()
    steps = gather.steps()
    slow = gather.sizes[0]
    for number, step in enumerate(steps):
        if number in (slow - 1, 2 * slow - 1):
            work()
        step()
    while jobs:
        work()
    gather.finish()


def gather_everywhere(values, collective_id, make_jobs=no_jobs, operands=(), shapes=()):
    exp_count, row_count = lax.axis_size("exp"), lax.axis_size("row")
    slow = min(4, exp_count)
    fast = exp_count // slow
    rows, width = values.shape
    blocks = exp_count * row_count
    result = jax.ShapeDtypeStruct((2, blocks, rows, width), values.dtype)
    sems = Gather.sems()
    gathered, *others = pl.pallas_call(
        functools.partial(
            gather_kernel, make_jobs=make_jobs, inputs=len(operands), sems=len(sems)
        ),
        out_shape=[result, *shapes],
        in_specs=[ANY_SPEC] * (1 + len(operands)),
        out_specs=[ANY_SPEC] * (1 + len(shapes)),
        scratch_shapes=[pltpu.VMEM(TOTAL, jnp.float32), *sems],
        compiler_params=pltpu.CompilerParams(
            collective_id=collective_id, has_side_effects=True, vmem_limit_bytes=VMEM_LIMIT
        ),
        cost_estimate=pl.CostEstimate(
            flops=0, bytes_accessed=4 * blocks * rows * width * 4, transcendentals=0
        ),
    )(values, *operands)
    return gathered.reshape(2, blocks * rows, width), others


def scatter_kernel(*refs, backward, make_jobs, inputs, outputs):
    if backward:
        gating, upward, gate, up, own_gating, own_upward, shared_gate, shared_up = refs[:8]
        lefts = [gating.at[0], gating.at[1], upward.at[0], upward.at[1]]
        refs = refs[8:]
    else:
        hidden, down, down_other, own_hidden, other_hidden, shared, shared_other = refs[:7]
        lefts = [hidden.at[0], hidden.at[1]]
        refs = refs[7:]
    count = len(lefts)
    job_inputs, result, job_outputs = (
        refs[:inputs], refs[inputs], refs[inputs + 1 : inputs + 1 + outputs]
    )
    refs = refs[inputs + 1 + outputs :]
    (
        left_tiles, rights, extra_left, extra_right, part, from_row, from_fast,
        from_fast_late, from_row_late, from_slow,
        left_sems, right_sems, extra_sems, row_sems, fast_sems, fast_late_sems, row_late_sems,
        slow_sems, job_sems, job_total,
    ) = refs
    (slow_at, fast_at, row_at, col_at), (slow, fast, row_count) = positions()
    slow_ids, fast_ids, row_ids, core_ids = peers(True)
    jobs = make_jobs(job_inputs, job_outputs, job_total, core_ids[0], job_sems)
    exp_count = slow * fast
    exp_index = lax.axis_index("exp")
    rows, width = result.shape
    half = rows // 2
    low, high = pl.ds(0, half), pl.ds(half, half)
    group = rows * row_count
    group_rows = pl.ds(pl.multiple_of(exp_index * group, group), group)
    own_half = pl.ds(pl.multiple_of(col_at * width, width), width)

    def slow_of(turn):
        return (slow_at + 1 + turn) % slow

    def order(step):
        return slow_of(step // fast) * fast + (fast_at + 1 + step % fast) % fast

    def loads(step, slot):
        first = pl.multiple_of(order(step) * group, group)
        return [
            pltpu.make_async_copy(
                left.at[:, pl.ds(first, group)], left_tiles.at[slot, number],
                left_sems.at[slot, number],
            )
            for number, left in enumerate(lefts)
        ]

    if backward:
        right_pairs = [(array.at[side], rights.at[2 * number + side])
                       for number, array in enumerate((gate, up)) for side in range(2)]
        extra_pairs = [
            (own_gating.at[group_rows], extra_left.at[0]),
            (own_upward.at[group_rows], extra_left.at[1]),
            (shared_gate, extra_right.at[0]),
            (shared_up, extra_right.at[1]),
        ]
        extra_product = matmul_right
    else:
        split = down.shape[1]
        right_pairs = []
        for side in range(2):
            for source, place in ((down, col_at), (down_other, 1 - col_at)):
                spot = pl.ds(pl.multiple_of(place * split, 16), split)
                right_pairs.append((source.at[side, :, own_half], rights.at[side, spot]))
        extra_pairs = [
            (own_hidden.at[:, group_rows], extra_left.at[0]),
            (other_hidden, extra_left.at[1]),
            (shared.at[:, own_half], extra_right.at[0]),
            (shared_other.at[:, own_half], extra_right.at[1]),
        ]
        extra_product = matmul_left
    prepared = [
        pltpu.make_async_copy(source, target, right_sems.at[number])
        for number, (source, target) in enumerate(right_pairs)
    ]
    extras = [
        pltpu.make_async_copy(source, target, extra_sems.at[number])
        for number, (source, target) in enumerate(extra_pairs)
    ]
    for copy in prepared + loads(0, 0) + extras:
        copy.start()
    enter((slow_ids, fast_ids, row_ids, core_ids))
    for copy in prepared:
        copy.wait()

    def make(step):
        slot = step % 2

        @pl.when(step + 1 < exp_count)
        def _():
            for copy in loads(step + 1, 1 - slot):
                copy.start()

        for copy in loads(step, slot):
            copy.wait()
        index = order(step)
        total = matmul_left(left_tiles[slot, 0], rights[0])
        for number in range(1, count):
            total = total + matmul_left(left_tiles[slot, number], rights[number])
        part[index] = total.astype(jnp.bfloat16).reshape(row_count, rows, width)

        @pl.when(step == exp_count - 1)
        def _():
            for copy in extras:
                copy.wait()
            extra = extra_product(extra_left[0], extra_right[0])
            extra = extra + extra_product(extra_left[1], extra_right[1])
            before = part[index].astype(jnp.float32)
            part[index] = (before + extra.reshape(before.shape)).astype(jnp.bfloat16)

        for number, device in enumerate(row_ids):
            goal = (row_at + number + 1) % row_count
            remote(
                part.at[index, goal, low], from_row.at[number, index], row_sems,
                (number, index), device,
            )
        slow_index = index // fast
        for number, device in enumerate(fast_ids):

            @pl.when(index % fast == (fast_at + number + 1) % fast)
            def _():
                for goal in range(row_count):
                    remote(
                        part.at[index, goal, high], from_fast.at[number, slow_index, goal],
                        fast_sems, (number, slow_index, goal), device,
                    )

    def add_up(index, goal, span, arrivals):
        total = part[index, goal, span].astype(jnp.float32)
        for buffer, sems, spot in arrivals:
            wait_arrived(buffer.at[spot], sems, spot)
            total = total + buffer[spot].astype(jnp.float32)
        return total

    def of_rows(index):
        return [(from_row, row_sems, (number, index)) for number in range(row_count - 1)]

    def of_fasts(slow_index, goal):
        return [
            (from_fast, fast_sems, (number, slow_index, goal)) for number in range(fast - 1)
        ]

    def second(slow_index):
        for number, device in enumerate(fast_ids):
            index = slow_index * fast + (fast_at + number + 1) % fast
            part[index, row_at, low] = add_up(index, row_at, low, of_rows(index)).astype(
                jnp.bfloat16
            )
            remote(
                part.at[index, row_at, low], from_fast_late.at[number, slow_index],
                fast_late_sems, (number, slow_index), device,
            )
        mine = slow_index * fast + fast_at
        for number, device in enumerate(row_ids):
            goal = (row_at + number + 1) % row_count
            part[mine, goal, high] = add_up(
                mine, goal, high, of_fasts(slow_index, goal)
            ).astype(jnp.bfloat16)
            remote(
                part.at[mine, goal, high], from_row_late.at[number, slow_index],
                row_late_sems, (number, slow_index), device,
            )

    def finish(slow_index, span, late):
        mine = slow_index * fast + fast_at
        if late == 0:
            arrivals = of_rows(mine) + [
                (from_fast_late, fast_late_sems, (number, slow_index))
                for number in range(fast - 1)
            ]
        else:
            arrivals = of_fasts(slow_index, row_at) + [
                (from_row_late, row_late_sems, (number, slow_index))
                for number in range(row_count - 1)
            ]
        return add_up(mine, row_at, span, arrivals)

    def third(number):
        slow_index = slow_of(number)
        mine = slow_index * fast + fast_at
        for late, span in enumerate((low, high)):
            part[mine, row_at, span] = finish(slow_index, span, late).astype(jnp.bfloat16)
            remote(
                part.at[mine, row_at, span], from_slow.at[late, number], slow_sems,
                (late, number), slow_ids[number],
            )

    for turn in range(slow + 1):
        if turn < slow:
            pl.loop(turn * fast, turn * fast + fast)(make)
        if turn >= 1:
            second(slow_of(turn - 1))
        if turn >= 2:
            third(turn - 2)
        if jobs:
            jobs.pop(0)()
    for job in jobs:
        job()
    for late, span in enumerate((low, high)):
        total = finish(slow_at, span, late)
        for number in range(slow - 1):
            wait_arrived(from_slow.at[late, number], slow_sems, (late, number))
            total = total + from_slow[late, number].astype(jnp.float32)
        result[span, :] = total

    @pl.loop(0, exp_count)
    def _(index):
        for number in range(row_count - 1):
            sent(from_row.at[number, index], row_sems, (number, index))

    @pl.loop(0, slow)
    def _(slow_index):
        for number in range(fast - 1):
            for goal in range(row_count):
                spot = (number, slow_index, goal)
                sent(from_fast.at[spot], fast_sems, spot)
            sent(from_fast_late.at[number, slow_index], fast_late_sems, (number, slow_index))
        for number in range(row_count - 1):
            sent(from_row_late.at[number, slow_index], row_late_sems, (number, slow_index))

    for number in range(slow - 1):
        for late in range(2):
            sent(from_slow.at[late, number], slow_sems, (late, number))


def no_scatter_jobs(inputs, outputs, total, core, sems):
    return []


def scatter_products(
    operands, backward, collective_id, make_jobs=no_scatter_jobs, job_operands=(), shapes=()
):
    exp_count, row_count = lax.axis_size("exp"), lax.axis_size("row")
    slow = min(4, exp_count)
    fast = exp_count // slow
    _, units, tokens = operands[0].shape
    rows = tokens // exp_count // row_count
    group = rows * row_count
    half = rows // 2
    kind = jnp.bfloat16
    if backward:
        count, (width, shared_units) = 4, operands[6].shape
        extra_shapes = [(2, group, shared_units), (2, width, shared_units)]
    else:
        count, shared_units, width = 2, operands[5].shape[0], operands[1].shape[2] // 2
        extra_shapes = [(2, shared_units, group), (2, shared_units, width)]
    return pl.pallas_call(
        functools.partial(
            scatter_kernel, backward=backward, make_jobs=make_jobs, inputs=len(job_operands),
            outputs=len(shapes),
        ),
        out_shape=[jax.ShapeDtypeStruct((rows, width), jnp.float32), *shapes],
        in_specs=[ANY_SPEC] * (len(operands) + len(job_operands)),
        out_specs=[pl.BlockSpec(memory_space=pltpu.VMEM)] + [ANY_SPEC] * len(shapes),
        scratch_shapes=[
            pltpu.VMEM((2, count, units, group), kind),
            pltpu.VMEM((count, units, width), kind),
            pltpu.VMEM(extra_shapes[0], kind),
            pltpu.VMEM(extra_shapes[1], kind),
            pltpu.VMEM((exp_count, row_count, rows, width), kind),
            pltpu.VMEM((row_count - 1, exp_count, half, width), kind),
            pltpu.VMEM((fast - 1, slow, row_count, half, width), kind),
            pltpu.VMEM((fast - 1, slow, half, width), kind),
            pltpu.VMEM((row_count - 1, slow, half, width), kind),
            pltpu.VMEM((2, slow - 1, half, width), kind),
            pltpu.SemaphoreType.DMA((2, count)),
            pltpu.SemaphoreType.DMA((4,)),
            pltpu.SemaphoreType.DMA((4,)),
            pltpu.SemaphoreType.DMA((2, row_count - 1, exp_count)),
            pltpu.SemaphoreType.DMA((2, fast - 1, slow, row_count)),
            pltpu.SemaphoreType.DMA((2, fast - 1, slow)),
            pltpu.SemaphoreType.DMA((2, row_count - 1, slow)),
            pltpu.SemaphoreType.DMA((2, 2, slow - 1)),
            pltpu.SemaphoreType.DMA((2, 1)),
            pltpu.VMEM(TOTAL if make_jobs is not no_scatter_jobs else (8, 128), jnp.float32),
        ],
        compiler_params=pltpu.CompilerParams(
            collective_id=collective_id, has_side_effects=True, vmem_limit_bytes=VMEM_LIMIT
        ),
        cost_estimate=pl.CostEstimate(
            flops=2 * tokens * units * width * count,
            bytes_accessed=tokens * units * count * 2 + 60 * 1024 * 1024,
            transcendentals=0,
        ),
    )(*operands, *job_operands)


def unit_grads(gating, upward, grad_hidden):
    bend = 0.5 * jnp.tanh(0.5 * gating)
    sigmoid = 0.5 + bend
    silu = gating * sigmoid
    grad_upward = (grad_hidden * silu).astype(jnp.bfloat16)
    grad_gating = (grad_hidden * upward * (sigmoid + silu * (0.5 - bend))).astype(jnp.bfloat16)
    return silu * upward, grad_gating, grad_upward


def units_kernel(
    mixer_rows, tables, all_grad,
    expert_gate, gate_other, expert_up, up_other, expert_down, down_other,
    shared_gate, shared_gate_other, shared_up, shared_up_other, shared_down, shared_down_other,
    all_mixer,
    expert_hidden, expert_gating, expert_upward, shared_hidden, shared_gating, shared_upward,
    mixer_turned,
    gates, ups, downs, shared_gates, shared_ups, shared_downs, inputs, table, tiles, turned_tiles,
    shared_tiles, shared_turned,
    weight_sems, input_sems, local_sems, send_sems, recv_sems, shared_local, shared_send,
    shared_recv, *gather_sems
):
    step = pl.program_id(0)
    steps = pl.num_programs(0)
    (slow_at, fast_at, _, col), (slow, fast, row_count) = positions()
    core = {"col": 1 - col}
    rows, width = mixer_rows.shape
    tile = rows * row_count
    part = tile // 2
    split = expert_down.shape[1]
    shared_split = shared_down.shape[0]
    shared_steps = steps // 2
    halves = [pl.ds(pl.multiple_of(side * width, width), width) for side in (col, 1 - col)]
    targets = [expert_hidden, expert_gating, expert_upward]
    shared_targets = [shared_gating, shared_upward]
    gather = Gather(
        mixer_rows, lambda index: all_mixer.at[0, index], lambda index: all_mixer.at[1, index],
        gather_sems, False,
    )

    def line_of(at):
        place = at % slow
        near = [
            sorted(range(slow), key=lambda line, own=own: (abs(line - own), line))
            for own in range(slow)
        ]
        line = jnp.int32(0)
        for own in range(slow):
            for number in range(slow):
                line = line + jnp.where(
                    (slow_at == own) & (place == number), near[own][number], 0
                ).astype(jnp.int32)
        return line

    def group_of(at):
        fast_off = at // slow
        return line_of(at) * fast + (fast_at + fast - fast_off) % fast

    def weight_copies():
        pairs = [
            (expert_gate.at[col], gates.at[0]),
            (gate_other, gates.at[1]),
            (expert_up.at[col], ups.at[0]),
            (up_other, ups.at[1]),
        ]
        own_rows = pl.ds(pl.multiple_of(col * split, 16), split)
        other_rows = pl.ds(pl.multiple_of((1 - col) * split, 16), split)
        shared_own = pl.ds(pl.multiple_of(col * shared_split, 16), shared_split)
        shared_other = pl.ds(pl.multiple_of((1 - col) * shared_split, 16), shared_split)
        for side in range(2):
            pairs += [
                (expert_down.at[col, :, halves[side]], downs.at[side, own_rows]),
                (down_other.at[col, :, halves[side]], downs.at[side, other_rows]),
            ]
        pairs += [
            (shared_gate, shared_gates.at[0]),
            (shared_gate_other, shared_gates.at[1]),
            (shared_up, shared_ups.at[0]),
            (shared_up_other, shared_ups.at[1]),
        ]
        for side in range(2):
            pairs += [
                (shared_down.at[:, halves[side]], shared_downs.at[side, shared_own]),
                (shared_down_other.at[:, halves[side]], shared_downs.at[side, shared_other]),
            ]
        return [
            pltpu.make_async_copy(src, dst, weight_sems.at[number])
            for number, (src, dst) in enumerate(pairs)
        ]

    def known_copies(at):
        group = group_of(at)
        slot = at % 3
        blocks = pl.ds(group * row_count, row_count)
        span = pl.ds(pl.multiple_of(group * tile, tile), tile)
        return [
            pltpu.make_async_copy(
                all_grad.at[blocks, side], inputs.at[slot, 2 + number],
                input_sems.at[slot, 2 + number],
            )
            for number, side in enumerate((col, 1 - col))
        ] + [pltpu.make_async_copy(tables.at[span], table.at[slot], input_sems.at[slot, 4])]

    def mixer_copies(at):
        slot = at % 3
        blocks = pl.ds(group_of(at) * row_count, row_count)
        return [
            pltpu.make_async_copy(
                all_mixer.at[side, blocks], inputs.at[slot, side], input_sems.at[slot, side]
            )
            for side in range(2)
        ]

    def results(at, slot):
        columns = pl.ds(pl.multiple_of(group_of(at) * tile, tile), tile)
        local, far = [], []
        for number, target in enumerate(targets):
            spot = target.at[col, :, columns]
            local.append(
                pltpu.make_async_copy(tiles.at[slot, number], spot, local_sems.at[slot, number])
            )
            far.append(
                pltpu.make_async_remote_copy(
                    src_ref=tiles.at[slot, number],
                    dst_ref=spot,
                    send_sem=send_sems.at[slot, number],
                    recv_sem=recv_sems.at[number, at],
                    device_id=core,
                    device_id_type=MESH,
                )
            )
        local.append(
            pltpu.make_async_copy(
                turned_tiles.at[slot], mixer_turned.at[:, columns], local_sems.at[slot, 3]
            )
        )
        return local, far

    def shared_span(turn, member, side):
        first = group_of(2 * turn + member) * tile + side * part
        return pl.ds(pl.multiple_of(first, part), part)

    def shared_results(turn, slot):
        own_rows = pl.ds(pl.multiple_of(col * shared_split, 16), shared_split)
        other_rows = pl.ds(pl.multiple_of((1 - col) * shared_split, 16), shared_split)
        local, far = [], []
        for member in range(2):
            span = shared_span(turn, member, col)
            here = pl.ds(member * part, part)
            triples = [
                (shared_tiles.at[slot, number, here], target.at[span],
                 shared_tiles.at[slot, number, here])
                for number, target in enumerate(shared_targets)
            ]
            triples.append(
                (shared_turned.at[slot, own_rows, here], shared_hidden.at[:, span],
                 shared_turned.at[slot, other_rows, here])
            )
            for number, (near, goal, away) in enumerate(triples):
                local.append(
                    pltpu.make_async_copy(near, goal, shared_local.at[slot, member, number])
                )
                far.append(
                    pltpu.make_async_remote_copy(
                        src_ref=away,
                        dst_ref=goal,
                        send_sem=shared_send.at[slot, member, number],
                        recv_sem=shared_recv.at[number, member, turn],
                        device_id=core,
                        device_id_type=MESH,
                    )
                )
        return local, far

    def wait_out(pair):
        local, far = pair
        for copy in local:
            copy.wait()
        for copy in far:
            copy.wait_send()

    def fetch(at):
        gather.ready(line_of(at), at // slow)
        for copy in mixer_copies(at):
            copy.start()

    weights_early = 8

    @pl.when(step == 0)
    def _():
        for copy in weight_copies()[:weights_early] + known_copies(0):
            copy.start()
        enter(peers(True))
        gather.start()
        for copy in weight_copies()[weights_early:]:
            copy.start()
        gather.corner(0)
        gather.hop(1)
        gather.keep().wait()
        fetch(0)
        for copy in weight_copies()[:weights_early]:
            copy.wait()

    slot = step % 2

    @pl.when(step + 1 < steps)
    def _():
        for copy in known_copies(step + 1):
            copy.start()

    @pl.when(step >= 2)
    def _():
        wait_out(results(step - 2, slot))

    for copy in known_copies(step) + mixer_copies(step):
        copy.wait()

    def block(at, number):
        return inputs[at % 3, number].reshape(tile, width)

    mixers = (block(step, 0), block(step, 1))
    grads = (block(step, 2), block(step, 3))
    turned_tiles[slot] = mixers[0].T

    def both(pair, weights, product):
        return product(pair[0], weights[0]) + product(pair[1], weights[1])

    def turned(weights, pair):
        return matmul_right(weights[0], pair[0]) + matmul_right(weights[1], pair[1])

    columns = table[step % 3].T
    own_expert = (lax.axis_index("exp") * expert_down.shape[0] + col).astype(jnp.float32)
    chosen = columns[TABLE["ids"] : TABLE["ids"] + TOP]
    router = columns[TABLE["router"] : TABLE["router"] + TOP]
    scale = jnp.sum(jnp.where(chosen == own_expert, router, 0.0), axis=0, keepdims=True)
    hidden, gating, upward = unit_grads(
        turned(gates, mixers), turned(ups, mixers), turned(downs, grads) * scale
    )
    tiles[slot, 0] = (hidden * scale).astype(jnp.bfloat16)
    tiles[slot, 1] = gating
    tiles[slot, 2] = upward
    local, far = results(step, slot)
    for copy in local + far:
        copy.start()

    @pl.when(step == 0)
    def _():
        gather.hop(2)
        gather.corner(1)
        for copy in weight_copies()[weights_early:]:
            copy.wait()

    @pl.when(step == 1)
    def _():
        gather.hop(3)
        gather.corner(2)

    @pl.when(step == 2)
    def _():
        gather.corner(3)
        gather.last(0)

    for number in range(1, slow):

        @pl.when(step == number + 2)
        def _():
            gather.last(number)

    @pl.when(step + 1 < steps)
    def _():
        fetch(step + 1)

    @pl.when(step % 2 == 1)
    def _():
        turn = step // 2
        turn_slot = turn % 2

        @pl.when(turn >= 2)
        def _():
            wait_out(shared_results(turn - 2, turn_slot))

        first = col * (row_count // 2)

        def pick(number):
            wanted = pl.ds(first, row_count // 2)
            return jnp.concatenate(
                [
                    inputs[at % 3, number, wanted].reshape(part, width)
                    for at in (step - 1, step)
                ],
                axis=0,
            )

        chosen_rows = [pick(number) for number in range(4)]
        hidden, gating, upward = unit_grads(
            both(chosen_rows[:2], shared_gates, matmul),
            both(chosen_rows[:2], shared_ups, matmul),
            both(chosen_rows[2:], shared_downs, matmul_right),
        )
        shared_tiles[turn_slot, 0] = gating
        shared_tiles[turn_slot, 1] = upward
        shared_turned[turn_slot] = hidden.astype(jnp.bfloat16).T
        local, far = shared_results(turn, turn_slot)
        for copy in local + far:
            copy.start()

    @pl.when(step == steps - 1)
    def _():
        for back in range(2):
            at = steps - 1 - back
            wait_out(results(at, at % 2))
            turn = shared_steps - 1 - back
            wait_out(shared_results(turn, turn % 2))

        @pl.loop(0, steps)
        def _(at):
            columns = pl.ds(pl.multiple_of(group_of(at) * tile, tile), tile)
            for number, target in enumerate(targets):
                spot = target.at[1 - col, :, columns]
                pltpu.make_async_copy(spot, spot, recv_sems.at[number, at]).wait()

        @pl.loop(0, shared_steps)
        def _(turn):
            for member in range(2):
                span = shared_span(turn, member, 1 - col)
                spots = [target.at[span] for target in shared_targets]
                spots.append(shared_hidden.at[:, span])
                for number, spot in enumerate(spots):
                    pltpu.make_async_copy(
                        spot, spot, shared_recv.at[number, member, turn]
                    ).wait()

        gather.finish(True)


def run_units(mixer_rows, tables, grad, weights, collective_id):
    rows, width = mixer_rows.shape
    exp_count, row_count = lax.axis_size("exp"), lax.axis_size("row")
    tokens = tables.shape[0]
    tile = rows * row_count
    units = weights[0].shape[1]
    shared_units = weights[6].shape[1]
    kind = jnp.bfloat16
    pair = jax.ShapeDtypeStruct((2, units, tokens), kind)
    shared = jax.ShapeDtypeStruct((tokens, shared_units), kind)
    half = jax.ShapeDtypeStruct((shared_units // 2, tokens), kind)
    steps = exp_count
    dma = pltpu.SemaphoreType.DMA
    mixer, *others = pl.pallas_call(
        units_kernel,
        out_shape=[
            jax.ShapeDtypeStruct((2, exp_count * row_count, rows, width), kind),
            pair, pair, pair, half, shared, shared, jax.ShapeDtypeStruct((width, tokens), kind),
        ],
        grid=(steps,),
        in_specs=[ANY_SPEC] * (len(weights) + 3),
        out_specs=[ANY_SPEC] * 8,
        scratch_shapes=[
            pltpu.VMEM((2, units, width), kind),
            pltpu.VMEM((2, units, width), kind),
            pltpu.VMEM((2, units, width), kind),
            pltpu.VMEM((2, width, shared_units), kind),
            pltpu.VMEM((2, width, shared_units), kind),
            pltpu.VMEM((2, shared_units, width), kind),
            pltpu.VMEM((3, 4, row_count, rows, width), kind),
            pltpu.VMEM((3, tile, 128), jnp.float32),
            pltpu.VMEM((2, 3, units, tile), kind),
            pltpu.VMEM((2, width, tile), kind),
            pltpu.VMEM((2, 2, tile, shared_units), kind),
            pltpu.VMEM((2, shared_units, tile), kind),
            dma((16,)),
            dma((3, 5)),
            dma((2, 4)),
            dma((2, 3)),
            dma((3, steps)),
            dma((2, 2, 3)),
            dma((2, 2, 3)),
            dma((3, 2, steps // 2)),
            *Gather.sems(),
        ],
        compiler_params=pltpu.CompilerParams(
            collective_id=collective_id, has_side_effects=True, vmem_limit_bytes=VMEM_LIMIT
        ),
        cost_estimate=pl.CostEstimate(
            flops=2 * tokens * units * width * 2 * 6,
            bytes_accessed=50 * 1024 * 1024,
            transcendentals=2 * tokens * units,
        ),
    )(mixer_rows, tables, grad, *weights)
    return mixer.reshape(2, tokens, width), *others


def tail_kernel(
    rows, inverse_one, gain, grad_hidden, sums_in, latent_normed, latent_scale, latent_gain,
    keyvalue_weight, query_other, latent_weight,
    grad_query, grad_keyvalue, grad_rope, query_weight,
    attended_turned, stream, attention_turned, compressed_turned,
    input_grad, sums, latent_all, output_weight_grad, keyvalue_weight_grad, query_weight_grad,
    queries, keyvalues, ropes, query_own, latent_out, latent_in, latent_row_in, wide_out, wide_in,
    wide_rows, wide_row_in, latent_block, squares, squares_in,
    running, slow_in, fast_in, row_in, core_in,
    total_scratch,
    local_sems, core_sems, row_sems, slow_sums, fast_sums, row_sums, core_sums, *gather_sems,
    fused
):
    (slow_at, fast_at, row_at, col_at), (slow, fast, row_count) = positions()
    slow_ids, fast_ids, row_ids, core_ids = peers(True)
    core = core_ids[0]
    count, width = rows.shape
    group = row_count * count
    group_rows = pl.ds(pl.multiple_of(lax.axis_index("exp") * group, group), group)
    query_width = query_own.shape[1]
    jobs = []
    if fused:
        jobs = weight_jobs(
            (
                attended_turned, stream, attention_turned, compressed_turned, grad_query,
                grad_keyvalue,
            ),
            (output_weight_grad, keyvalue_weight_grad, query_weight_grad),
            total_scratch,
        )

    def work():
        if jobs:
            jobs.pop(0)()

    own_heads = pl.ds(pl.multiple_of(col_at * query_width, query_width), query_width)
    loads = [
        pltpu.make_async_copy(source, target, local_sems.at[number])
        for number, (source, target) in enumerate(
            (
                (grad_keyvalue.at[group_rows], keyvalues),
                (grad_rope.at[group_rows], ropes),
                (grad_query.at[0, group_rows], queries),
                (query_weight.at[:, own_heads], query_own),
            )
        )
    ]
    for copy in loads:
        copy.start()
    enter((slow_ids, fast_ids, row_ids, core_ids))
    for copy in loads:
        copy.wait()
    compressed = matmul_right(keyvalues[...], keyvalue_weight[...])
    unit = latent_normed[...]
    scaled = compressed * latent_gain[:1]
    inner = jnp.mean(scaled * unit, axis=1, keepdims=True)
    raw = latent_scale[...] * (scaled - unit * inner)
    latent_out[0] = jnp.concatenate([raw, ropes[...]], axis=1).astype(jnp.bfloat16)
    started = [remote(latent_out.at[0], latent_in, core_sems, (0,), core)]
    wide_out[...] = matmul_right(queries[...], query_other[...]).astype(jnp.bfloat16)
    started.append(remote(wide_out, wide_in, core_sems, (1,), core))
    latent_gain_part = jnp.sum(compressed * unit, axis=0, keepdims=True)
    own_wide = matmul_right(queries[...], query_own[...])
    wait_arrived(latent_in, core_sems, (0,))
    latent_out[1] = (
        latent_out[0].astype(jnp.float32) + latent_in[...].astype(jnp.float32)
    ).astype(jnp.bfloat16)
    for number, device in enumerate(row_ids):
        started.append(
            remote(latent_out.at[1], latent_row_in.at[number], row_sems, (0, number), device)
        )
    wait_arrived(wide_in, core_sems, (1,))
    own_wide = own_wide + wide_in[...].astype(jnp.float32)
    wide_rows[...] = own_wide.astype(jnp.bfloat16).reshape(wide_rows.shape)
    for number, device in enumerate(row_ids):
        goal = (row_at + number + 1) % row_count
        started.append(
            remote(wide_rows.at[goal], wide_row_in.at[number], row_sems, (1, number), device)
        )
    work()
    latent = latent_out[1].astype(jnp.float32)
    for number in range(row_count - 1):
        wait_arrived(latent_row_in.at[number], row_sems, (0, number))
        latent = latent + latent_row_in[number].astype(jnp.float32)
    latent_out[2] = latent.astype(jnp.bfloat16)
    part = count // 2
    first = pl.multiple_of(row_at * count, count)
    latent_block[...] = latent_out[2, pl.ds(pl.multiple_of(first + col_at * part, part), part)]
    gather = Gather(
        latent_block, lambda index: latent_all.at[index, col_at],
        lambda index: latent_all.at[index, 1 - col_at], gather_sems, True,
    )
    gather.start()
    steps = gather.steps()
    gradient = matmul(latent_out[2, pl.ds(first, count)], latent_weight[...])
    gradient = gradient + wide_rows[row_at].astype(jnp.float32)
    for number in range(row_count - 1):
        wait_arrived(wide_row_in.at[number], row_sems, (1, number))
        gradient = gradient + wide_row_in[number].astype(jnp.float32)
    scale = inverse_one[:, :1]
    normed = rows[...].astype(jnp.float32) * scale
    scaled = gradient * gain[:1]
    squares[...] = jnp.broadcast_to(
        jnp.sum(scaled * normed, axis=1, keepdims=True), squares.shape
    )
    started.append(remote(squares, squares_in, core_sems, (2,), core))
    steps.pop(0)()
    gain_part = jnp.sum(gradient * normed, axis=0, keepdims=True)
    row = lax.broadcasted_iota(jnp.int32, sums_in.shape, 0)
    padded = jnp.concatenate(
        [latent_gain_part, jnp.zeros((1, width - latent_gain_part.shape[1]), jnp.float32)], axis=1
    )
    total = jnp.where(row == 0, gain_part, jnp.where(row == 2, padded, sums_in[...]))
    wait_arrived(squares_in, core_sems, (2,))
    inner = (squares[...] + squares_in[...])[:, :1] / (2 * width)
    input_grad[...] = grad_hidden[...] + scale * (scaled - normed * inner)
    work()
    stages = (
        (slow_ids, slow_in, slow_sums),
        (fast_ids, fast_in, fast_sums),
        (row_ids, row_in, row_sums),
        (core_ids, core_in, core_sums),
    )
    for stage, (devices, buffer, sems) in enumerate(stages):
        running[stage] = total
        for number, device in enumerate(devices):
            started.append(
                remote(running.at[stage], buffer.at[number], sems, (number,), device)
            )
        steps.pop(0)()
        for number in range(len(devices)):
            wait_arrived(buffer.at[number], sems, (number,))
            arrived = buffer[number]
            total = total + (jnp.where(row == 2, arrived, 0.0) if stage == 3 else arrived)
    sums[...] = total
    for step in steps[: slow - 1]:
        step()
    while jobs:
        work()
    for step in steps[slow - 1 :]:
        step()
    gather.finish()
    for copy in started:
        copy.wait_send()


def weight_jobs(inputs, outputs, total):
    attended, stream, turned, small_turned, query_both, keyvalue = inputs
    return [
        row_job(small_turned, keyvalue, outputs[1], total),
        sided_job(attended, stream, outputs[0], total),
        sided_job(turned, query_both, outputs[2], total),
    ]


def tail(operands, shapes, fused, collective_id):
    exp_count, row_count = lax.axis_size("exp"), lax.axis_size("row")
    slow = min(4, exp_count)
    fast = exp_count // slow
    rows = operands[0]
    count, width = rows.shape
    group = row_count * count
    latent_width = operands[10].shape[0]
    query_width, keyvalue_width = operands[9].shape[1], operands[8].shape[1]
    low, high = jnp.bfloat16, jnp.float32
    vmem = pl.BlockSpec(memory_space=pltpu.VMEM)
    dma = pltpu.SemaphoreType.DMA
    sums = (8, width)
    counts = (slow - 1, fast - 1, row_count - 1, 1)
    return pl.pallas_call(
        functools.partial(tail_kernel, fused=fused),
        out_shape=[
            jax.ShapeDtypeStruct((count, width), high),
            jax.ShapeDtypeStruct(sums, high),
            jax.ShapeDtypeStruct((exp_count * row_count, 2, count // 2, latent_width), low),
            *shapes,
        ],
        in_specs=[vmem] * 11 + [ANY_SPEC] * 8,
        out_specs=[vmem, vmem] + [ANY_SPEC] * 4,
        scratch_shapes=[
            pltpu.VMEM((group, query_width), low),
            pltpu.VMEM((group, keyvalue_width), low),
            pltpu.VMEM((group, DR), high),
            pltpu.VMEM((width, query_width), low),
            pltpu.VMEM((3, group, latent_width), low),
            pltpu.VMEM((group, latent_width), low),
            pltpu.VMEM((row_count - 1, group, latent_width), low),
            pltpu.VMEM((group, width), low),
            pltpu.VMEM((group, width), low),
            pltpu.VMEM((row_count, count, width), low),
            pltpu.VMEM((row_count - 1, count, width), low),
            pltpu.VMEM((count // 2, latent_width), low),
            pltpu.VMEM((count, 128), high),
            pltpu.VMEM((count, 128), high),
            pltpu.VMEM((4, *sums), high),
            *[pltpu.VMEM((number, *sums), high) for number in counts],
            pltpu.VMEM(TOTAL if fused else (8, 128), high),
            dma((4,)),
            dma((2, 3)),
            dma((2, 2, row_count - 1)),
            *[dma((2, number)) for number in counts],
            *Gather.sems(),
        ],
        compiler_params=pltpu.CompilerParams(
            collective_id=collective_id, has_side_effects=True, vmem_limit_bytes=VMEM_LIMIT
        ),
    )(*operands)


def local(
    layer_input,
    attention_gain,
    query_weight,
    latent_weight,
    latent_gain,
    keyvalue_weight,
    output_weight,
    feedforward_gain,
    shared_gate,
    shared_up,
    shared_down,
    expert_gate,
    expert_up,
    expert_down,
    sequence_lengths,
    expert_ids,
    expert_weights,
    output_grad,
):
    exp_index, row_index, col_index = (
        lax.axis_index("exp"),
        lax.axis_index("row"),
        lax.axis_index("col"),
    )
    exp_count = lax.axis_size("exp")
    local_tokens, half_width = layer_input.shape
    full_width = 2 * half_width
    per_device = expert_gate.shape[0]
    group_size = local_tokens * lax.axis_size("row")
    tokens = group_size * exp_count
    group_start = exp_index * group_size

    def part_of(array, side, axis):
        width = array.shape[axis] // 2
        return lax.dynamic_slice_in_dim(array, side * width, width, axis)

    def split_exchange(array, axis):
        return part_of(array, col_index, axis), swap_core(part_of(array, 1 - col_index, axis))

    def own_rows(array):
        return lax.dynamic_slice_in_dim(array, group_start, group_size, 0)

    col = col_index.reshape(1)
    top = expert_ids.shape[1]
    _, places = sequence_layout(sequence_lengths[0], group_size)
    cosine, sine = rope_tables(places)
    first_key = jnp.arange(group_size, dtype=jnp.int32) - places

    def widened(array, width):
        return jnp.pad(array.astype(jnp.float32), ((0, 0), (0, width - array.shape[1])))

    tables = jnp.concatenate(
        [
            widened(expert_ids, 8),
            widened(expert_weights, 8),
            widened(first_key[:, None], 16),
            cosine,
            sine,
            jnp.zeros((group_size, 32), jnp.float32),
        ],
        axis=1,
    )
    latent_turned = latent_weight.T
    gate_turned, up_turned = expert_gate.swapaxes(1, 2), expert_up.swapaxes(1, 2)
    gain_own = jnp.broadcast_to(attention_gain.astype(jnp.float32), (8, half_width))
    latent_gains = jnp.broadcast_to(latent_gain.astype(jnp.float32), (8, R))

    gain_two = feedforward_gain.astype(jnp.float32)
    (
        own_normed, own_scale, inverse_one, hidden_state, normed_two, scale_two, mixer_input,
        tables_all, grad_all, input_all, query_other, latent_other, gain_other,
        gate_other, up_other, down_other, shared_gate_other, shared_up_other, shared_down_other,
    ) = prologue(
        layer_input, gain_own, latent_gains, keyvalue_weight, output_weight,
        gain_two[None], tables, query_weight, latent_turned, output_grad,
        (gate_turned, up_turned, expert_down, shared_gate, shared_up, shared_down), 6,
    )
    scale_two = scale_two[:, :1]
    weights = (
        gain_own, gain_other, query_weight, query_other, latent_turned, latent_other,
        latent_gains, keyvalue_weight,
    )
    tables_all = tables_all.reshape(tokens, -1)
    (
        mixer, both_hidden, both_gating, both_upward, shared_hidden, shared_gating, shared_upward,
        mixer_turned,
    ) = run_units(
        mixer_input,
        tables_all,
        grad_all,
        (
            gate_turned, gate_other, up_turned, up_other, expert_down, down_other,
            shared_gate, shared_gate_other, shared_up, shared_up_other,
            shared_down, shared_down_other,
        ),
        1,
    )
    fused = tokens <= 2048
    low = jnp.bfloat16

    def shape(*sizes, kind=low):
        return jax.ShapeDtypeStruct(sizes, kind)

    units, shared_units = gate_turned.shape[1], shared_gate.shape[1]

    def gate_jobs(inputs, outputs, total, *_):
        gating, upward, rows, rows_turned, own_gating, own_upward = inputs
        return [
            stacked_job(gating, rows, outputs[0], total),
            stacked_job(upward, rows, outputs[1], total),
            row_job(rows_turned, own_gating, outputs[2], total),
            row_job(rows_turned, own_upward, outputs[3], total),
        ]

    gate_operands = (
        both_gating, both_upward, mixer, mixer_turned, shared_gating, shared_upward
    )
    gate_shapes = [shape(per_device, units, half_width)] * 2 + [
        shape(half_width, shared_units)
    ] * 2
    products = (
        both_gating, both_upward, gate_turned, up_turned, shared_gating, shared_upward,
        shared_gate, shared_up,
    )
    if fused:
        mixer_grad, *gate_grads = scatter_products(
            products, True, 2, gate_jobs, gate_operands, gate_shapes
        )
    else:
        (mixer_grad,) = scatter_products(products, True, 2)
        gate_grads = run_jobs(gate_jobs, gate_operands, gate_shapes)

    upstream = output_grad.astype(jnp.float32)
    grad_norm_two, gain_two_grad = norm_backward(mixer_grad, normed_two, scale_two, gain_two)
    grad_hidden = upstream + grad_norm_two

    heads_width = keyvalue_weight.shape[1] // 2
    query_width = query_weight.shape[1] // 2

    def stream_jobs(inputs, outputs, total):
        hidden, own_hidden, grads, values = inputs[:4]
        return [
            *project_jobs(values, inputs[4:12], inputs[12], outputs[2:], 2),
            expert_down_job(hidden, grads, outputs[0], total),
            shared_down_job(own_hidden, grads, outputs[1], total),
        ]

    stream_operands = (
        both_hidden, shared_hidden, grad_all, input_all, *weights, tables_all
    )
    stream_shapes = [
        shape(*expert_down.shape),
        shape(*shared_down.shape),
        shape(tokens, query_width),
        shape(tokens, keyvalue_weight.shape[1]),
        shape(tokens, DR),
        shape(half_width, tokens),
        shape(R, tokens),
    ]
    stream_input = grad_hidden.astype(jnp.bfloat16)
    if fused:
        stream, results = gather_everywhere(
            stream_input, 3, stream_jobs, stream_operands, stream_shapes
        )
    else:
        stream, _ = gather_everywhere(stream_input, 3)
        results = run_jobs(stream_jobs, stream_operands, stream_shapes)
    (
        expert_down_grad, shared_down_grad, query_all, keyvalue_all, rope_key_all,
        attention_turned, compressed_turned,
    ) = results

    other_hidden = swap_core(
        lax.dynamic_slice_in_dim(shared_hidden, group_start, group_size, 1)
    )

    def attention_part(inputs, outputs, total, core, sems):
        arrays, (stream_ref, weight) = inputs[:4], inputs[4:]
        attended_ref, query_both, keyvalue_ref, rope_ref = outputs
        jobs = attention_jobs(
            arrays, stream_ref, weight,
            (attended_ref, query_both.at[0], keyvalue_ref, rope_ref), exp_count, 4,
        )

        def exchange():
            remote(query_both.at[0], query_both.at[1], sems, (0,), core).wait()

        return [*jobs, exchange]

    weight_shapes = [
        shape(*output_weight.shape), shape(*keyvalue_weight.shape), shape(*query_weight.shape)
    ]
    (
        produced, attended_turned, query_grads, grad_keyvalue, grad_rope
    ) = scatter_products(
        (
            both_hidden, expert_down, down_other, shared_hidden, other_hidden,
            shared_down, shared_down_other,
        ),
        False,
        4,
        attention_part,
        (
            tables_all, query_all, keyvalue_all, rope_key_all, stream, output_weight,
        ),
        [
            shape(heads_width, tokens),
            shape(2, tokens, query_width),
            shape(tokens, keyvalue_weight.shape[1]),
            shape(tokens, DR, kind=jnp.float32),
        ],
    )
    layer_result = (hidden_state + produced).astype(jnp.bfloat16)
    sums_in = jnp.pad(gain_two_grad[None], ((1, 6), (0, 0)))
    weight_operands = (attended_turned, stream, attention_turned, compressed_turned)
    input_grad, sums, latent_all, *weight_grads = tail(
        (
            layer_input, inverse_one, gain_own, grad_hidden, sums_in, own_normed, own_scale,
            latent_gains, keyvalue_weight, query_other, latent_turned,
            query_grads, grad_keyvalue, grad_rope, query_weight, *weight_operands,
        ),
        weight_shapes,
        fused,
        5,
    )
    if not fused:
        weight_grads = run_jobs(
            weight_jobs, (*weight_operands, query_grads, grad_keyvalue), weight_shapes
        )
    output_weight_grad, keyvalue_weight_grad, query_weight_grad = weight_grads
    latent_weight_grad = matmul(attention_turned, latent_all.reshape(tokens, -1))
    wide = [
        array.astype(jnp.float32)
        for array in (
            query_weight_grad, keyvalue_weight_grad, output_weight_grad, *gate_grads,
            shared_down_grad, expert_down_grad,
        )
    ]
    return (
        layer_result,
        input_grad,
        sums[0],
        wide[0],
        latent_weight_grad,
        sums[2, : latent_gain.shape[0]],
        wide[1],
        wide[2],
        sums[1],
        wide[5],
        wide[6],
        wide[7],
        wide[3].swapaxes(1, 2),
        wide[4].swapaxes(1, 2),
        wide[8],
    )


def solution(mesh):
    in_specs = (
        P(("exp", "row"), "col"),
        P("col"),
        P("col", "row"),
        P("col", None),
        P(),
        P(None, ("row", "col")),
        P(("row", "col"), None),
        P("col"),
        P("col", "row"),
        P("col", "row"),
        P(("row", "col"), None),
        P("exp", "col", "row"),
        P("exp", "col", "row"),
        P("exp", ("row", "col"), None),
        P("exp", None),
        P("exp", None),
        P("exp", None),
        P(("exp", "row"), "col"),
    )
    out_specs = (
        P(("exp", "row"), "col"),
        P(("exp", "row"), "col"),
        P("col"),
        P("col", "row"),
        P("col", None),
        P(),
        P(None, ("row", "col")),
        P(("row", "col"), None),
        P("col"),
        P("col", "row"),
        P("col", "row"),
        P(("row", "col"), None),
        P("exp", "col", "row"),
        P("exp", "col", "row"),
        P("exp", ("row", "col"), None),
    )
    return jax.shard_map(local, mesh=mesh, in_specs=in_specs, out_specs=out_specs, check_vma=False)
```

time: 624 us -> 544 us (0.87)
  waiting for transfers between devices: 26.4 us -> 0.01 us
  matrix products: 31.8 us -> 7.15 us
  blocking collectives: 26.5 us -> 2.46 us
  other arithmetic: 17.9 us -> 37.4 us
  between operations: 14.5 us -> 1.3 us
  Pallas kernels: 484 us -> 476 us
    all_gather x3 -> x0, waiting for transfers between devices: 25.6 us -> none  [the longest x1 25.6 us: local(): grad_own = lax.all_gather(output_grad, ('exp', 'row'), axis=0, tiled=True)]
    convert_element_type x5 -> x10, other arithmetic: 2.52 us -> 26.2 us  [the longest x7 24.4 us: local(): array.astype(jnp.float32)]
    psum x1 -> x0, blocking collectives: 21.5 us -> none  [local(): lax.psum(jnp.concatenate([grad_craw, own_rows(grad_rope)], axis=1), ('row...]
    dot_general x6 -> x0, matrix products: 18.2 us -> none  [matmul_right(): lax.dot_general(former, latter, (((1,), (1,)), ((), ())), preferred_eleme...]
    pallas_call x20 -> x6, Pallas kernels: 484 us -> 476 us  [the longest x2 140 us: scatter_products(): pl.pallas_call(functools.partial(scatter_kernel, backward=backward, make_...]
    dot_general x2 -> x1, matrix products: 13.7 us -> 7.15 us  [matmul(): return jnp.dot(former, latter, preferred_element_type=jnp.float32)]
  transfers between devices with their start and end apart: 15 -> 1, of which waited for: 1 -> 0; matrix products, arithmetic and copies ran while one was open for 9% -> 5% of each run, Pallas kernels for 79% -> 31%
where the time goes in v2:
time: 544 us; the launch traced here: 537 us
  Pallas kernels  476 us (88%)
  other arithmetic  37.4 us (7%)
  local copies, waits for them, and re-layouts  12.9 us (2%)
  matrix products  7.15 us (1%)
    pallas_call x2, Pallas kernels, scatter_products(): pl.pallas_call(functools.partial(scatter_kernel, backward=backward, make_...  140 us
    pallas_call x1, Pallas kernels, prologue(): pl.pallas_call(prologue_kernel, out_shape=[jax.ShapeDtypeStruct((group, R...  102 us
    pallas_call x1, Pallas kernels, gather_everywhere(): pl.pallas_call(functools.partial(gather_kernel, make_jobs=make_jobs, inpu...  91.1 us
    pallas_call x1, Pallas kernels, run_units(): pl.pallas_call(units_kernel, out_shape=[jax.ShapeDtypeStruct((2, exp_coun...  82.7 us
    pallas_call x1, Pallas kernels, tail(): pl.pallas_call(functools.partial(tail_kernel, fused=fused), out_shape=[ja...  59.9 us
    convert_element_type x7, other arithmetic, local(): array.astype(jnp.float32)  24.4 us
  transfers between devices with their start and end apart: 1, of which 0 were waited for; matrix products, arithmetic and copies ran while one was open for 5% of the time, Pallas kernels for 31%

profile of v2, /device:TPU:0, one launch (start us, length us, event | category | flops | bytes accessed | tf_op | source)
XLA Modules:
  0.0 537.5 jit_solution(17471712224273554590)
XLA Ops:
  0.7 0.8 reduce-window.4
  2.3 1.3 convert_element_type.78
  4.7 0.8 copy.42
  6.1 0.9 concatenate.3.table.tables
  7.0 1.3 broadcast_in_dim.40.latent_gain.refs_11_
  8.3 1.3 broadcast_in_dim.39.gain.refs_5_
  9.6 102.2 %shard_map.289 = (f32[256,512]{1,0:T(8,128)}, f32[256,1]{1,0:T(8,128)}, f32[128,128]{1,0:T(8,128)}, f32[128,1024]{1,0:T(8,128)}, f32[128,1024]{1,0:T(8,128)}, /*...) custom-call(bf16[128,1024]{1,0:T(8,128)(2,1)} %rows.3, ...), custom_call_target="tpu_custom_call" | custom-call | tf_op jit(solution)/shard_map/pallas_call | solution.py:636
  111.8 82.7 %shard_map.290 = (bf16[2,16,128,1024]{3,2,1,0:T(8,128)(2,1)}, bf16[2,704,2048]{2,1,0:T(8,128)(2,1)}, bf16[2,704,2048]{2,1,0:T(8,128)(2,1)}, bf16[2,704,2048]{2,1...) custom-call(bf16[128,1024]{1,0:T(8,128)(2,1)} %get-tuple-element.67., ...), custom_call_target="tpu_custom_call" | custom-call | flops 35433480192 | bytes 52428800 | tf_op jit(solution)/shard_map/pallas_call | solution.py:1614
  194.5 1.0 constant_dynamic-slice_fusion
  196.0 75.8 %shard_map.291 = (f32[128,1024]{1,0:T(8,128)}, bf16[2,704,1024]{2,1,0:T(8,128)(2,1)}, bf16[2,704,1024]{2,1,0:T(8,128)(2,1)}, bf16[1024,1408]{1,0:T(8,128)(2,1)}, bf16[1024,1408]{1,0:T(8,128)(2,1)}) custom-call(bf16[2,704,2048]{2,1,0:T(8,128)(2,1)} %get-tuple-element.79.refs_0_.refs_8_, bf16[2,704,2048]{2,1,0:T(8,128)(2,1)} %get-tuple-element.80.refs_1_.refs_9_, ...), custom_call_target="tpu_custom_call" | custom-call | flops 11811160064 | bytes 74448896 | tf_op jit(solution)/shard_map/pallas_call | solution.py:1226
  271.8 1.2 multiply_reduce_fusion
  273.1 2.5 psum.7
  276.2 4.9 convert_element_type.85
  281.0 2.9 convert_element_type.86
  283.9 1.1 fusion.1
  285.0 91.1 %shard_map.292 = (bf16[2,16,128,1024]{3,2,1,0:T(8,128)(2,1)}, bf16[2,352,2048]{2,1,0:T(8,128)(2,1)}, bf16[704,2048]{1,0:T(8,128)(2,1)}, bf16[2048,768]{1,0:T(8,1...) custom-call(bf16[128,1024]{1,0:T(8,128)(2,1)} %get-tuple-element.119, ...), custom_call_target="tpu_custom_call" | custom-call | bytes 33554432 | tf_op jit(solution)/shard_map/pallas_call | solution.py:961
  376.1 5.3 convert_element_type.87
  381.4 3.7 convert_element_type.88
  385.1 1.1 copy-done.4
  386.2 5.8 %convert_bitcast_fusion = (f32[2,1024,704]{1,2,0:T(8,128)}, f32[2,1024,704]{1,2,0:T(8,128)}) fusion(bf16[2,704,1024]{2,1,0:T(8,128)(2,1)S(1)} %copy-done.4, bf16[2,704,1024]{2,1,0:T(8,128)(2,1)S(1)} %copy-done.3), kind=kLoop, calls=%fused_computation | loop fusion | flops 2883584 | bytes 17301504 | tf_op jit(solution)/shard_map/transpose | solution.py:2120
  391.9 0.7 copy-done.13
  392.7 64.1 %shard_map.293 = (f32[128,1024]{1,0:T(8,128)}, bf16[512,2048]{1,0:T(8,128)(2,1)}, bf16[2,2048,768]{2,1,0:T(8,128)(2,1)}, bf16[2048,1024]{1,0:T(8,128)(2,1)}, f32[2048,64]{1,0:T(8,128)}) custom-call(bf16[2,704,2048]{2,1,0:T(8,128)(2,1)} %get-tuple-element.76.refs_1_.refs_0_, bf16[2,352,2048]{2,1,0:T(8,128)(2,1)} %refs_1_.1, ...), custom_call_target="tpu_custom_call" | custom-call | flops 5905580032 | bytes 68681728 | tf_op jit(solution)/shard_map/pallas_call | solution.py:1226
  456.8 59.9 %shard_map.294 = (f32[128,1024]{1,0:T(8,128)}, f32[8,1024]{1,0:T(8,128)}, bf16[16,2,64,576]{3,2,1,0:T(8,128)(2,1)}, bf16[512,2048]{1,0:T(8,128)(2,1)}, bf16[512,...) custom-call(bf16[128,1024]{1,0:T(8,128)(2,1)} %rows.3, f32[128,128]{1,0:T(8,128)} %get-tuple-element.96.inverse_one, ...), custom_call_target="tpu_custom_call" | custom-call | tf_op jit(solution)/shard_map/pallas_call | solution.py:1827
  516.8 1.3 slice.14
  518.1 1.4 fusion.2
  519.5 7.1 %fusion.3 = f32[1024,576]{0,1:T(8,128)} fusion(bf16[1024,2048]{1,0:T(8,128)(2,1)} %get-tuple-element.103.attention_turned, bf16[2048,576]{1,0:T(8,128)(2,1)} %bitcast.48), kind=kOutput, calls=%fused_computation.22 | convolution fusion | flops 2415919104 | bytes 8912896 | tf_op jit(solution)/shard_map/dot_general | solution.py:23
  526.6 1.6 convert_element_type.83
  528.2 0.8 copy-done.5
  529.0 2.5 convert_element_type.84
  531.9 3.6 convert_element_type.82
  535.5 0.8 add_convert_fusion
  536.2 0.8 copy.46
  (49 shorter events, 3.9 us)
Async XLA Ops:
  111.8 84.0 %copy-start.15 = (f32[128,128]{1,0:T(8,128)S(1)}, f32[128,128]{1,0:T(8,128)}, u32[]{:S(2)}) copy-start(f32[128,128]{1,0:T(8,128)} %get-tuple-element.78) | copy-start | bytes 196612
  195.5 196.4 %collective-permute-start = (bf16[704,256]{1,0:T(8,128)(2,1)S(1)}, bf16[704,256]{1,0:T(8,128)(2,1)S(1)}, u32[]{:S(2)}, u32[]{:S(2)}) collective-permute-start(bf16[704,256]{1,0:T(8,128)(2,1)S(1)} %constant_dynamic-slice_fusion), channel_id=1, source_target_pairs={{0,1},{1,0},{2,3},{3,2},{4,5},{5,4},{6,7},{7,6},{8,9},{9,8},{10,11... | collective-permute-start | bytes 1081352 | tf_op jit(solution)/shard_map/ppermute | solution.py:74
  196.0 75.9 %copy-start.6 = (f32[128,1024]{1,0:T(8,128)S(1)}, f32[128,1024]{1,0:T(8,128)}, u32[]{:S(2)}) copy-start(f32[128,1024]{1,0:T(8,128)} %get-tuple-element.86) | copy-start | bytes 1572868
  196.0 75.9 %copy-start.14 = (f32[1024]{0:T(1024)S(1)}, f32[1024]{0:T(1024)}, u32[]{:S(2)}) copy-start(f32[1024]{0:T(1024)} %convert_element_type.78) | copy-start | bytes 12292
  276.1 4.9 copy-start.1
  281.0 2.9 copy-start.7
  281.0 2.9 copy-start.8
  376.1 5.3 copy-start.2
  381.4 3.7 copy-start.3
  381.4 4.8 copy-start.4
  391.9 0.7 copy-start.13
  519.5 7.2 %copy-start.9 = (bf16[512,1024]{1,0:T(8,128)(2,1)S(1)}, bf16[512,1024]{1,0:T(8,128)(2,1)}, u32[]{:S(2)}) copy-start(bf16[512,1024]{1,0:T(8,128)(2,1)} %get-tuple-element.109) | copy-start | bytes 3145732
  526.6 2.3 copy-start.5
  529.0 2.9 copy-start
  531.9 3.6 copy-start.10
  531.9 3.6 copy-start.11
  531.9 4.4 copy-start.12

commit v3 on v2

--- a/solution.py
+++ b/solution.py
@@ -466,10 +466,10 @@
 
 def prologue_kernel(
     rows, gain, latent_gain, keyvalue_weight, output_weight, table,
-    gain_two, tables, query_weight, latent_weight, upstream, rows_source,
+    gain_two, tables, query_weight, latent_weight, upstream,
     gate, up, down, shared_gate, shared_up, shared_down,
     latent_normed, latent_scale, inverse_one, hidden, normed, inverse, mixer,
-    tables_all, grad_all, rows_all, query_far, latent_far, gain_far,
+    tables_all, grad_all, query_far, latent_far, gain_far,
     gate_far, up_far, down_far, shared_gate_far, shared_up_far, shared_down_far,
     rows_own, rows_other, query_own, query_other, latent_own, latent_other, gain_other,
     query, keyvalue, rope_key, attended, scales, given, from_core, rows_out, from_rows,
@@ -487,7 +487,7 @@
     given_heads = pl.ds(pl.multiple_of((1 - col_at) * query_width, query_width), query_width)
     gather = Gather(
         upstream, lambda index: grad_all.at[index, col_at],
-        lambda index: grad_all.at[index, 1 - col_at], gather_sems[: len(gather_sems) // 2], True,
+        lambda index: grad_all.at[index, 1 - col_at], gather_sems, True,
     )
     loads = [
         pltpu.make_async_copy(query_weight.at[:, own_heads], query_own, local_sems.at[0]),
@@ -511,12 +511,7 @@
     for number, device in enumerate(fast_ids):
         started.append(remote(tables, tables_all.at[mine], fast_sems, (number, 0), device))
     gather.start()
-    late = Gather(
-        rows_source, lambda index: rows_all.at[index, col_at],
-        lambda index: rows_all.at[index, 1 - col_at], gather_sems[len(gather_sems) // 2 :], True,
-    )
     steps = gather.steps()
-    late_steps = [late.start] + late.steps()
     for offset in range(1, row_count):
         index = (row_at + row_count - offset) % row_count
         wait_arrived(rows_own.at[index], row_sems, (offset - 1,))
@@ -590,23 +585,19 @@
     squares[...] = jnp.broadcast_to(own_squares, squares.shape)
     started.append(remote(squares, squares_in, mix_core, (1,), core))
     steps.pop(0)()
-    late_steps.pop(0)()
     wait_arrived(squares_in, mix_core, (1,))
     rms = lax.rsqrt((squares[...] + squares_in[...]) / (2 * width) + EPSILON)
     inverse[...] = rms
     unit = state * rms[:, :1]
     normed[...] = unit
     mixer[...] = (unit * gain_two[...]).astype(jnp.bfloat16)
-    while steps or late_steps:
-        for queue in (steps, late_steps):
-            if queue:
-                queue.pop(0)()
+    for step in steps:
+        step()
     for offset in range(slow):
         for number in range(1, fast):
             index = (slow_at + slow - offset) % slow * fast + (fast_at + fast - number) % fast
             wait_arrived(tables_all.at[index], fast_sems, (number - 1, offset))
     gather.finish()
-    late.finish()
     for number, (_, target) in enumerate(exchanged):
         wait_arrived(target, weight_sems, (number,))
     for copy in started:
@@ -642,7 +633,6 @@
             jax.ShapeDtypeStruct((count, width), low),
             jax.ShapeDtypeStruct((exp_count, *tables.shape), high),
             jax.ShapeDtypeStruct((exp_count * row_count, 2, count, width), low),
-            jax.ShapeDtypeStruct((exp_count * row_count, 2, count, width), low),
             jax.ShapeDtypeStruct((width, query_width), low),
             jax.ShapeDtypeStruct(latent_weight.shape, low),
             jax.ShapeDtypeStruct(gain.shape, high),
@@ -651,8 +641,8 @@
                 for number, array in enumerate(others)
             ],
         ],
-        in_specs=[vmem] * 7 + [ANY_SPEC] * 11,
-        out_specs=[vmem] * 7 + [ANY_SPEC] * 12,
+        in_specs=[vmem] * 7 + [ANY_SPEC] * 10,
+        out_specs=[vmem] * 7 + [ANY_SPEC] * 11,
         scratch_shapes=[
             pltpu.VMEM((row_count, count, width), low),
             pltpu.VMEM((row_count, count, width), low),
@@ -682,14 +672,13 @@
             dma((2, row_count - 1)),
             dma((2, 6)),
             *Gather.sems(),
-            *Gather.sems(),
         ],
         compiler_params=pltpu.CompilerParams(
             collective_id=collective_id, has_side_effects=True, vmem_limit_bytes=VMEM_LIMIT
         ),
     )(
         rows, gain, latent_gain, keyvalue_weight, output_weight, tables, gain_two, tables,
-        query_weight, latent_weight, upstream, rows, *others,
+        query_weight, latent_weight, upstream, *others,
     )
 
 
@@ -942,7 +931,7 @@
     steps = gather.steps()
     slow = gather.sizes[0]
     for number, step in enumerate(steps):
-        if number in (slow - 1, 2 * slow - 1):
+        if number in (0, slow - 2, slow + 1, 2 * slow):
             work()
         step()
     while jobs:
@@ -1274,10 +1263,10 @@
 
 
 def units_kernel(
-    mixer_rows, tables, all_grad,
+    mixer_rows, tables, all_grad, layer_rows,
     expert_gate, gate_other, expert_up, up_other, expert_down, down_other,
     shared_gate, shared_gate_other, shared_up, shared_up_other, shared_down, shared_down_other,
-    all_mixer,
+    all_mixer, all_rows,
     expert_hidden, expert_gating, expert_upward, shared_hidden, shared_gating, shared_upward,
     mixer_turned,
     gates, ups, downs, shared_gates, shared_ups, shared_downs, inputs, table, tiles, turned_tiles,
@@ -1300,7 +1289,11 @@
     shared_targets = [shared_gating, shared_upward]
     gather = Gather(
         mixer_rows, lambda index: all_mixer.at[0, index], lambda index: all_mixer.at[1, index],
-        gather_sems, False,
+        gather_sems[: len(gather_sems) // 2], False,
+    )
+    late = Gather(
+        layer_rows, lambda index: all_rows.at[index, col],
+        lambda index: all_rows.at[index, 1 - col], gather_sems[len(gather_sems) // 2 :], True,
     )
 
     def line_of(at):
@@ -1508,28 +1501,28 @@
     for copy in local + far:
         copy.start()
 
-    @pl.when(step == 0)
-    def _():
-        gather.hop(2)
-        gather.corner(1)
+    def acts(*number_and_acts):
+        for number, chosen in number_and_acts:
+
+            @pl.when(step == number)
+            def _():
+                for act, *arguments in chosen:
+                    act(*arguments)
+
+    def wait_weights():
         for copy in weight_copies()[weights_early:]:
             copy.wait()
 
-    @pl.when(step == 1)
-    def _():
-        gather.hop(3)
-        gather.corner(2)
-
-    @pl.when(step == 2)
-    def _():
-        gather.corner(3)
-        gather.last(0)
-
-    for number in range(1, slow):
-
-        @pl.when(step == number + 2)
-        def _():
-            gather.last(number)
+    acts(
+        (0, [(gather.hop, 2), (gather.corner, 1), (gather.hop, 3), (wait_weights,)]),
+        (1, [(gather.corner, 2), (gather.last, 0)]),
+        (2, [(gather.corner, 3), (gather.last, 1), (late.start,)]),
+        (3, [(gather.last, 2), (late.hop, 1)]),
+        (4, [(gather.last, 3), (late.hop, 2)]),
+        (5, [(late.hop, 3), (late.corner, 0)]),
+        (6, [(late.corner, 1), (late.corner, 2), (late.last, 0)]),
+        (7, [(late.corner, 3), (late.last, 1)]),
+    )
 
     @pl.when(step + 1 < steps)
     def _():
@@ -1596,9 +1589,12 @@
                     ).wait()
 
         gather.finish(True)
-
-
-def run_units(mixer_rows, tables, grad, weights, collective_id):
+        late.last(2)
+        late.last(3)
+        late.finish()
+
+
+def run_units(mixer_rows, tables, grad, layer_rows, weights, collective_id):
     rows, width = mixer_rows.shape
     exp_count, row_count = lax.axis_size("exp"), lax.axis_size("row")
     tokens = tables.shape[0]
@@ -1615,11 +1611,12 @@
         units_kernel,
         out_shape=[
             jax.ShapeDtypeStruct((2, exp_count * row_count, rows, width), kind),
+            jax.ShapeDtypeStruct(grad.shape, kind),
             pair, pair, pair, half, shared, shared, jax.ShapeDtypeStruct((width, tokens), kind),
         ],
         grid=(steps,),
-        in_specs=[ANY_SPEC] * (len(weights) + 3),
-        out_specs=[ANY_SPEC] * 8,
+        in_specs=[ANY_SPEC] * (len(weights) + 4),
+        out_specs=[ANY_SPEC] * 9,
         scratch_shapes=[
             pltpu.VMEM((2, units, width), kind),
             pltpu.VMEM((2, units, width), kind),
@@ -1642,6 +1639,7 @@
             dma((2, 2, 3)),
             dma((3, 2, steps // 2)),
             *Gather.sems(),
+            *Gather.sems(),
         ],
         compiler_params=pltpu.CompilerParams(
             collective_id=collective_id, has_side_effects=True, vmem_limit_bytes=VMEM_LIMIT
@@ -1651,7 +1649,7 @@
             bytes_accessed=50 * 1024 * 1024,
             transcendentals=2 * tokens * units,
         ),
-    )(mixer_rows, tables, grad, *weights)
+    )(mixer_rows, tables, grad, layer_rows, *weights)
     return mixer.reshape(2, tokens, width), *others
 
 
@@ -1935,7 +1933,7 @@
     gain_two = feedforward_gain.astype(jnp.float32)
     (
         own_normed, own_scale, inverse_one, hidden_state, normed_two, scale_two, mixer_input,
-        tables_all, grad_all, input_all, query_other, latent_other, gain_other,
+        tables_all, grad_all, query_other, latent_other, gain_other,
         gate_other, up_other, down_other, shared_gate_other, shared_up_other, shared_down_other,
     ) = prologue(
         layer_input, gain_own, latent_gains, keyvalue_weight, output_weight,
@@ -1949,12 +1947,13 @@
     )
     tables_all = tables_all.reshape(tokens, -1)
     (
-        mixer, both_hidden, both_gating, both_upward, shared_hidden, shared_gating, shared_upward,
-        mixer_turned,
+        mixer, input_all, both_hidden, both_gating, both_upward, shared_hidden, shared_gating,
+        shared_upward, mixer_turned,
     ) = run_units(
         mixer_input,
         tables_all,
         grad_all,
+        layer_input,
         (
             gate_turned, gate_other, up_turned, up_other, expert_down, down_other,
             shared_gate, shared_gate_other, shared_up, shared_up_other,
@@ -2007,9 +2006,9 @@
     def stream_jobs(inputs, outputs, total):
         hidden, own_hidden, grads, values = inputs[:4]
         return [
-            *project_jobs(values, inputs[4:12], inputs[12], outputs[2:], 2),
             expert_down_job(hidden, grads, outputs[0], total),
             shared_down_job(own_hidden, grads, outputs[1], total),
+            *project_jobs(values, inputs[4:12], inputs[12], outputs[2:], 2),
         ]
 
     stream_operands = (

time: 544 us -> 509 us (0.936)
  Pallas kernels: 476 us -> 441 us
    pallas_call x1, Pallas kernels: 102 us -> 67.7 us  [prologue(): pl.pallas_call(prologue_kernel, out_shape=[jax.ShapeDtypeStruct((group, R...]
    pallas_call x1, Pallas kernels: 91.1 us -> 79.3 us  [gather_everywhere(): pl.pallas_call(functools.partial(gather_kernel, make_jobs=make_jobs, inpu...]
    pallas_call x1, Pallas kernels: 82.7 us -> 92 us  [run_units(): pl.pallas_call(units_kernel, out_shape=[jax.ShapeDtypeStruct((2, exp_coun...]
where the time goes in v3:
time: 509 us; the launch traced here: 503 us
  Pallas kernels  441 us (87%)
  other arithmetic  37.4 us (7%)
  local copies, waits for them, and re-layouts  12.9 us (3%)
  matrix products  7.15 us (1%)
    pallas_call x2, Pallas kernels, scatter_products(): pl.pallas_call(functools.partial(scatter_kernel, backward=backward, make_...  143 us
    pallas_call x1, Pallas kernels, run_units(): pl.pallas_call(units_kernel, out_shape=[jax.ShapeDtypeStruct((2, exp_coun...  92 us
    pallas_call x1, Pallas kernels, gather_everywhere(): pl.pallas_call(functools.partial(gather_kernel, make_jobs=make_jobs, inpu...  79.3 us
    pallas_call x1, Pallas kernels, prologue(): pl.pallas_call(prologue_kernel, out_shape=[jax.ShapeDtypeStruct((group, R...  67.7 us
    pallas_call x1, Pallas kernels, tail(): pl.pallas_call(functools.partial(tail_kernel, fused=fused), out_shape=[ja...  59.7 us
    convert_element_type x7, other arithmetic, local(): array.astype(jnp.float32)  24.4 us
  transfers between devices with their start and end apart: 1, of which 0 were waited for; matrix products, arithmetic and copies ran while one was open for 5% of the time, Pallas kernels for 31%

profile of v3, /device:TPU:0, one launch (start us, length us, event | category | flops | bytes accessed | tf_op | source)
XLA Modules:
  0.0 502.8 jit_solution(14054460730984685408)
XLA Ops:
  0.7 0.8 reduce-window.4
  2.3 1.3 convert_element_type.78
  4.7 0.8 copy.42
  6.1 0.9 concatenate.3.table.tables
  7.0 1.3 broadcast_in_dim.40.latent_gain.refs_11_
  8.3 1.3 broadcast_in_dim.39.gain.refs_5_
  9.6 67.7 %shard_map.289 = (f32[256,512]{1,0:T(8,128)}, f32[256,1]{1,0:T(8,128)}, f32[128,128]{1,0:T(8,128)}, f32[128,1024]{1,0:T(8,128)}, f32[128,1024]{1,0:T(8,128)}, /*...) custom-call(bf16[128,1024]{1,0:T(8,128)(2,1)} %rows.3, ...), custom_call_target="tpu_custom_call" | custom-call | tf_op jit(solution)/shard_map/pallas_call | solution.py:627
  77.3 92.0 %shard_map.290 = (bf16[2,16,128,1024]{3,2,1,0:T(8,128)(2,1)}, bf16[16,2,128,1024]{3,2,1,0:T(8,128)(2,1)}, bf16[2,704,2048]{2,1,0:T(8,128)(2,1)}, bf16[2,704,2048...) custom-call(bf16[128,1024]{1,0:T(8,128)(2,1)} %get-tuple-element.67., ...), custom_call_target="tpu_custom_call" | custom-call | flops 35433480192 | bytes 52428800 | tf_op jit(solution)/shard_map/pallas_call | solution.py:1610
  169.2 1.0 constant_dynamic-slice_fusion
  170.7 76.0 %shard_map.291 = (f32[128,1024]{1,0:T(8,128)}, bf16[2,704,1024]{2,1,0:T(8,128)(2,1)}, bf16[2,704,1024]{2,1,0:T(8,128)(2,1)}, bf16[1024,1408]{1,0:T(8,128)(2,1)}, bf16[1024,1408]{1,0:T(8,128)(2,1)}) custom-call(bf16[2,704,2048]{2,1,0:T(8,128)(2,1)} %get-tuple-element.79.refs_0_.refs_8_, bf16[2,704,2048]{2,1,0:T(8,128)(2,1)} %get-tuple-element.80.refs_1_.refs_9_, ...), custom_call_target="tpu_custom_call" | custom-call | flops 11811160064 | bytes 74448896 | tf_op jit(solution)/shard_map/pallas_call | solution.py:1215
  246.8 1.2 multiply_reduce_fusion
  248.0 2.5 psum.7
  251.1 4.9 convert_element_type.85
  255.9 2.9 convert_element_type.86
  258.9 1.1 fusion.1
  259.9 79.3 %shard_map.292 = (bf16[2,16,128,1024]{3,2,1,0:T(8,128)(2,1)}, bf16[2,352,2048]{2,1,0:T(8,128)(2,1)}, bf16[704,2048]{1,0:T(8,128)(2,1)}, bf16[2048,768]{1,0:T(8,1...) custom-call(bf16[128,1024]{1,0:T(8,128)(2,1)} %get-tuple-element.119, ...), custom_call_target="tpu_custom_call" | custom-call | bytes 33554432 | tf_op jit(solution)/shard_map/pallas_call | solution.py:950
  339.2 5.3 %convert_element_type.87 = f32[704,2048]{1,0:T(8,128)} convert(bf16[704,2048]{1,0:T(8,128)(2,1)} %get-tuple-element.113) | non-fusion elementwise | flops 1441792 | bytes 8650752 | tf_op jit(solution)/shard_map/convert_element_type | solution.py:2099
  344.5 3.7 convert_element_type.88
  348.2 1.1 copy-done.4
  349.3 5.8 %convert_bitcast_fusion = (f32[2,1024,704]{1,2,0:T(8,128)}, f32[2,1024,704]{1,2,0:T(8,128)}) fusion(bf16[2,704,1024]{2,1,0:T(8,128)(2,1)S(1)} %copy-done.4, bf16[2,704,1024]{2,1,0:T(8,128)(2,1)S(1)} %copy-done.3), kind=kLoop, calls=%fused_computation | loop fusion | flops 2883584 | bytes 17301504 | tf_op jit(solution)/shard_map/transpose | solution.py:2119
  355.1 0.7 copy-done.13
  355.8 66.9 %shard_map.293 = (f32[128,1024]{1,0:T(8,128)}, bf16[512,2048]{1,0:T(8,128)(2,1)}, bf16[2,2048,768]{2,1,0:T(8,128)(2,1)}, bf16[2048,1024]{1,0:T(8,128)(2,1)}, f32[2048,64]{1,0:T(8,128)}) custom-call(bf16[2,704,2048]{2,1,0:T(8,128)(2,1)} %get-tuple-element.76.refs_1_.refs_0_, bf16[2,352,2048]{2,1,0:T(8,128)(2,1)} %refs_1_.1, ...), custom_call_target="tpu_custom_call" | custom-call | flops 5905580032 | bytes 68681728 | tf_op jit(solution)/shard_map/pallas_call | solution.py:1215
  422.6 59.7 %shard_map.294 = (f32[128,1024]{1,0:T(8,128)}, f32[8,1024]{1,0:T(8,128)}, bf16[16,2,64,576]{3,2,1,0:T(8,128)(2,1)}, bf16[512,2048]{1,0:T(8,128)(2,1)}, bf16[512,...) custom-call(bf16[128,1024]{1,0:T(8,128)(2,1)} %rows.3, f32[128,128]{1,0:T(8,128)} %get-tuple-element.96.inverse_one, ...), custom_call_target="tpu_custom_call" | custom-call | tf_op jit(solution)/shard_map/pallas_call | solution.py:1825
  482.3 1.3 slice.14
  483.6 1.4 fusion.2
  485.1 7.1 %fusion.3 = f32[1024,576]{0,1:T(8,128)} fusion(bf16[1024,2048]{1,0:T(8,128)(2,1)} %get-tuple-element.103.attention_turned, bf16[2048,576]{1,0:T(8,128)(2,1)} %bitcast.48), kind=kOutput, calls=%fused_computation.22 | convolution fusion | flops 2415919104 | bytes 8912896 | tf_op jit(solution)/shard_map/dot_general | solution.py:23
  492.2 1.6 convert_element_type.83
  493.8 0.8 copy-done.5
  494.6 2.5 convert_element_type.84
  497.4 3.6 convert_element_type.82
  501.0 0.8 add_convert_fusion
  501.8 0.8 copy.46
  (49 shorter events, 3.9 us)
Async XLA Ops:
  77.3 93.3 %copy-start.15 = (f32[128,128]{1,0:T(8,128)S(1)}, f32[128,128]{1,0:T(8,128)}, u32[]{:S(2)}) copy-start(f32[128,128]{1,0:T(8,128)} %get-tuple-element.78) | copy-start | bytes 196612
  170.3 184.8 %collective-permute-start = (bf16[704,256]{1,0:T(8,128)(2,1)S(1)}, bf16[704,256]{1,0:T(8,128)(2,1)S(1)}, u32[]{:S(2)}, u32[]{:S(2)}) collective-permute-start(bf16[704,256]{1,0:T(8,128)(2,1)S(1)} %constant_dynamic-slice_fusion), channel_id=1, source_target_pairs={{0,1},{1,0},{2,3},{3,2},{4,5},{5,4},{6,7},{7,6},{8,9},{9,8},{10,11... | collective-permute-start | bytes 1081352 | tf_op jit(solution)/shard_map/ppermute | solution.py:74
  170.7 76.0 %copy-start.6 = (f32[128,1024]{1,0:T(8,128)S(1)}, f32[128,1024]{1,0:T(8,128)}, u32[]{:S(2)}) copy-start(f32[128,1024]{1,0:T(8,128)} %get-tuple-element.86) | copy-start | bytes 1572868
  170.7 76.0 %copy-start.14 = (f32[1024]{0:T(1024)S(1)}, f32[1024]{0:T(1024)}, u32[]{:S(2)}) copy-start(f32[1024]{0:T(1024)} %convert_element_type.78) | copy-start | bytes 12292
  251.1 4.9 copy-start.1
  255.9 2.9 copy-start.7
  255.9 2.9 copy-start.8
  339.2 5.3 %copy-start.2 = (bf16[2,352,2048]{2,1,0:T(8,128)(2,1)S(1)}, bf16[2,352,2048]{2,1,0:T(8,128)(2,1)}, u32[]{:S(2)}) copy-start(bf16[2,352,2048]{2,1,0:T(8,128)(2,1)} %get-tuple-element.116) | copy-start | bytes 8650756
  344.5 3.7 copy-start.3
  344.5 4.8 copy-start.4
  355.0 0.7 copy-start.13
  485.1 7.2 %copy-start.9 = (bf16[512,1024]{1,0:T(8,128)(2,1)S(1)}, bf16[512,1024]{1,0:T(8,128)(2,1)}, u32[]{:S(2)}) copy-start(bf16[512,1024]{1,0:T(8,128)(2,1)} %get-tuple-element.109) | copy-start | bytes 3145732
  492.2 2.3 copy-start.5
  494.5 2.9 copy-start
  497.4 3.6 copy-start.10
  497.4 3.6 copy-start.11
  497.4 4.4 copy-start.12

commit v4 on v3

--- a/solution.py
+++ b/solution.py
@@ -532,7 +532,8 @@
         started.append(remote(source, target, weight_sems, (number,), core))
     for copy in loads:
         copy.wait()
-    steps.pop(0)()
+    for _ in range(slow - 2):
+        steps.pop(0)()
     keeps = [
         pltpu.make_async_copy(source, target, local_sems.at[number])
         for number, (source, target) in enumerate(
@@ -1515,13 +1516,13 @@
 
     acts(
         (0, [(gather.hop, 2), (gather.corner, 1), (gather.hop, 3), (wait_weights,)]),
-        (1, [(gather.corner, 2), (gather.last, 0)]),
-        (2, [(gather.corner, 3), (gather.last, 1), (late.start,)]),
-        (3, [(gather.last, 2), (late.hop, 1)]),
-        (4, [(gather.last, 3), (late.hop, 2)]),
-        (5, [(late.hop, 3), (late.corner, 0)]),
-        (6, [(late.corner, 1), (late.corner, 2), (late.last, 0)]),
-        (7, [(late.corner, 3), (late.last, 1)]),
+        (1, [(gather.corner, 2), (gather.last, 0), (late.start,)]),
+        (2, [(gather.corner, 3), (gather.last, 1), (late.hop, 1)]),
+        (3, [(gather.last, 2), (late.hop, 2)]),
+        (4, [(gather.last, 3), (late.hop, 3), (late.corner, 0)]),
+        (5, [(late.corner, 1), (late.corner, 2)]),
+        (6, [(late.corner, 3), (late.last, 0), (late.last, 1)]),
+        (7, [(late.last, 2), (late.last, 3)]),
     )
 
     @pl.when(step + 1 < steps)
@@ -1589,8 +1590,6 @@
                     ).wait()
 
         gather.finish(True)
-        late.last(2)
-        late.last(3)
         late.finish()
 
 

time: 509 us -> 504 us (level)
    pallas_call x1, Pallas kernels: 92 us -> 86.2 us  [run_units(): pl.pallas_call(units_kernel, out_shape=[jax.ShapeDtypeStruct((2, exp_coun...]
  transfers between devices with their start and end apart: 1 -> 1, of which waited for: 0 -> 0; matrix products, arithmetic and copies ran while one was open for 5% -> 5% of each run, Pallas kernels for 31% -> 32%
where the time goes in v4:
time: 504 us; the launch traced here: 498 us
  Pallas kernels  436 us (87%)
  other arithmetic  37.4 us (7%)
  local copies, waits for them, and re-layouts  12.9 us (3%)
  matrix products  7.15 us (1%)
    pallas_call x2, Pallas kernels, scatter_products(): pl.pallas_call(functools.partial(scatter_kernel, backward=backward, make_...  146 us
    pallas_call x1, Pallas kernels, run_units(): pl.pallas_call(units_kernel, out_shape=[jax.ShapeDtypeStruct((2, exp_coun...  86.2 us
    pallas_call x1, Pallas kernels, gather_everywhere(): pl.pallas_call(functools.partial(gather_kernel, make_jobs=make_jobs, inpu...  77.7 us
    pallas_call x1, Pallas kernels, prologue(): pl.pallas_call(prologue_kernel, out_shape=[jax.ShapeDtypeStruct((group, R...  67.7 us
    pallas_call x1, Pallas kernels, tail(): pl.pallas_call(functools.partial(tail_kernel, fused=fused), out_shape=[ja...  59.3 us
    convert_element_type x7, other arithmetic, local(): array.astype(jnp.float32)  24.4 us
  transfers between devices with their start and end apart: 1, of which 0 were waited for; matrix products, arithmetic and copies ran while one was open for 5% of the time, Pallas kernels for 32%

profile of v4, /device:TPU:0, one launch (start us, length us, event | category | flops | bytes accessed | tf_op | source)
XLA Modules:
  0.0 497.8 jit_solution(1624330875028702616)
XLA Ops:
  0.7 0.8 reduce-window.4
  2.3 1.3 convert_element_type.78
  4.7 0.8 copy.42
  6.1 0.9 concatenate.3.table.tables
  7.0 1.3 broadcast_in_dim.40.latent_gain.refs_11_
  8.3 1.3 broadcast_in_dim.39.gain.refs_5_
  9.6 67.7 %shard_map.289 = (f32[256,512]{1,0:T(8,128)}, f32[256,1]{1,0:T(8,128)}, f32[128,128]{1,0:T(8,128)}, f32[128,1024]{1,0:T(8,128)}, f32[128,1024]{1,0:T(8,128)}, /*...) custom-call(bf16[128,1024]{1,0:T(8,128)(2,1)} %rows.3, ...), custom_call_target="tpu_custom_call" | custom-call | tf_op jit(solution)/shard_map/pallas_call | solution.py:628
  77.3 86.2 %shard_map.290 = (bf16[2,16,128,1024]{3,2,1,0:T(8,128)(2,1)}, bf16[16,2,128,1024]{3,2,1,0:T(8,128)(2,1)}, bf16[2,704,2048]{2,1,0:T(8,128)(2,1)}, bf16[2,704,2048...) custom-call(bf16[128,1024]{1,0:T(8,128)(2,1)} %get-tuple-element.67., ...), custom_call_target="tpu_custom_call" | custom-call | flops 35433480192 | bytes 52428800 | tf_op jit(solution)/shard_map/pallas_call | solution.py:1609
  163.5 1.0 constant_dynamic-slice_fusion
  164.9 79.1 %shard_map.291 = (f32[128,1024]{1,0:T(8,128)}, bf16[2,704,1024]{2,1,0:T(8,128)(2,1)}, bf16[2,704,1024]{2,1,0:T(8,128)(2,1)}, bf16[1024,1408]{1,0:T(8,128)(2,1)}, bf16[1024,1408]{1,0:T(8,128)(2,1)}) custom-call(bf16[2,704,2048]{2,1,0:T(8,128)(2,1)} %get-tuple-element.79.refs_0_.refs_8_, bf16[2,704,2048]{2,1,0:T(8,128)(2,1)} %get-tuple-element.80.refs_1_.refs_9_, ...), custom_call_target="tpu_custom_call" | custom-call | flops 11811160064 | bytes 74448896 | tf_op jit(solution)/shard_map/pallas_call | solution.py:1216
  244.1 1.2 multiply_reduce_fusion
  245.3 2.5 psum.7
  248.4 4.9 convert_element_type.85
  253.2 2.9 convert_element_type.86
  256.2 1.1 fusion.1
  257.2 77.7 %shard_map.292 = (bf16[2,16,128,1024]{3,2,1,0:T(8,128)(2,1)}, bf16[2,352,2048]{2,1,0:T(8,128)(2,1)}, bf16[704,2048]{1,0:T(8,128)(2,1)}, bf16[2048,768]{1,0:T(8,1...) custom-call(bf16[128,1024]{1,0:T(8,128)(2,1)} %get-tuple-element.119, ...), custom_call_target="tpu_custom_call" | custom-call | bytes 33554432 | tf_op jit(solution)/shard_map/pallas_call | solution.py:951
  334.9 5.3 %convert_element_type.87 = f32[704,2048]{1,0:T(8,128)} convert(bf16[704,2048]{1,0:T(8,128)(2,1)} %get-tuple-element.113) | non-fusion elementwise | flops 1441792 | bytes 8650752 | tf_op jit(solution)/shard_map/convert_element_type | solution.py:2098
  340.2 3.7 convert_element_type.88
  343.9 1.1 copy-done.4
  345.0 5.8 %convert_bitcast_fusion = (f32[2,1024,704]{1,2,0:T(8,128)}, f32[2,1024,704]{1,2,0:T(8,128)}) fusion(bf16[2,704,1024]{2,1,0:T(8,128)(2,1)S(1)} %copy-done.4, bf16[2,704,1024]{2,1,0:T(8,128)(2,1)S(1)} %copy-done.3), kind=kLoop, calls=%fused_computation | loop fusion | flops 2883584 | bytes 17301504 | tf_op jit(solution)/shard_map/transpose | solution.py:2118
  350.8 0.7 copy-done.13
  351.5 66.4 %shard_map.293 = (f32[128,1024]{1,0:T(8,128)}, bf16[512,2048]{1,0:T(8,128)(2,1)}, bf16[2,2048,768]{2,1,0:T(8,128)(2,1)}, bf16[2048,1024]{1,0:T(8,128)(2,1)}, f32[2048,64]{1,0:T(8,128)}) custom-call(bf16[2,704,2048]{2,1,0:T(8,128)(2,1)} %get-tuple-element.76.refs_1_.refs_0_, bf16[2,352,2048]{2,1,0:T(8,128)(2,1)} %refs_1_.1, ...), custom_call_target="tpu_custom_call" | custom-call | flops 5905580032 | bytes 68681728 | tf_op jit(solution)/shard_map/pallas_call | solution.py:1216
  417.9 59.3 %shard_map.294 = (f32[128,1024]{1,0:T(8,128)}, f32[8,1024]{1,0:T(8,128)}, bf16[16,2,64,576]{3,2,1,0:T(8,128)(2,1)}, bf16[512,2048]{1,0:T(8,128)(2,1)}, bf16[512,...) custom-call(bf16[128,1024]{1,0:T(8,128)(2,1)} %rows.3, f32[128,128]{1,0:T(8,128)} %get-tuple-element.96.inverse_one, ...), custom_call_target="tpu_custom_call" | custom-call | tf_op jit(solution)/shard_map/pallas_call | solution.py:1824
  477.3 1.3 slice.14
  478.6 1.4 fusion.2
  480.0 7.1 %fusion.3 = f32[1024,576]{0,1:T(8,128)} fusion(bf16[1024,2048]{1,0:T(8,128)(2,1)} %get-tuple-element.103.attention_turned, bf16[2048,576]{1,0:T(8,128)(2,1)} %bitcast.48), kind=kOutput, calls=%fused_computation.22 | convolution fusion | flops 2415919104 | bytes 8912896 | tf_op jit(solution)/shard_map/dot_general | solution.py:23
  487.2 1.6 convert_element_type.83
  488.7 0.8 copy-done.5
  489.5 2.5 convert_element_type.84
  492.4 3.6 convert_element_type.82
  496.0 0.8 add_convert_fusion
  496.8 0.8 copy.46
  (49 shorter events, 3.8 us)
Async XLA Ops:
  77.3 87.5 %copy-start.15 = (f32[128,128]{1,0:T(8,128)S(1)}, f32[128,128]{1,0:T(8,128)}, u32[]{:S(2)}) copy-start(f32[128,128]{1,0:T(8,128)} %get-tuple-element.78) | copy-start | bytes 196612
  164.5 186.3 %collective-permute-start = (bf16[704,256]{1,0:T(8,128)(2,1)S(1)}, bf16[704,256]{1,0:T(8,128)(2,1)S(1)}, u32[]{:S(2)}, u32[]{:S(2)}) collective-permute-start(bf16[704,256]{1,0:T(8,128)(2,1)S(1)} %constant_dynamic-slice_fusion), channel_id=1, source_target_pairs={{0,1},{1,0},{2,3},{3,2},{4,5},{5,4},{6,7},{7,6},{8,9},{9,8},{10,11... | collective-permute-start | bytes 1081352 | tf_op jit(solution)/shard_map/ppermute | solution.py:74
  164.9 79.2 %copy-start.6 = (f32[128,1024]{1,0:T(8,128)S(1)}, f32[128,1024]{1,0:T(8,128)}, u32[]{:S(2)}) copy-start(f32[128,1024]{1,0:T(8,128)} %get-tuple-element.86) | copy-start | bytes 1572868
  164.9 79.2 %copy-start.14 = (f32[1024]{0:T(1024)S(1)}, f32[1024]{0:T(1024)}, u32[]{:S(2)}) copy-start(f32[1024]{0:T(1024)} %convert_element_type.78) | copy-start | bytes 12292
  248.4 4.9 copy-start.1
  253.2 2.9 copy-start.7
  253.2 2.9 copy-start.8
  334.9 5.3 %copy-start.2 = (bf16[2,352,2048]{2,1,0:T(8,128)(2,1)S(1)}, bf16[2,352,2048]{2,1,0:T(8,128)(2,1)}, u32[]{:S(2)}) copy-start(bf16[2,352,2048]{2,1,0:T(8,128)(2,1)} %get-tuple-element.116) | copy-start | bytes 8650756
  340.2 3.7 copy-start.3
  340.2 4.8 copy-start.4
  350.8 0.7 copy-start.13
  480.0 7.2 %copy-start.9 = (bf16[512,1024]{1,0:T(8,128)(2,1)S(1)}, bf16[512,1024]{1,0:T(8,128)(2,1)}, u32[]{:S(2)}) copy-start(bf16[512,1024]{1,0:T(8,128)(2,1)} %get-tuple-element.109) | copy-start | bytes 3145732
  487.2 2.3 copy-start.5
  489.5 2.9 copy-start
  492.4 3.6 copy-start.10
  492.4 3.6 copy-start.11
  492.4 4.4 copy-start.12
